TPU v7x, 32 devices: a whole 2x2x4 slice. The times are simulated.
32 devices in a mesh: role: 2 (over x), seq: 4 (over z), tp: 4 (over y, core).
Axes of the slice: x: 2, y: 2, z: 4, core: 2. Of those that a mesh axis runs over, the one named last changes fastest.
Arguments:
- hidden: bfloat16 [2048, 8192], P(('role', 'seq')), may hold values from -11 to 11
- w_query: bfloat16 [8192, 4096], P(None, 'tp'), may hold values from -0.0625 to 0.0625
- w_key: bfloat16 [896, 4096], P(None, 'tp'), may hold values from -0.1875 to 0.1875
- w_value: bfloat16 [896, 4096], P(None, 'tp'), may hold values from -0.1875 to 0.1875
- enc_gain: float32 [896], replicated, may hold values from 0.1 to 1.9
- w_in: bfloat16 [896, 1792], replicated, may hold values from -0.1875 to 0.1875
- w_out: bfloat16 [1792, 896], replicated, may hold values from -0.125 to 0.125
- db_states: bfloat16 [128, 128, 896], P(('role', 'seq'), 'tp'), may hold values from -24 to 24
- neighbours: int32 [32, 2], P(('role', 'seq')), may hold values from 0 to 127, as said below
- d_attended: bfloat16 [2048, 4096], P(('role', 'seq'), 'tp'), may hold values from -24 to 24
Outputs:
- attended: bfloat16 [2048, 4096], P(('role', 'seq'), 'tp')
- grad_rows: bfloat16 [128, 128, 896], P(('role', 'seq'), 'tp')
Inputs may be any that keep to these rules, and one draw needn't show every extreme that they name: Database rows; shard g of role+seq holds rows g * 16 to (g + 1) * 16 - 1. Of the 8 neighbours of the stretches on one index of role+seq, at most 2 lie in one shard (repeats counted), and exactly 2 in some shard.
All inputs are finite; a program needn't handle non-finite values.
Results may differ from a plain program's by a relative error of at most 0.02.
The roundings to bfloat16 on the way count: a program that leaves them out, or rounds other values in their place, can miss the bound.
Values may be sent and summed in bfloat16 or wider, within the bound.
No kernel may reach another device: no remote copies, remote signals or barrier semaphores. Data moves between devices by JAX's collectives and lax.ppermute only.
A program may use at most 128 MiB of HBM per device.

v0:
```python
import jax
import jax.numpy as jnp
from jax import lax
from jax.sharding import PartitionSpec as P

HD = 128
STRETCH = 64


EPS = 1e-06


def from_behind(value, axis, by):
    peers = lax.axis_size(axis)
    pairs = [(i, i + by) for i in range(peers) if 0 <= i + by < peers]
    return lax.ppermute(value, axis, pairs)


def encode(flat_rows, enc_gain, w_in, w_out):
    row_values = flat_rows.astype(jnp.float32)
    inverse = lax.rsqrt(jnp.mean(row_values * row_values, axis=-1, keepdims=True) + EPS)
    normed = (row_values * inverse * enc_gain).astype(jnp.bfloat16)
    pre_act = jnp.dot(normed, w_in, preferred_element_type=jnp.float32)
    active = jax.nn.gelu(pre_act).astype(jnp.bfloat16)
    encoded = (row_values + jnp.dot(active, w_out, preferred_element_type=jnp.float32)).astype(
        jnp.bfloat16
    )
    return (encoded, inverse, pre_act)


def encode_back(flat_rows, inverse, pre_act, row_grad, enc_gain, w_in, w_out):
    row_values = flat_rows.astype(jnp.float32)
    upstream = row_grad.astype(jnp.bfloat16)
    d_act = jnp.dot(upstream, w_out.T, preferred_element_type=jnp.float32)
    d_pre = jax.vjp(jax.nn.gelu, pre_act)[1](d_act)[0]
    d_norm = jnp.dot(d_pre.astype(jnp.bfloat16), w_in.T, preferred_element_type=jnp.float32)
    scaled = d_norm * enc_gain
    cubed = inverse * inverse * inverse
    back_term = inverse * scaled - row_values * cubed * jnp.mean(
        scaled * row_values, axis=-1, keepdims=True
    )
    return (row_grad + back_term).astype(jnp.bfloat16)


def attend(queries, key_rows, value_rows, score_scale):
    scores = (
        jnp.einsum("bqhe,bkhe->bhqk", queries, key_rows, preferred_element_type=jnp.float32)
        * score_scale
    )
    maximum = jnp.max(scores, axis=-1, keepdims=True)
    weights = jnp.exp(scores - maximum)
    probability = weights / jnp.sum(weights, axis=-1, keepdims=True)
    rounded = probability.astype(jnp.bfloat16)
    outputs = jnp.einsum("bhqk,bkhe->bqhe", rounded, value_rows, preferred_element_type=jnp.float32)
    return (outputs, probability, rounded)


def attend_back(queries, value_rows, probability, rounded, cotangent, score_scale):
    value_grads = jnp.einsum(
        "bhqk,bqhe->bkhe", rounded, cotangent, preferred_element_type=jnp.float32
    )
    dprobs = jnp.einsum(
        "bqhe,bkhe->bhqk", cotangent, value_rows, preferred_element_type=jnp.float32
    )
    centre = jnp.sum(probability * dprobs, axis=-1, keepdims=True)
    dscores = (probability * (dprobs - centre)).astype(jnp.bfloat16)
    key_grads = (
        jnp.einsum("bhqk,bqhe->bkhe", dscores, queries, preferred_element_type=jnp.float32)
        * score_scale
    )
    return (key_grads, value_grads)


def body(hidden, w_query, w_key, w_value, enc_gain, w_in, w_out, db_states, neighbours, d_attended):
    groups = lax.axis_size(("role", "seq"))
    shards = lax.axis_size("tp")
    my_group = lax.axis_index(("role", "seq"))
    row_count, piece_len, enc_width = db_states.shape
    stretch_count, fan_out = neighbours.shape
    slot_count = stretch_count * fan_out
    tok_count = hidden.shape[0]
    feat_dev = w_query.shape[1]
    head_count = feat_dev // HD
    row_tokens = piece_len * shards
    span = fan_out * row_tokens
    capacity = max(2, 2 * ((stretch_count - 1 + groups - 2) // (groups - 1)))
    score_scale = HD ** (-0.5)
    all_ids = lax.all_gather(neighbours, ("role", "seq"), axis=0, tiled=True).reshape(
        groups, slot_count
    )
    owner_of = all_ids // row_count
    earlier = jnp.arange(slot_count)[None, :] < jnp.arange(slot_count)[:, None]
    rank_of = jnp.sum((owner_of[:, :, None] == owner_of[:, None, :]) & earlier[None], axis=2)
    levels = jnp.arange(capacity, dtype=jnp.int32)
    cited_here = (owner_of == my_group)[:, None, :] & (rank_of[:, None, :] == levels[None, :, None])
    local_ids = all_ids - my_group * row_count
    row_for = jnp.sum(jnp.where(cited_here, local_ids[:, None, :], 0), axis=2)
    sent_here = jnp.any(cited_here, axis=2)
    mine_owner = lax.dynamic_index_in_dim(owner_of, my_group, 0, keepdims=False)
    mine_rank = lax.dynamic_index_in_dim(rank_of, my_group, 0, keepdims=False)
    group_ids = jnp.arange(groups, dtype=jnp.int32)
    asked = (mine_owner[None, None, :] == group_ids[:, None, None]) & (
        mine_rank[None, None, :] == levels[None, :, None]
    )
    slot_for = jnp.sum(jnp.where(asked, jnp.arange(slot_count)[None, None, :], 0), axis=2)
    slot_used = jnp.any(asked, axis=2).astype(jnp.float32)
    flat_rows = db_states.reshape(row_count * piece_len, enc_width)
    encoded, inverse, pre_act = encode(flat_rows, enc_gain, w_in, w_out)
    outgoing = jnp.take(
        encoded.reshape(row_count, piece_len, enc_width), row_for.reshape(-1), axis=0
    )
    outgoing = outgoing.reshape(groups, capacity, piece_len, enc_width)
    queries = jnp.dot(hidden, w_query, preferred_element_type=jnp.float32).astype(jnp.bfloat16)
    queries = queries.reshape(tok_count, head_count, HD)
    cotangent = d_attended.reshape(tok_count, head_count, HD)
    copies = jnp.broadcast_to(outgoing[:, None], (groups, shards, capacity, piece_len, enc_width))
    arrived = lax.all_to_all(
        copies.reshape(groups * shards, capacity, piece_len, enc_width),
        ("role", "seq", "tp"),
        split_axis=0,
        concat_axis=0,
        tiled=True,
    )
    arrived = arrived.reshape(groups, shards, capacity, piece_len, enc_width)
    wanted = arrived[mine_owner, :, mine_rank].reshape(slot_count * row_tokens, enc_width)
    key_rows = jnp.dot(wanted, w_key, preferred_element_type=jnp.float32).astype(jnp.bfloat16)
    value_rows = jnp.dot(wanted, w_value, preferred_element_type=jnp.float32).astype(jnp.bfloat16)
    key_value = jnp.stack([key_rows, value_rows]).reshape(2, slot_count, row_tokens, feat_dev)
    key_value = key_value.reshape(2, stretch_count, span, head_count, HD)
    prior_kv = from_behind(key_value[:, stretch_count - 1], "seq", 1)
    all_kv = jnp.concatenate([prior_kv[:, None], key_value], axis=1)
    edges = ((1, STRETCH - 1), (0, 0), (0, 0))
    block_q = jnp.pad(queries, edges).reshape(stretch_count + 1, STRETCH, head_count, HD)
    outputs, probability, rounded = attend(block_q, all_kv[0], all_kv[1], score_scale)
    attended = outputs.reshape(-1, feat_dev)[1 : tok_count + 1].astype(jnp.bfloat16)
    block_d = jnp.pad(cotangent, edges).reshape(stretch_count + 1, STRETCH, head_count, HD)
    key_all, value_all = attend_back(block_q, all_kv[1], probability, rounded, block_d, score_scale)
    carried = from_behind(jnp.stack([key_all[0], value_all[0]]), "seq", -1)
    key_grads = key_all[1:].at[stretch_count - 1].add(carried[0])
    value_grads = value_all[1:].at[stretch_count - 1].add(carried[1])
    key_back = key_grads.astype(jnp.bfloat16).reshape(slot_count, row_tokens, feat_dev)
    value_back = value_grads.astype(jnp.bfloat16).reshape(slot_count, row_tokens, feat_dev)
    key_tokens = key_back.transpose(1, 0, 2)
    value_tokens = value_back.transpose(1, 0, 2)
    key_part = key_tokens.reshape(-1, feat_dev)
    value_part = value_tokens.reshape(-1, feat_dev)
    term = jnp.dot(key_part, w_key.T, preferred_element_type=jnp.float32)
    term = term + jnp.dot(value_part, w_value.T, preferred_element_type=jnp.float32)
    summed = lax.psum_scatter(
        term.reshape(piece_len * lax.axis_size("tp"), slot_count, enc_width),
        "tp",
        scatter_dimension=0,
        tiled=True,
    )
    picked = jnp.take(summed, slot_for.reshape(-1), axis=1) * slot_used.reshape(1, -1, 1)
    outgoing_grads = picked.reshape(piece_len, groups, capacity, enc_width).transpose(1, 2, 0, 3)
    totals = lax.all_to_all(
        outgoing_grads, ("role", "seq"), split_axis=0, concat_axis=0, tiled=True
    )
    totals = totals.reshape(groups * capacity, piece_len, enc_width)
    onehot = (row_for.reshape(-1)[:, None] == jnp.arange(row_count)[None, :]) & sent_here.reshape(
        -1
    )[:, None]
    row_grad = jnp.einsum(
        "sr,spd->rpd", onehot.astype(jnp.float32), totals, precision=lax.Precision.HIGHEST
    )
    grads = encode_back(
        flat_rows, inverse, pre_act, row_grad.reshape(-1, enc_width), enc_gain, w_in, w_out
    )
    return (attended, grads.reshape(row_count, piece_len, enc_width))


def solution(mesh):
    in_specs = (
        P(("role", "seq"), None),
        P(None, "tp"),
        P(None, "tp"),
        P(None, "tp"),
        P(),
        P(),
        P(),
        P(("role", "seq"), "tp", None),
        P(("role", "seq"), None),
        P(("role", "seq"), "tp"),
    )
    out_specs = (P(("role", "seq"), "tp"), P(("role", "seq"), "tp", None))
    return jax.shard_map(body, mesh=mesh, in_specs=in_specs, out_specs=out_specs, check_vma=False)
```

profile of v0, /device:TPU:0, one launch (start us, length us, event | category | flops | bytes accessed | tf_op | source)
XLA Modules:
  0.0 412.9 jit_solution(4636647529783346314)
XLA Ops:
  7.2 22.6 %all-gather = s32[8,4,2]{1,2,0:T(2,128)S(1)} all-gather(s32[1,4,2]{1,2,0:T(2,128)} %bitcast.156), channel_id=1, replica_groups=mesh['role'=2,'seq'=4,'tp'=4] {'role','seq'}, dimensions={0}, use_global_device_ids=true | all-gather | bytes 288 | tf_op jit(solution)/shard_map/all_gather | solution.py:88
  30.9 1.4 fusion.24
  32.4 1.5 fusion.26
  33.9 2.1 fusion.105
  36.1 3.2 fusion.27
  39.3 2.8 gather_fusion
  42.1 1.3 broadcast_select_fusion
  43.4 2.3 broadcast_in_dim.47
  45.8 3.5 all-to-all-start
  49.6 83.3 %all-to-all-done = bf16[32,2,32,896]{3,2,1,0:T(8,128)(2,1)} async-done(((bf16[32,2,32,896]{3,2,1,0:T(8,128)(2,1)}), bf16[32,2,32,896]{3,2,1,0:T(8,128)(2,1)}, u32[]{:S(2)}, u32[]{:S(2)}) %all-to-all-start) | async-done | bytes 3670048 | tf_op jit(solution)/shard_map/all_to_all | solution.py:117
  132.9 4.0 gather_fusion.1
  136.9 4.4 %convert_bitcast_fusion = bf16[128,8,8,128]{3,1,2,0:T(8,128)(2,1)S(1)} fusion(bf16[1024,896]{1,0:T(8,128)(2,1)} %bitcast.144, bf16[896,1024]{1,0:T(8,128)(2,1)} %param.17), kind=kOutput, calls=%fused_computation.38 | convolution fusion | flops 1880096768 | bytes 5767168 | tf_op jit(solution)/shard_map/dot_general | solution.py:127
  143.4 2.3 convert_bitcast_fusion.1
  147.6 1.8 collective-permute-start
  150.4 8.2 %fusion.44 = bf16[32,8,8,128]{3,1,2,0:T(8,128)(2,1)S(1)} fusion(bf16[256,8192]{1,0:T(8,128)(2,1)S(1)} %copy-done.12, bf16[8192,1024]{1,0:T(8,128)(2,1)} %param.15), kind=kOutput, calls=%fused_computation.70 | convolution fusion | flops 4295229440 | bytes 21495808 | tf_op jit(solution)/shard_map/dot_general | solution.py:113
  159.9 11.8 %collective-permute-done = bf16[2,256,8,128]{3,1,2,0:T(8,128)(2,1)S(1)} collective-permute-done((bf16[2,256,8,128]{3,1,2,0:T(8,128)(2,1)S(1)}, bf16[2,256,8,128]{3,1,2,0:T(8,128)(2,1)S(1)}, u32[]{:S(2)}, u32[]{:S(2)}) %collective-permute-start) | collective-permute-done | bytes 1048608 | tf_op jit(solution)/shard_map/ppermute | solution.py:16
  171.7 1.2 fusion.10
  172.9 2.3 fusion.102
  175.2 10.0 %convolution_bitcast_fusion = f32[5,256,8,128]{1,3,2,0:T(8,128)} fusion(bf16[5,64,8,128]{3,2,1,0:T(8,128)(2,1)} %bitcast.151, f32[5,8,64]{2,1,0:T(8,128)S(1)} %get-tuple-element.30, f32[5,8,64,256]{3,2,1,0:T(8,128)} %copy-done.3), kind=kOutput, calls=%fused_computation.26 | convolution fusion | flops 171051776 | bytes 8529920 | tf_op jit(solution)/shard_map/bhqk,bqhe->bkhe/dot_general | solution.py:59
  185.2 5.3 %multiply_reduce_fusion = (f32[5,8,64]{2,1,0:T(8,128)S(1)}, f32[5,8,64,256]{3,2,1,0:T(8,128)}) fusion(f32[5,8,64,256]{3,2,1,0:T(8,128)} %get-tuple-element.31, f32[5,8,64]{2,1,0:T(8,128)S(1)} %get-tuple-element.30, bf16[2,4,256,8,128]{4,2,3,1,0:T(8,128)(2,1)} %copy-done.2, bf16[2,1,256,8,128]{4,2,3,1,0:T(8,128)(2,1)} %bitcast.147, ...), kind=kOutput, calls=%fused_computation.24 | convolution fusion | flops 171046400 | bytes 11161600 | tf_op jit(solution)/shard_map/bqhe,bkhe->bhqk/dot_general | solution.py:62
  190.5 11.2 %multiply_bitcast_fusion = f32[5,256,8,128]{1,3,2,0:T(8,128)} fusion(f32[5,8,64,256]{3,2,1,0:T(8,128)} %get-tuple-element.33, f32[5,8,64]{2,1,0:T(8,128)S(1)} %get-tuple-element.32, bf16[5,64,8,128]{3,2,1,0:T(8,128)(2,1)} %bitcast.137, f32[5,8,64]{2,1,0:T(8,128)S(1)} %get-tuple-element.30, f32[5,8,64,256]{3,2,1,0:T(8,128)} %copy-done.3), kind=kOutput, calls=%fused_computation.8 | convolution fusion | flops 173673216 | bytes 11161600 | tf_op jit(solution)/shard_map/bhqk,bqhe->bkhe/dot_general | solution.py:68
  201.7 1.2 slice-done.2
  203.8 1.8 collective-permute-start.1
  206.1 1.6 slice.115
  207.7 1.6 slice.110
  209.3 44.1 %collective-permute-done.1 = f32[2,256,8,128]{1,3,2,0:T(8,128)S(1)} collective-permute-done((f32[2,256,8,128]{1,3,2,0:T(8,128)S(1)}, f32[2,256,8,128]{1,3,2,0:T(8,128)S(1)}, u32[]{:S(2)}, u32[]{:S(2)}) %collective-permute-start.1) | collective-permute-done | bytes 2097184 | tf_op jit(solution)/shard_map/ppermute | solution.py:16
  253.4 1.3 fusion.46
  254.7 4.3 %copy.80 = bf16[4,256,8,128]{3,2,1,0:T(8,128)(2,1)} copy(bf16[4,256,8,128]{1,3,2,0:T(8,128)(2,1)} %get-tuple-element.28) | data formatting | bytes 4194304 | tf_op jit(solution)/shard_map/convert_element_type | solution.py:141
  259.0 4.2 %reshape.463 = bf16[8,128,1024]{2,1,0:T(8,128)(2,1)} reshape(bf16[4,256,8,128]{3,2,1,0:T(8,128)(2,1)} %copy.80) | data formatting | bytes 4194304 | tf_op jit(solution)/shard_map/reshape | solution.py:141
  263.1 4.3 %copy.82 = bf16[4,256,8,128]{3,2,1,0:T(8,128)(2,1)} copy(bf16[4,256,8,128]{1,3,2,0:T(8,128)(2,1)} %get-tuple-element.29) | data formatting | bytes 4194304 | tf_op jit(solution)/shard_map/convert_element_type | solution.py:142
  267.4 4.2 %reshape.465 = bf16[8,128,1024]{2,1,0:T(8,128)(2,1)} reshape(bf16[4,256,8,128]{3,2,1,0:T(8,128)(2,1)} %copy.82) | data formatting | bytes 4194304 | tf_op jit(solution)/shard_map/reshape | solution.py:142
  271.6 4.9 %fusion.16 = f32[1024,896]{1,0:T(8,128)S(1)} fusion(bf16[896,1024]{1,0:T(8,128)(2,1)} %param.17, bf16[128,8,1024]{2,0,1:T(8,128)(2,1)} %bitcast.141), kind=kOutput, calls=%fused_computation.30 | convolution fusion | flops 1879048192 | bytes 7602176 | tf_op jit(solution)/shard_map/dot_general | solution.py:148
  276.5 2.6 add_bitcast_fusion
  279.1 2.5 copy.84
  282.4 40.7 %reduce-scatter.2.cloned.1.call-done = f32[32,8,896]{2,0,1:T(8,128)} async-done(((f32[128,8,896]{2,0,1:T(8,128)}), f32[32,8,896]{2,0,1:T(8,128)}) %reduce-scatter.2.cloned.1.call-update) | async-done | bytes 917520 | tf_op jit(solution)/shard_map/reduce_scatter | solution.py:149
  323.0 3.1 gather_fusion.2
  326.1 4.6 %fusion.32 = f32[8,2,32,896]{3,1,2,0:T(2,128)} fusion(f32[32,8,2,896]{3,0,2,1:T(8,128)} %bitcast.132, pred[8,2]{1,0:T(8,128)(4,1)S(1)} %copy.76, f32[8,2]{1,0:T(8,128)S(1)} %copy.87), kind=kLoop, calls=%fused_computation.58 | loop fusion | flops 917504 | bytes 3670096 | tf_op jit(solution)/shard_map/transpose | solution.py:156
  330.7 5.8 %all-to-all-start.1 = ((f32[8,2,32,896]{3,1,2,0:T(2,128)}), f32[8,2,32,896]{3,1,2,0:T(2,128)}, u32[]{:S(2)}, u32[]{:S(2)}) async-start(f32[8,2,32,896]{3,1,2,0:T(2,128)} %fusion.32), calls=%async_computation.2 | async-start | bytes 3670016 | tf_op jit(solution)/shard_map/all_to_all | solution.py:157
  336.9 8.6 %fusion.43 = bf16[5,64,8,128]{3,1,2,0:T(8,128)(2,1)} fusion(bf16[2,4,256,8,128]{4,2,3,1,0:T(8,128)(2,1)} %copy-done.2, bf16[2,1,256,8,128]{4,2,3,1,0:T(8,128)(2,1)} %bitcast.148, f32[5,8,64]{2,1,0:T(8,128)S(1)} %get-tuple-element.30, f32[5,8,64,256]{3,2,1,0:T(8,128)} %copy-done.3), kind=kOutput, calls=%fused_computation.69 | convolution fusion | flops 176622336 | bytes 8529920 | tf_op jit(solution)/shard_map/bhqk,bkhe->bqhe/dot_general | solution.py:54
  345.6 1.5 copy.73
  348.2 31.9 %all-to-all-done.1 = f32[8,2,32,896]{3,1,2,0:T(2,128)} async-done(((f32[8,2,32,896]{3,1,2,0:T(2,128)}), f32[8,2,32,896]{3,1,2,0:T(2,128)}, u32[]{:S(2)}, u32[]{:S(2)}) %all-to-all-start.1) | async-done | bytes 1835040 | tf_op jit(solution)/shard_map/all_to_all | solution.py:157
  380.0 3.4 copy.88
  383.4 3.7 reshape.469
  387.1 2.5 fusion.61
  390.3 1.2 copy-done.1
  391.5 1.0 bitcast_convert_fusion
  392.5 9.2 %fusion.30 = (f32[512]{0:T(512)S(1)}, f32[512,896]{1,0:T(8,128)}) fusion(bf16[16,32,896]{2,1,0:T(8,128)(2,1)} %param.21, f32[896]{0:T(1024)S(1)} %copy-done.11, bf16[896,1792]{1,0:T(8,128)(2,1)S(1)} %copy-done, f32[512,1792]{1,0:T(8,128)} %copy-done.16, bf16[512,896]{1,0:T(8,128)(2,1)} %bitcast_convert_fusion, bf16[1792,896]{1,0:T(8,128)(2,1)} %param.20), kind=kOutput, calls=%fused_computation.55 | convolution fusion | flops 3308518912 | bytes 13768192 | tf_op jit(solution)/shard_map/dot_general | solution.py:36
  401.7 3.8 fusion.23
  (93 shorter events, 11.8 us)
Async XLA Ops:
  7.2 26.7 %copy-start = (bf16[896,1792]{1,0:T(8,128)(2,1)S(1)}, bf16[896,1792]{1,0:T(8,128)(2,1)}, u32[]{:S(2)}) copy-start(bf16[896,1792]{1,0:T(8,128)(2,1)} %param.19) | copy-start | bytes 9633796
  33.9 2.1 copy-start.4
  33.9 2.2 copy-start.13
  36.1 3.2 copy-start.16
  45.8 87.1 %all-to-all-start = ((bf16[32,2,32,896]{3,2,1,0:T(8,128)(2,1)}), bf16[32,2,32,896]{3,2,1,0:T(8,128)(2,1)}, u32[]{:S(2)}, u32[]{:S(2)}) async-start(bf16[32,2,32,896]{3,2,1,0:T(8,128)(2,1)} %bitcast.129), calls=%async_computation | async-start | bytes 7340032 | tf_op jit(solution)/shard_map/all_to_all | solution.py:117
  49.3 273.7 %reduce-scatter.2.cloned.1.call-start = ((), (), s32[]{:S(2)}) async-start(), calls=%async_computation.3 | async-start | bytes 4587520 | tf_op jit(solution)/shard_map/reduce_scatter | solution.py:149
  141.3 1.5 copy-start.8
  141.3 2.0 copy-start.14
  146.8 3.6 copy-start.12
  147.5 24.2 %copy-start.2 = (bf16[2,4,256,8,128]{4,2,3,1,0:T(8,128)(2,1)}, bf16[2,4,256,8,128]{4,2,3,1,0:T(8,128)(2,1)S(1)}, u32[]{:S(2)}) copy-start(bf16[2,4,256,8,128]{4,2,3,1,0:T(8,128)(2,1)S(1)} %copy_dynamic-update-slice_fusion) | copy-start | bytes 12582916
  147.6 11.1 %copy-start.10 = (bf16[256,1024]{1,0:T(8,128)(2,1)S(1)}, bf16[256,1024]{1,0:T(8,128)(2,1)}, u32[]{:S(2)}) copy-start(bf16[256,1024]{1,0:T(8,128)(2,1)} %param.23) | copy-start | bytes 1572868
  147.6 24.0 %collective-permute-start = (bf16[2,256,8,128]{3,1,2,0:T(8,128)(2,1)S(1)}, bf16[2,256,8,128]{3,1,2,0:T(8,128)(2,1)S(1)}, u32[]{:S(2)}, u32[]{:S(2)}) collective-permute-start(bf16[2,256,8,128]{3,1,2,0:T(8,128)(2,1)S(1)} %slice_bitcast_fusion), channel_id=1, source_target_pairs={{0,4},{4,8},{8,12},{1,5},{5,9},{9,13},{2,6},{6,10},{10,14},{3,7},{... | collective-permute-start | bytes 3145736 | tf_op jit(solution)/shard_map/ppermute | solution.py:16
  158.9 13.9 %copy-start.6 = (bf16[320,8,128]{2,1,0:T(8,128)(2,1)}, bf16[320,8,128]{2,1,0:T(8,128)(2,1)S(1)}, u32[]{:S(2)}) copy-start(bf16[320,8,128]{2,1,0:T(8,128)(2,1)S(1)} %pad.11) | copy-start | bytes 1966084
  171.7 1.2 copy-start.9
  172.9 2.3 copy-start.3
  201.7 1.2 slice-start.2
  201.7 1.9 slice-start.3
  201.7 4.4 %copy-start.5 = (f32[5,256,8,128]{1,3,2,0:T(8,128)S(1)}, f32[5,256,8,128]{1,3,2,0:T(8,128)}, u32[]{:S(2)}) copy-start(f32[5,256,8,128]{1,3,2,0:T(8,128)} %convolution_bitcast_fusion) | copy-start | bytes 15728644
  201.7 6.0 %slice-start = ((s8[5242880]{0:T(1024)(128)(4,1)}), s8[4194304]{0:T(1024)(128)(4,1)S(1)}, s32[]{:S(2)}) async-start(s8[5242880]{0:T(1024)(128)(4,1)} %bitcast.133), calls=%async_computation.4 | async-start | bytes 8388608
  203.6 4.1 slice-start.1
  203.8 49.6 %collective-permute-start.1 = (f32[2,256,8,128]{1,3,2,0:T(8,128)S(1)}, f32[2,256,8,128]{1,3,2,0:T(8,128)S(1)}, u32[]{:S(2)}, u32[]{:S(2)}) collective-permute-start(f32[2,256,8,128]{1,3,2,0:T(8,128)S(1)} %pad_maximum_fusion.1), channel_id=1, source_target_pairs={{4,0},{8,4},{12,8},{5,1},{9,5},{13,9},{6,2},{10,6},{14,10},{7,3},{... | collective-permute-start | bytes 6291464 | tf_op jit(solution)/shard_map/ppermute | solution.py:16
  271.6 4.9 %copy-start.7 = (bf16[8,128,1024]{2,1,0:T(8,128)(2,1)S(1)}, bf16[8,128,1024]{2,1,0:T(8,128)(2,1)}, u32[]{:S(2)}) copy-start(bf16[8,128,1024]{2,1,0:T(8,128)(2,1)} %reshape.463) | copy-start | bytes 6291460
  271.6 4.9 %copy-start.15 = (bf16[896,1024]{1,0:T(8,128)(2,1)S(1)}, bf16[896,1024]{1,0:T(8,128)(2,1)}, u32[]{:S(2)}) copy-start(bf16[896,1024]{1,0:T(8,128)(2,1)} %param.16) | copy-start | bytes 5505028
  330.7 49.3 %all-to-all-start.1 = ((f32[8,2,32,896]{3,1,2,0:T(2,128)}), f32[8,2,32,896]{3,1,2,0:T(2,128)}, u32[]{:S(2)}, u32[]{:S(2)}) async-start(f32[8,2,32,896]{3,1,2,0:T(2,128)} %fusion.32), calls=%async_computation.2 | async-start | bytes 3670016 | tf_op jit(solution)/shard_map/all_to_all | solution.py:157
  389.6 2.9 copy-start.11
  390.3 1.3 copy-start.1
Sparse Core Ops, SparseCore 0:
  281.7 41.2 reduce-scatter.1
where the time goes:
time: 421 us; the launch traced here: 413 us
  waiting for transfers between devices  212 us (50%)
  matrix products  75.8 us (18%)
  local copies, waits for them, and re-layouts  56.4 us (13%)
  blocking collectives  22.6 us (5%)
  other arithmetic  18.3 us (4%)
  between operations  15 us (4%)
  starting transfers between devices  13 us (3%)
    all_to_all x1, waiting for transfers between devices, body(): lax.all_to_all(copies.reshape(groups * shards, capacity, piece_len, enc_w...  83.3 us
    ppermute x2, waiting for transfers between devices, from_behind(): return lax.ppermute(value, axis, pairs)  55.8 us
    reduce_scatter x1, waiting for transfers between devices, body(): lax.psum_scatter(term.reshape(piece_len * lax.axis_size('tp'), slot_count...  40.7 us
    all_to_all x1, waiting for transfers between devices, body(): lax.all_to_all(outgoing_grads, ('role', 'seq'), split_axis=0, concat_axis...  31.9 us
    all_gather x1, blocking collectives, body(): lax.all_gather(neighbours, ('role', 'seq'), axis=0, tiled=True)  22.6 us
    dot_general x1, matrix products, attend_back(): jnp.einsum('bhqk,bqhe->bkhe', dscores, queries, preferred_element_type=jn...  11.2 us
    dot_general x1, matrix products, attend_back(): jnp.einsum('bhqk,bqhe->bkhe', rounded, cotangent, preferred_element_type=...  10 us
    dot_general x1, matrix products, encode_back(): jnp.dot(d_pre.astype(jnp.bfloat16), w_in.T, preferred_element_type=jnp.fl...  9.21 us
  transfers between devices with their start and end apart: 5, of which 5 were waited for; matrix products, arithmetic and copies ran while one was open for 6% of the time, Pallas kernels for 0%

commit v1 on v0

v1 whole, which is shorter than its diff:
```python
import functools

import jax
import jax.numpy as jnp
from jax import lax
from jax.experimental import pallas as pl
from jax.experimental.pallas import tpu as pltpu
from jax.sharding import PartitionSpec as P

HD = 128
STRETCH = 64
EPS = 1e-06
GELU_A = 0.7978845608028654
GELU_B = 0.044715
F32 = jnp.float32
BF16 = jnp.bfloat16


def params(mib):
    return pltpu.CompilerParams(vmem_limit_bytes=mib * 1024 * 1024)


def dot(a, b):
    return jnp.dot(a, b, preferred_element_type=F32)


def dot_nt(a, b):
    return lax.dot_general(a, b, (((1,), (1,)), ((), ())), preferred_element_type=F32)


def dot_tn(a, b):
    return lax.dot_general(a, b, (((0,), (0,)), ((), ())), preferred_element_type=F32)


def whole(shape):
    return pl.BlockSpec(shape, lambda *_: (0,) * len(shape))


def smem():
    return pl.BlockSpec(memory_space=pltpu.SMEM)


def vmem():
    return pl.BlockSpec(memory_space=pltpu.VMEM)


def anywhere():
    return pl.BlockSpec(memory_space=pl.ANY)


def hbm(*arrays):
    return [pltpu.with_memory_space_constraint(array, pltpu.HBM) for array in arrays]


def tiles(size, part):
    return [(at, min(part, size - at)) for at in range(0, size, part)]


def exchange_masks(groups, peers):
    masks = range(1, groups)
    far = sorted([m for m in masks if m & (peers // 2)], reverse=True)
    near = sorted([m for m in masks if not m & (peers // 2)], key=lambda m: (m % peers != 0, -m))
    return [0] + near[:2] + far + near[2:]


def each_request(ids_ref, g, first, row_count, capacity, act):
    fan_out = ids_ref.shape[1]
    rank = jnp.int32(0)
    for s in range(ids_ref.shape[2] * fan_out):
        local = ids_ref[g, s % fan_out, s // fan_out] - first
        mine = (local >= 0) & (local < row_count)
        place = jnp.minimum(rank, capacity - 1)

        @pl.when(mine)
        def _():
            act(jnp.clip(local, 0, row_count - 1), place)

        rank = rank + mine.astype(jnp.int32)


def norm_of(x, gain):
    inverse = lax.rsqrt(jnp.mean(x * x, axis=-1, keepdims=True) + EPS)
    return (x * inverse * gain).astype(BF16), inverse


def encode_kernel(
    gain_hbm, x_hbm, w_in_hbm, w_out_hbm, enc_ref,
    gain_ref, x_ref, w_in, w_out, normed, active, sems, in_sems,
):
    rows, width = x_ref.shape
    hidden = w_in.shape[1]
    x_copy = pltpu.make_async_copy(x_hbm, x_ref, sems.at[0])
    x_copy.start()
    gain_copy = pltpu.make_async_copy(gain_hbm, gain_ref, sems.at[2])
    gain_copy.start()
    parts = [pl.ds(at, part) for at, part in tiles(hidden, hidden // 2)]
    in_copies = []
    for i, cols in enumerate(parts):
        copy = pltpu.make_async_copy(w_in_hbm.at[:, cols], w_in.at[:, cols], in_sems.at[i])
        copy.start()
        in_copies.append(copy)
    out_copy = pltpu.make_async_copy(w_out_hbm, w_out, sems.at[1])
    x_copy.wait()
    gain_copy.wait()
    normed[...], _ = norm_of(x_ref[...].astype(F32), gain_ref[...].reshape(1, width))
    for i, cols in enumerate(parts):
        in_copies[i].wait()
        if i == 0:
            out_copy.start()
        for at, part in tiles(cols.size, 256):
            band = pl.ds(cols.start + at, part)
            pre = dot(normed[...], w_in[:, band])
            tanh = jnp.tanh(GELU_A * (pre + GELU_B * (pre * pre * pre)))
            active[:, band] = (pre * (0.5 * (1.0 + tanh))).astype(BF16)
    out_copy.wait()
    for at, part in tiles(rows, 256):
        band = pl.ds(at, part)
        total = x_ref[band, :].astype(F32) + dot(active[band, :], w_out[...])
        enc_ref[band, :] = total.astype(BF16)


def encode(flat_rows, enc_gain, w_in, w_out):
    rows, width = flat_rows.shape
    hidden = w_in.shape[1]
    return pl.pallas_call(
        encode_kernel,
        in_specs=[anywhere()] * 4,
        out_specs=vmem(),
        out_shape=pltpu.VMEM((rows, width), BF16),
        scratch_shapes=[
            pltpu.VMEM((width,), F32),
            pltpu.VMEM((rows, width), BF16),
            pltpu.VMEM((width, hidden), BF16),
            pltpu.VMEM((hidden, width), BF16),
            pltpu.VMEM((rows, width), BF16),
            pltpu.VMEM((rows, hidden), BF16),
            pltpu.SemaphoreType.DMA((3,)),
            pltpu.SemaphoreType.DMA((2,)),
        ],
        compiler_params=params(14),
        cost_estimate=pl.CostEstimate(
            flops=4 * rows * width * hidden,
            bytes_accessed=4 * width * hidden + 4 * rows * width,
            transcendentals=rows * hidden,
        ),
        name="encode",
    )(*hbm(enc_gain, flat_rows, w_in, w_out))


def send_kernel(masks, ids_ref, me_ref, enc_ref, h_hbm, *refs):
    out_refs, (h_ref, h_sem, sems) = refs[:-3], refs[-3:]
    h_copy = pltpu.make_async_copy(h_hbm, h_ref, h_sem)
    h_copy.start()
    row_count = enc_ref.shape[0]
    capacity = out_refs[0].shape[0]
    me = me_ref[0]

    def copy_of(k, row, place):
        return pltpu.make_async_copy(enc_ref.at[row], out_refs[k].at[place], sems.at[k, place])

    for k, mask in enumerate(masks):
        each_request(
            ids_ref, me ^ mask, me * row_count, row_count, capacity,
            lambda row, place: copy_of(k, row, place).start(),
        )
    for k, mask in enumerate(masks):
        each_request(
            ids_ref, me ^ mask, me * row_count, row_count, capacity,
            lambda row, place: copy_of(k, row, place).wait(),
        )
    h_copy.wait()


def send_rows(all_ids, me, encoded, tokens, capacity, masks):
    row_count, piece, width = encoded.shape
    groups = all_ids.shape[0]
    return pl.pallas_call(
        functools.partial(send_kernel, masks),
        in_specs=[smem(), smem(), vmem(), anywhere()],
        out_specs=[anywhere()] * groups + [vmem()],
        out_shape=[jax.ShapeDtypeStruct((capacity, piece, width), BF16)] * groups
        + [pltpu.VMEM(tokens.shape, BF16)],
        scratch_shapes=[
            pltpu.SemaphoreType.DMA,
            pltpu.SemaphoreType.DMA((groups, capacity)),
        ],
        compiler_params=params(4),
        name="send_rows",
    )(all_ids, me, encoded, *hbm(tokens))


def query_kernel(h_ref, d_ref, w_hbm, out_ref, edge_ref, blocks, total, sems):
    part = blocks.shape[1]
    count = h_ref.shape[1] // part
    copies = [
        pltpu.make_async_copy(w_hbm.at[pl.ds(i * part, part), :], blocks.at[i % 3], sems.at[i % 3])
        for i in range(count)
    ]
    for copy in copies[:3]:
        copy.start()
    for i in range(count):
        copies[i].wait()
        value = dot(h_ref[:, pl.ds(i * part, part)], blocks[i % 3])
        total[...] = value if i == 0 else total[...] + value
        if i + 3 < count:
            copies[i + 3].start()
    out_ref[...] = total[...].astype(BF16)
    edge_ref[:STRETCH, :] = total[:STRETCH, :].astype(BF16)
    edge_ref[STRETCH:, :] = d_ref[:STRETCH, :]


def query(tokens, w_query, cotangent):
    count, depth = tokens.shape
    feats = w_query.shape[1]
    return pl.pallas_call(
        query_kernel,
        in_specs=[vmem()] * 2 + [anywhere()],
        out_specs=[vmem()] * 2,
        out_shape=[
            jax.ShapeDtypeStruct((count, feats), BF16),
            jax.ShapeDtypeStruct((2 * STRETCH, feats), BF16),
        ],
        scratch_shapes=[
            pltpu.VMEM((3, 1024, feats), BF16),
            pltpu.VMEM((count, feats), F32),
            pltpu.SemaphoreType.DMA((3,)),
        ],
        compiler_params=params(12),
        cost_estimate=pl.CostEstimate(
            flops=2 * count * depth * feats,
            bytes_accessed=2 * depth * feats + 4 * count * feats,
            transcendentals=0,
        ),
        name="query",
    )(tokens, cotangent, *hbm(w_query))


def places_of(ids_ref, me, row_count, capacity):
    fan_out, stretch_count = ids_ref.shape
    ids = [ids_ref[s % fan_out, s // fan_out] for s in range(fan_out * stretch_count)]
    if row_count & (row_count - 1):
        owners = [lax.div(row, jnp.int32(row_count)) for row in ids]
    else:
        bits = jnp.int32(row_count.bit_length() - 1)
        owners = [lax.shift_right_logical(row, bits) for row in ids]
    places = []
    for s, owner in enumerate(owners):
        rank = jnp.int32(0)
        for other in owners[:s]:
            rank = rank + (other == owner).astype(jnp.int32)
        places.append((owner ^ me, jnp.minimum(rank, capacity - 1)))
    return places


def pick_kernel(row_count, masks, halves, ids_ref, me_ref, *refs):
    arrived_refs, refs = refs[: len(masks)], refs[len(masks) :]
    out_refs, sems = refs[:halves], refs[halves]
    capacity = arrived_refs[0].shape[0]
    slots = out_refs[0].shape[0]
    for s, (mask, rank) in enumerate(places_of(ids_ref, me_ref[0], row_count, capacity)):
        out_ref = out_refs[s // slots]
        for here, ref in zip(masks, arrived_refs):

            @pl.when(mask == here)
            def _():
                pltpu.make_async_copy(ref.at[rank], out_ref.at[s % slots], sems.at[s]).start()

    for s in range(slots * halves):
        out_ref = out_refs[s // slots].at[s % slots]
        pltpu.make_async_copy(arrived_refs[0].at[0], out_ref, sems.at[s]).wait()


def pick_rows(neighbours, me, arrived, row_count, masks, halves):
    capacity, piece, width = arrived[0].shape
    slots = neighbours.size
    return pl.pallas_call(
        functools.partial(pick_kernel, row_count, masks, halves),
        in_specs=[smem(), smem()] + [anywhere()] * len(arrived),
        out_specs=[anywhere()] * halves,
        out_shape=[jax.ShapeDtypeStruct((slots // halves, piece, width), BF16)] * halves,
        scratch_shapes=[pltpu.SemaphoreType.DMA((slots,))],
        compiler_params=params(4),
        name="pick_rows",
    )(neighbours, me, *arrived)


def return_kernel(row_count, masks, counts, ids_ref, me_ref, *refs):
    share_refs, refs = refs[: sum(counts)], refs[sum(counts) :]
    out_refs, (total, sems) = refs[: len(masks)], refs[len(masks) :]
    shares = []
    for count in counts:
        shares.append(share_refs[:count])
        share_refs = share_refs[count:]
    capacity = out_refs[0].shape[0]
    slots = total.shape[0]
    for s, (mask, rank) in enumerate(places_of(ids_ref, me_ref[0], row_count, capacity)):
        value = None
        for share in shares:
            each = slots // len(share)
            part = share[s // each][s % each].astype(F32)
            value = part if value is None else value + part
        total[s] = value.astype(BF16)
        for here, ref in zip(masks, out_refs):

            @pl.when(mask == here)
            def _():
                pltpu.make_async_copy(total.at[s], ref.at[rank], sems.at[s]).start()

    for s in range(slots):
        pltpu.make_async_copy(total.at[s], out_refs[0].at[0], sems.at[s]).wait()


def return_grads(neighbours, me, shares, row_count, masks, capacity):
    _, piece, width = shares[0][0].shape
    slots = neighbours.size
    groups = len(masks)
    counts = [len(share) for share in shares]
    return pl.pallas_call(
        functools.partial(return_kernel, row_count, masks, counts),
        in_specs=[smem(), smem()] + [vmem()] * sum(counts),
        out_specs=[anywhere()] * groups,
        out_shape=[jax.ShapeDtypeStruct((capacity, piece, width), BF16)] * groups,
        scratch_shapes=[
            pltpu.VMEM((slots, piece, width), BF16),
            pltpu.SemaphoreType.DMA((slots,)),
        ],
        compiler_params=params(8),
        name="return_grads",
    )(neighbours, me, *[part for share in shares for part in share])


def fill_keys(x, wk_ref, wv_ref, keys, values):
    for w_ref, out in ((wk_ref, keys), (wv_ref, values)):
        for at, part in tiles(w_ref.shape[1], 256):
            cols = pl.ds(at, part)
            out[:, cols] = dot(x, w_ref[:, cols]).astype(BF16)


def project_kernel(count, *refs):
    piece_refs, (wk_ref, wv_ref, *out_refs) = refs[:-2 - 2 * count], refs[-2 - 2 * count :]
    each = len(piece_refs) // count
    for i in range(count):
        x = [ref[...] for ref in piece_refs[i * each : (i + 1) * each]]
        x = jnp.concatenate(x, axis=0)
        fill_keys(x, wk_ref, wv_ref, out_refs[2 * i], out_refs[2 * i + 1])


def project(halves, w_key, w_value):
    pieces = [piece for half in halves for piece in half]
    rows, width = pieces[0].shape
    rows *= len(halves[0])
    feats = w_key.shape[1]
    count = len(halves)
    out = pl.pallas_call(
        functools.partial(project_kernel, count),
        in_specs=[vmem()] * (len(pieces) + 2),
        out_specs=[vmem()] * (2 * count),
        out_shape=[jax.ShapeDtypeStruct((rows, feats), BF16)] * (2 * count),
        compiler_params=params(16),
        cost_estimate=pl.CostEstimate(
            flops=4 * count * rows * width * feats,
            bytes_accessed=4 * width * feats + 2 * count * rows * (width + 2 * feats),
            transcendentals=0,
        ),
        name="project",
    )(*pieces, w_key, w_value)
    return [out[2 * i : 2 * i + 2] for i in range(count)]


def two_blocks(value):
    zeros = jnp.zeros((value.shape[0], HD), value.dtype)
    top = jnp.concatenate([value[:, :HD], zeros], axis=1)
    low = jnp.concatenate([zeros, value[:, HD:]], axis=1)
    return jnp.concatenate([top, low], axis=0)


def moved_up(rows, by):
    return pltpu.roll(rows.astype(F32), rows.shape[0] - by, 0)


def attend_kernel(far_count, first, count, has_edges, *refs):
    near_refs, far_refs, refs = refs[:2], refs[2 : 2 + far_count], refs[2 + far_count :]
    weight_refs, token_refs, refs = refs[:2], refs[2 : 4 + has_edges], refs[4 + has_edges :]
    att_ref, near_dk, near_dv, far_dk, far_dv, far_k, far_v, block_q, block_d = refs
    x = jnp.concatenate([ref[...] for ref in far_refs], axis=0)
    fill_keys(x, *weight_refs, far_k, far_v)
    rows = far_refs[0].shape[0]
    part = rows // count
    block = STRETCH
    for i, out in enumerate((block_q, block_d)):
        own = token_refs[i]
        begin = first * block + block - 16
        size = own.shape[0] - begin if has_edges else count * block + 16
        for at, wide in tiles(own.shape[1], 256):
            cols = pl.ds(at, wide)
            values = own[pl.ds(begin, size), cols]
            if has_edges:
                edge = token_refs[2][pl.ds(i * block, block), cols]
                values = jnp.concatenate([values, edge], axis=0)
            out[:, cols] = moved_up(values, 15)[: count * block].astype(BF16)
    scale = HD ** (-0.5)

    def bands(near, far, c):
        at = [(ref, i) for ref in (near, far) for i in range(far_count)]
        return [(ref, pl.ds(pl.multiple_of(i * rows + c * part, part), part)) for ref, i in at]

    def stretch(c, carry):
        mine = pl.ds(pl.multiple_of(c * block, block), block)
        for h in range(0, block_q.shape[1], 2 * HD):
            cols = pl.ds(h, 2 * HD)
            here = [bands(near_refs[0], far_k, c), bands(near_refs[1], far_v, c)]
            k, v = (jnp.concatenate([ref[b, cols] for ref, b in pair], axis=0) for pair in here)
            q, d = two_blocks(block_q[mine, cols]), two_blocks(block_d[mine, cols])
            scores = dot_nt(k, q) * scale
            weights = jnp.exp(scores - jnp.max(scores, axis=0, keepdims=True))
            probability = weights * (1.0 / jnp.sum(weights, axis=0, keepdims=True))
            rounded = probability.astype(BF16)
            out = dot_tn(rounded, v)
            att_ref[mine, cols] = jnp.concatenate(
                [out[:block, :HD], out[block:, HD:]], axis=1
            ).astype(BF16)
            value_grads = dot(rounded, d).astype(BF16)
            dprobs = dot_nt(v, d)
            centre = jnp.sum(probability * dprobs, axis=0, keepdims=True)
            dscores = (probability * (dprobs - centre)).astype(BF16)
            key_grads = (dot(dscores, q) * scale).astype(BF16)
            for i, (ref, b) in enumerate(bands(near_dk, far_dk, c)):
                ref[b, cols] = key_grads[i * part : (i + 1) * part]
            for i, (ref, b) in enumerate(bands(near_dv, far_dv, c)):
                ref[b, cols] = value_grads[i * part : (i + 1) * part]
        return carry

    lax.fori_loop(0, count, stretch, 0)


def attend(near, far, w_key, w_value, tokens, first, count):
    width, feats = w_key.shape
    rows = near[0].shape[0]
    return pl.pallas_call(
        functools.partial(attend_kernel, len(far), first, count, len(tokens) - 2),
        in_specs=[vmem()] * (4 + len(far) + len(tokens)),
        out_specs=[vmem()] * 5,
        out_shape=[jax.ShapeDtypeStruct((count * STRETCH, feats), BF16)]
        + [jax.ShapeDtypeStruct((rows, feats), BF16)] * 4,
        scratch_shapes=[pltpu.VMEM((rows, feats), BF16)] * 2
        + [pltpu.VMEM((count * STRETCH, feats), BF16)] * 2,
        compiler_params=params(20),
        cost_estimate=pl.CostEstimate(
            flops=4 * rows * width * feats + 40 * rows * STRETCH * feats,
            bytes_accessed=4 * width * feats + 12 * rows * feats,
            transcendentals=2 * rows * STRETCH * feats // HD,
        ),
        name="attend",
    )(*near, *far, w_key, w_value, *tokens)


def terms_kernel(number, *refs):
    *grad_refs, wk_ref, wv_ref, term_ref = refs

    def rows_of(halves):
        part = term_ref.shape[0] // len(halves)
        return jnp.concatenate([ref[pl.ds(number * part, part), :] for ref in halves], axis=0)

    half = len(grad_refs) // 2
    term = dot_nt(rows_of(grad_refs[:half]), wk_ref[...])
    term = term + dot_nt(rows_of(grad_refs[half:]), wv_ref[...])
    term_ref[...] = term.astype(BF16)


def slot_terms(key_grads, value_grads, w_key, w_value, number, rows):
    width, feats = w_key.shape
    return pl.pallas_call(
        functools.partial(terms_kernel, number),
        in_specs=[vmem()] * (len(key_grads) + len(value_grads) + 2),
        out_specs=vmem(),
        out_shape=jax.ShapeDtypeStruct((rows, width), BF16),
        compiler_params=params(16),
        cost_estimate=pl.CostEstimate(
            flops=4 * rows * width * feats,
            bytes_accessed=4 * width * feats + 2 * rows * (width + 2 * feats),
            transcendentals=0,
        ),
        name="slot_terms",
    )(*key_grads, *value_grads, w_key, w_value)


def stage_kernel(
    gain_ref, x_ref, w_in_ref, w_out_ref, inv_ref, slope_ref, w_in_turned, w_out_turned, normed
):
    rows, width = x_ref.shape
    normed[...], inv_ref[...] = norm_of(
        x_ref[...].astype(F32), gain_ref[...].reshape(1, width)
    )
    for at, part in tiles(w_in_ref.shape[1], 256):
        cols = pl.ds(at, part)
        pre = dot(normed[...], w_in_ref[:, cols])
        square = pre * pre
        tanh = jnp.tanh(GELU_A * pre * (1.0 + GELU_B * square))
        slope_ref[:, cols] = 0.5 * (1.0 + tanh) + 0.5 * pre * (1.0 - tanh * tanh) * (
            GELU_A * (1.0 + 3.0 * GELU_B * square)
        )
        w_in_turned[cols, :] = w_in_ref[:, cols].T
        w_out_turned[:, cols] = w_out_ref[cols, :].T


def stage(flat_rows, enc_gain, w_in, w_out):
    rows, width = flat_rows.shape
    hidden = w_in.shape[1]
    return pl.pallas_call(
        stage_kernel,
        in_specs=[vmem()] * 4,
        out_specs=[vmem()] * 4,
        out_shape=[
            jax.ShapeDtypeStruct((rows, 1), F32),
            jax.ShapeDtypeStruct((rows, hidden), F32),
            jax.ShapeDtypeStruct((hidden, width), BF16),
            jax.ShapeDtypeStruct((width, hidden), BF16),
        ],
        scratch_shapes=[pltpu.VMEM((rows, width), BF16)],
        compiler_params=params(24),
        cost_estimate=pl.CostEstimate(
            flops=2 * rows * width * hidden,
            bytes_accessed=8 * width * hidden + 4 * rows * hidden + 4 * rows * width,
            transcendentals=rows * hidden,
        ),
        name="stage",
    )(enc_gain, flat_rows, w_in, w_out)


def encode_back_kernel(
    masks, ids_ref, me_ref, gain_ref, x_ref, inv_ref, slope_ref, w_in_turned, w_out_turned, *refs
):
    arrived_refs, (out_ref, row_grad, upstream, d_pre) = refs[:-4], refs[-4:]
    capacity, piece, width = arrived_refs[0].shape
    row_count = row_grad.shape[0]
    rows = x_ref.shape[0]
    row_grad[...] = jnp.zeros_like(row_grad)
    me = me_ref[0]
    for mask, ref in zip(masks, arrived_refs):

        def add(row, place):
            row_grad[row] += ref[place].astype(F32)

        each_request(ids_ref, me ^ mask, me * row_count, row_count, capacity, add)
    upstream[...] = row_grad[...].reshape(upstream.shape).astype(BF16)
    for at, part in tiles(w_out_turned.shape[1], 256):
        cols = pl.ds(at, part)
        d_act = dot(upstream[...], w_out_turned[:, cols])
        d_pre[:, cols] = (d_act * slope_ref[:, cols]).astype(BF16)
    gain = gain_ref[...].reshape(1, width)
    for at, part in tiles(rows, 256):
        band = pl.ds(at, part)
        scaled = dot(d_pre[band, :], w_in_turned[...]) * gain
        x = x_ref[band, :].astype(F32)
        inverse = inv_ref[band, :]
        mean = jnp.mean(scaled * x, axis=-1, keepdims=True)
        back = inverse * scaled - x * (inverse * inverse * inverse * mean)
        summed = row_grad[at // piece : (at + part) // piece].reshape(part, width)
        out_ref[band, :] = (summed + back).astype(BF16)


def encode_back(all_ids, me, enc_gain, flat_rows, staged, arrived, masks):
    rows, hidden = staged[1].shape
    _, piece, width = arrived[0].shape
    return pl.pallas_call(
        functools.partial(encode_back_kernel, masks),
        in_specs=[smem(), smem()] + [vmem()] * (6 + len(arrived)),
        out_specs=vmem(),
        out_shape=jax.ShapeDtypeStruct((rows, width), BF16),
        scratch_shapes=[
            pltpu.VMEM((rows // piece, piece, width), F32),
            pltpu.VMEM((rows, width), BF16),
            pltpu.VMEM((rows, hidden), BF16),
        ],
        compiler_params=params(28),
        cost_estimate=pl.CostEstimate(
            flops=4 * rows * width * hidden,
            bytes_accessed=4 * width * hidden + 4 * rows * hidden + 8 * rows * width,
            transcendentals=0,
        ),
        name="encode_back",
    )(all_ids, me, enc_gain, flat_rows, *staged, *arrived)


def shift(value, axis, by):
    peers = lax.axis_size(axis)
    pairs = [(i, i + by) for i in range(peers) if 0 <= i + by < peers]
    return lax.ppermute(value, axis, pairs)


def swap(value, axis, bit):
    return lax.ppermute(value, axis, [(i, i ^ bit) for i in range(lax.axis_size(axis))])


def exchange(buffers, masks, later):
    axes = ("role", "seq")
    count = len(buffers)
    arrived = [buffers[0]] + [swap(buffers[k], axes, masks[k]) for k in range(1, count - 2)]
    for early, k in ((1, count - 2), (2, count - 1)):
        arrived[early], value, later = lax.optimization_barrier((arrived[early], buffers[k], later))
        arrived.append(swap(value, axes, masks[k]))
    return arrived, later


def add_up(shares):
    if len(shares) == 1:
        return shares[0]
    return functools.reduce(jnp.add, [share.astype(F32) for share in shares]).astype(BF16)


def body(hidden, w_query, w_key, w_value, enc_gain, w_in, w_out, db_states, neighbours, d_attended):
    groups = lax.axis_size(("role", "seq"))
    shards = lax.axis_size("tp")
    me = lax.axis_index(("role", "seq")).astype(jnp.int32).reshape(1)
    masks = exchange_masks(groups, lax.axis_size("seq"))
    row_count, piece, width = db_states.shape
    stretch_count, fan_out = neighbours.shape
    slots = stretch_count * fan_out
    tokens = hidden.shape[0]
    edge = STRETCH - 1
    capacity = max(2, 2 * ((stretch_count - 1 + groups - 2) // (groups - 1)))
    neighbours = neighbours.T
    all_ids = lax.all_to_all(
        jnp.broadcast_to(neighbours[None], (groups, fan_out, stretch_count)),
        ("role", "seq"), 0, 0, tiled=True,
    )
    flat_rows = db_states.reshape(row_count * piece, width)
    encoded = encode(flat_rows, enc_gain, w_in, w_out)
    *outgoing, hidden = send_rows(
        all_ids, me, encoded.reshape(row_count, piece, width), hidden, capacity, masks
    )
    arrived, (d_attended,) = exchange(outgoing, masks, (d_attended,))
    queries, edges = query(hidden, w_query, d_attended)
    queries, neighbours = lax.optimization_barrier((queries, neighbours))
    count = stretch_count // 2
    first_own, last_own = [
        value.reshape(slots * piece // 2, width)
        for value in pick_rows(neighbours, me, arrived, row_count, masks, 2)
    ]
    first_own, edges = lax.optimization_barrier((first_own, edges))
    edges = shift(edges, "seq", -1)
    bits = [1 << i for i in range(shards.bit_length() - 1)]
    half = shards // 2

    def gathered(pieces):
        for bit in reversed(bits[:-1]):
            pieces.update({mask | bit: swap(pieces[mask], "tp", bit) for mask in list(pieces)})
        return [pieces[mask] for mask in sorted(pieces)]

    first_far = swap(first_own, "tp", half)
    first_near = gathered({0: first_own})
    last_far = swap(last_own, "tp", half)
    last_near = gathered({0: last_own})
    first_kv, last_kv = project([first_near, last_near], w_key, w_value)
    first_far, first_kv, last_kv = lax.optimization_barrier((first_far, first_kv, last_kv))
    first_o, *first_grads = attend(
        first_kv, gathered({half: first_far}), w_key, w_value, (queries, d_attended), 0, count
    )
    first_o, last_far = lax.optimization_barrier((first_o, last_far))
    last_far = gathered({half: last_far})

    rows = slots * piece // 2

    def fold(shares):
        for bit in bits[:-1]:
            for mask in sorted([mask for mask in shares if mask & bit], reverse=True):
                shares[mask ^ bit].append(swap(add_up(shares.pop(mask)), "tp", bit))
        return shares[0]

    def to_send(grads, tied):
        terms = {
            j: [slot_terms(grads[2:3], grads[3:], w_key, w_value, j, rows)]
            for j in reversed(range(1, half))
        }
        near = {0: []}
        near.update({
            j: [slot_terms(grads[0:1], grads[1:2], w_key, w_value, j, rows)]
            for j in reversed(range(1, half))
        })
        tied, grads = lax.optimization_barrier((tied, grads))
        terms[0] = [slot_terms(grads[2:3], grads[3:], w_key, w_value, 0, rows)]
        return add_up(fold(terms)), fold(near), tied

    sent, first_core, edges = to_send(first_grads, edges)
    sent, edges = lax.optimization_barrier((sent, edges))
    first_back = swap(sent, "tp", half)
    last_o, *last_grads = attend(
        last_kv, last_far, w_key, w_value, (queries, d_attended, edges), count, count
    )
    o_edge = shift(last_o[last_o.shape[0] - STRETCH :], "seq", 1)
    sent, last_core, first_back = to_send(last_grads, first_back)
    last_back = swap(sent, "tp", half)
    own_term = slot_terms(
        (first_grads[0], last_grads[0]), (first_grads[1], last_grads[1]),
        w_key, w_value, 0, slots * piece,
    )
    shares = [[own_term]] + [list(pair) for pair in zip(first_core, last_core)]
    shares.append([first_back, last_back])
    shares = [[part.reshape(-1, piece, width) for part in share] for share in shares]
    shares, o_edge = lax.optimization_barrier((shares, o_edge))
    outgoing_grads = return_grads(neighbours, me, shares, row_count, masks, capacity)
    attended = jnp.concatenate([o_edge[1:], first_o, last_o[: last_o.shape[0] - edge]], axis=0)
    totals, (flat_rows,) = exchange(outgoing_grads, masks, (flat_rows,))
    staged = stage(flat_rows, enc_gain, w_in, w_out)
    grads = encode_back(all_ids, me, enc_gain, flat_rows, staged, totals, masks)
    return (attended, grads.reshape(row_count, piece, width))


def solution(mesh):
    in_specs = (
        P(("role", "seq"), None),
        P(None, "tp"),
        P(None, "tp"),
        P(None, "tp"),
        P(),
        P(),
        P(),
        P(("role", "seq"), "tp", None),
        P(("role", "seq"), None),
        P(("role", "seq"), "tp"),
    )
    out_specs = (P(("role", "seq"), "tp"), P(("role", "seq"), "tp", None))
    return jax.shard_map(body, mesh=mesh, in_specs=in_specs, out_specs=out_specs, check_vma=False)
```

time: 421 us -> 122 us (0.29); the launches traced: 413 us -> 122 us
  waiting for transfers between devices: 212 us -> 22.6 us
  matrix products: 75.8 us -> 0 us
  local copies, waits for them, and re-layouts: 56.4 us -> 1.38 us
  Pallas kernels: 0 us -> 54 us
  starting transfers between devices: 13 us -> 42 us
  blocking collectives: 22.6 us -> 0 us
  other arithmetic: 18.3 us -> 1.02 us
  between operations: 15 us -> 0.98 us
    all_to_all x2 -> x1, waiting for transfers between devices: 115 us -> 0.01 us  [body(): lax.all_to_all(jnp.broadcast_to(neighbours[None], (groups, fan_out, stret...]
    dot_general x14 -> x0, matrix products: 75.8 us -> none  [the longest x1 11.2 us: attend_back(): jnp.einsum('bhqk,bqhe->bkhe', dscores, queries, preferred_element_type=jn...]
    pallas_call x0 -> x17, Pallas kernels: none -> 54 us  [the longest x2 9.67 us: attend(): pl.pallas_call(functools.partial(attend_kernel, len(far), first, count, l...]
    reduce_scatter x1 -> x0, waiting for transfers between devices: 40.7 us -> none  [body(): lax.psum_scatter(term.reshape(piece_len * lax.axis_size('tp'), slot_count...]
    ppermute x2 -> x28, waiting for transfers between devices: 55.8 us -> 22.6 us  [the longest x26 18.4 us: swap(): lax.ppermute(value, axis, [(i, i ^ bit) for i in range(lax.axis_size(axis...]
    ppermute x2 -> x28, starting transfers between devices: 3.56 us -> 34.7 us  [the longest x26 31.2 us: swap(): lax.ppermute(value, axis, [(i, i ^ bit) for i in range(lax.axis_size(axis...]
    all_gather x1 -> x0, blocking collectives: 22.6 us -> none  [body(): lax.all_gather(neighbours, ('role', 'seq'), axis=0, tiled=True)]
    reshape x7 -> x0, local copies, waits for them, and re-layouts: 14.8 us -> none  [the longest x1 4.17 us: body(): value_grads.astype(jnp.bfloat16).reshape(slot_count, row_tokens, feat_dev)]
  transfers between devices with their start and end apart: 5 -> 29, of which waited for: 5 -> 8; matrix products, arithmetic and copies ran while one was open for 6% -> 1% of each run, Pallas kernels for 0% -> 33%
where the time goes in v1:
time: 122 us
  Pallas kernels  54 us (44%)
  starting transfers between devices  42 us (34%)
  waiting for transfers between devices  22.6 us (19%)
  local copies, waits for them, and re-layouts  1.38 us (1%)
    ppermute x26, starting transfers between devices, swap(): lax.ppermute(value, axis, [(i, i ^ bit) for i in range(lax.axis_size(axis...  31.2 us
    ppermute x26, waiting for transfers between devices, swap(): lax.ppermute(value, axis, [(i, i ^ bit) for i in range(lax.axis_size(axis...  18.4 us
    pallas_call x2, Pallas kernels, attend(): pl.pallas_call(functools.partial(attend_kernel, len(far), first, count, l...  9.67 us
    pallas_call x7, Pallas kernels, slot_terms(): pl.pallas_call(functools.partial(terms_kernel, number), in_specs=[vmem()]...  8.87 us
    pallas_call x1, Pallas kernels, query(): pl.pallas_call(query_kernel, in_specs=[vmem()] * 2 + [anywhere()], out_sp...  8.32 us
    all_to_all x1, starting transfers between devices, body(): lax.all_to_all(jnp.broadcast_to(neighbours[None], (groups, fan_out, stret...  7.25 us
    pallas_call x1, Pallas kernels, encode_back(): pl.pallas_call(functools.partial(encode_back_kernel, masks), in_specs=[sm...  7.16 us
    pallas_call x1, Pallas kernels, encode(): pl.pallas_call(encode_kernel, in_specs=[anywhere()] * 4, out_specs=vmem()...  6.94 us
  transfers between devices with their start and end apart: 29, of which 8 were waited for; matrix products, arithmetic and copies ran while one was open for 1% of the time, Pallas kernels for 33%

profile of v1, /device:TPU:0, one launch (start us, length us, event | category | flops | bytes accessed | tf_op | source)
XLA Modules:
  0.0 122.0 jit_solution(11283018828853599367)
XLA Ops:
  0.6 1.3 %broadcast_in_dim.2 = s32[8,2,4]{2,1,0:T(2,128)} broadcast(s32[2,4]{1,0:T(2,128)} %bitcast.21), dimensions={1,2} | broadcast | bytes 288 | tf_op jit(solution)/shard_map/broadcast_in_dim | solution.py:624
  1.9 7.3 %all-to-all-start = ((s32[8,2,4]{2,1,0:T(2,128)}), s32[8,2,4]{2,1,0:T(2,128)S(1)}, u32[]{:S(2)}, u32[]{:S(2)}) async-start(s32[8,2,4]{2,1,0:T(2,128)} %broadcast_in_dim.2), calls=%async_computation | async-start | bytes 16384 | tf_op jit(solution)/shard_map/all_to_all | solution.py:623
  9.2 6.9 %encode.1 = bf16[512,896]{1,0:T(8,128)(2,1)S(1)} custom-call(f32[896]{0:T(1024)} %gain_ref.3, bf16[512,896]{1,0:T(8,128)(2,1)} %bitcast.12, bf16[896,1792]{1,0:T(8,128)(2,1)} %w_in_ref.1, bf16[1792,896]{1,0:T(8,128)(2,1)} %w_out_ref.1), custom_call_target="tpu_custom_call" | custom-call | flops 3288334336 | bytes 8257536 | tf_op jit(solution)/shard_map/encode/pallas_call | solution.py:125
  16.1 3.1 %send_rows.1 = (bf16[2,32,896]{2,1,0:T(8,128)(2,1)S(1)}, bf16[2,32,896]{2,1,0:T(8,128)(2,1)S(1)}, bf16[2,32,896]{2,1,0:T(8,128)(2,1)S(1)}, bf16[2,32,896]{2,1,0:...) custom-call(s32[8,2,4]{2,1,0:T(2,128)S(1)} %all-to-all-done.ids_ref,, ...), custom_call_target="tpu_custom_call" | custom-call | tf_op jit(solution)/shard_map/send_rows/pallas_call | solution.py:177
  19.3 2.0 %collective-permute-start.1 = (bf16[2,32,896]{2,1,0:T(8,128)(2,1)S(1)}, bf16[2,32,896]{2,1,0:T(8,128)(2,1)S(1)}, u32[]{:S(2)}, u32[]{:S(2)}) collective-permute-start(bf16[2,32,896]{2,1,0:T(8,128)(2,1)S(1)} %get-tuple-element.81), channel_id=1, source_target_pairs={{0,16},{4,20},{8,24},{12,28},{16,0},{20,4},{24,8},{28,12},{1,17},{... | collective-permute-start | bytes 344072 | tf_op jit(solution)/shard_map/ppermute | solution.py:592
  21.2 1.5 %collective-permute-start = (bf16[2,32,896]{2,1,0:T(8,128)(2,1)S(1)}, bf16[2,32,896]{2,1,0:T(8,128)(2,1)S(1)}, u32[]{:S(2)}, u32[]{:S(2)}) collective-permute-start(bf16[2,32,896]{2,1,0:T(8,128)(2,1)S(1)} %get-tuple-element.79), channel_id=1, source_target_pairs={{0,20},{4,16},{8,28},{12,24},{16,4},{20,0},{24,12},{28,8},{1,21},{... | collective-permute-start | bytes 344072 | tf_op jit(solution)/shard_map/ppermute | solution.py:592
  22.7 3.3 %collective-permute-start.2 = (bf16[2,32,896]{2,1,0:T(8,128)(2,1)S(1)}, bf16[2,32,896]{2,1,0:T(8,128)(2,1)S(1)}, u32[]{:S(2)}, u32[]{:S(2)}) collective-permute-start(bf16[2,32,896]{2,1,0:T(8,128)(2,1)S(1)} %get-tuple-element.90), channel_id=1, source_target_pairs={{0,28},{4,24},{8,20},{12,16},{16,12},{20,8},{24,4},{28,0},{1,29},{... | collective-permute-start | bytes 344072 | tf_op jit(solution)/shard_map/ppermute | solution.py:592
  26.0 2.9 %collective-permute-start.4 = (bf16[2,32,896]{2,1,0:T(8,128)(2,1)S(1)}, bf16[2,32,896]{2,1,0:T(8,128)(2,1)S(1)}, u32[]{:S(2)}, u32[]{:S(2)}) collective-permute-start(bf16[2,32,896]{2,1,0:T(8,128)(2,1)S(1)} %get-tuple-element.92), channel_id=1, source_target_pairs={{0,12},{4,8},{8,4},{12,0},{16,28},{20,24},{24,20},{28,16},{1,13},{... | collective-permute-start | bytes 344072 | tf_op jit(solution)/shard_map/ppermute | solution.py:592
  28.9 2.9 %collective-permute-start.6 = (bf16[2,32,896]{2,1,0:T(8,128)(2,1)S(1)}, bf16[2,32,896]{2,1,0:T(8,128)(2,1)S(1)}, u32[]{:S(2)}, u32[]{:S(2)}) collective-permute-start(bf16[2,32,896]{2,1,0:T(8,128)(2,1)S(1)} %get-tuple-element.94), channel_id=1, source_target_pairs={{0,4},{4,0},{8,12},{12,8},{16,20},{20,16},{24,28},{28,24},{1,5},{5... | collective-permute-start | bytes 344072 | tf_op jit(solution)/shard_map/ppermute | solution.py:592
  31.8 1.7 %collective-permute-start.5 = (bf16[2,32,896]{2,1,0:T(8,128)(2,1)S(1)}, bf16[2,32,896]{2,1,0:T(8,128)(2,1)S(1)}, u32[]{:S(2)}, u32[]{:S(2)}) collective-permute-start(bf16[2,32,896]{2,1,0:T(8,128)(2,1)S(1)} %get-tuple-element.93), channel_id=1, source_target_pairs={{0,8},{4,12},{8,0},{12,4},{16,24},{20,28},{24,16},{28,20},{1,9},{5... | collective-permute-start | bytes 344072 | tf_op jit(solution)/shard_map/ppermute | solution.py:592
  33.5 8.3 %query.1 = (bf16[256,1024]{1,0:T(8,128)(2,1)S(1)}, bf16[128,1024]{1,0:T(8,128)(2,1)S(1)}) custom-call(bf16[256,8192]{1,0:T(8,128)(2,1)S(1)} %get-tuple-element.78.h_ref, bf16[256,1024]{1,0:T(8,128)(2,1)S(1)} %copy-done.2, bf16[8192,1024]{1,0:T(8,128)(2,1)} %w_hbm.1), custom_call_target="tpu_custom_call" | custom-call | flops 4294967296 | bytes 17825792 | tf_op jit(solution)/shard_map/query/pallas_call | solution.py:215
  41.9 3.5 %collective-permute-done.5.refs_6_ = bf16[2,32,896]{2,1,0:T(8,128)(2,1)S(1)} collective-permute-done((bf16[2,32,896]{2,1,0:T(8,128)(2,1)S(1)}, bf16[2,32,896]{2,1,0:T(8,128)(2,1)S(1)}, u32[]{:S(2)}, u32[]{:S(2)}) %collective-permute-start.5) | collective-permute-done | bytes 114720 | tf_op jit(solution)/shard_map/ppermute | solution.py:592
  45.4 2.0 %pick_rows.1 = (bf16[4,32,896]{2,1,0:T(8,128)(2,1)S(1)}, bf16[4,32,896]{2,1,0:T(8,128)(2,1)S(1)}) custom-call(s32[2,4]{1,0:T(2,128)S(1)} %bitcast.22, s32[1]{0:T(128)} %bitcast.1.me_ref, bf16[2,32,896]{2,1,0:T(8,128)(2,1)S(1)} %get-tuple-element.87.refs_0_, bf16[2,32,896]{2,1,0:T(8,128)(2,1)S(1)} %collective-permute-done.1.refs_1_, ...), custom_call_target="tpu_custom_call" | custom-call | tf_op jit(solution)/shard_map/pick_rows/pallas_call | solution.py:276
  47.4 0.5 collective-permute-start.9
  47.9 1.5 %collective-permute-start.7 = (bf16[128,896]{1,0:T(8,128)(2,1)S(1)}, bf16[128,896]{1,0:T(8,128)(2,1)S(1)}, u32[]{:S(2)}, u32[]{:S(2)}) collective-permute-start(bf16[128,896]{1,0:T(8,128)(2,1)S(1)} %bitcast.28), channel_id=1, source_target_pairs={{0,2},{1,3},{2,0},{3,1},{4,6},{5,7},{6,4},{7,5},{8,10},{9,11},{10,... | collective-permute-start | bytes 688136 | tf_op jit(solution)/shard_map/ppermute | solution.py:592
  49.5 2.3 %project.1 = (bf16[256,1024]{1,0:T(8,128)(2,1)S(1)}, bf16[256,1024]{1,0:T(8,128)(2,1)S(1)}, bf16[256,1024]{1,0:T(8,128)(2,1)S(1)}, bf16[256,1024]{1,0:T(8,128)(2,1)S(1)}) custom-call(bf16[128,896]{1,0:T(8,128)(2,1)S(1)} %bitcast.29, bf16[128,896]{1,0:T(8,128)(2,1)S(1)} %collective-permute-done.8.refs_1_, bf16[128,896]{1,0:T(8,128)(2,1)S(1)} %bitcast.25, ...), custom_call_target="tpu_custom_call" | custom-call | flops 1879048192 | bytes 6684672 | tf_op jit(solution)/shard_map/project/pallas_call | solution.py:354
  51.8 3.7 %collective-permute-done.7.refs_2_ = bf16[128,896]{1,0:T(8,128)(2,1)S(1)} collective-permute-done((bf16[128,896]{1,0:T(8,128)(2,1)S(1)}, bf16[128,896]{1,0:T(8,128)(2,1)S(1)}, u32[]{:S(2)}, u32[]{:S(2)}) %collective-permute-start.7) | collective-permute-done | bytes 229408 | tf_op jit(solution)/shard_map/ppermute | solution.py:592
  55.5 1.5 %collective-permute-start.11 = (bf16[128,896]{1,0:T(8,128)(2,1)S(1)}, bf16[128,896]{1,0:T(8,128)(2,1)S(1)}, u32[]{:S(2)}, u32[]{:S(2)}) collective-permute-start(bf16[128,896]{1,0:T(8,128)(2,1)S(1)} %bitcast.26), channel_id=1, source_target_pairs={{0,2},{1,3},{2,0},{3,1},{4,6},{5,7},{6,4},{7,5},{8,10},{9,11},{10,... | collective-permute-start | bytes 688136 | tf_op jit(solution)/shard_map/ppermute | solution.py:592
  57.1 1.3 %collective-permute-start.13 = (bf16[128,1024]{1,0:T(8,128)(2,1)S(1)}, bf16[128,1024]{1,0:T(8,128)(2,1)S(1)}, u32[]{:S(2)}, u32[]{:S(2)}) collective-permute-start(bf16[128,1024]{1,0:T(8,128)(2,1)S(1)} %get-tuple-element.112), channel_id=1, source_target_pairs={{4,0},{8,4},{12,8},{5,1},{9,5},{13,9},{6,2},{10,6},{14,10},{7,3},{... | collective-permute-start | bytes 786440 | tf_op jit(solution)/shard_map/ppermute | solution.py:588
  58.3 4.8 %attend.2 = (bf16[128,1024]{1,0:T(8,128)(2,1)S(1)}, bf16[256,1024]{1,0:T(8,128)(2,1)S(1)}, bf16[256,1024]{1,0:T(8,128)(2,1)S(1)}, bf16[256,1024]{1,0:T(8,128)(2,1)S(1)}, bf16[256,1024]{1,0:T(8,128)(2,1)S(1)}) custom-call(bf16[256,1024]{1,0:T(8,128)(2,1)S(1)} %get-tuple-element.103.refs_0_, bf16[256,1024]{1,0:T(8,128)(2,1)S(1)} %get-tuple-element.104.refs_1_, ...), custom_call_target="tpu_custom_call" | custom-call | flops 1610612736 | bytes 6815744 | tf_op jit(solution)/shard_map/attend/pallas_call | solution.py:439
  63.2 1.3 %slot_terms.8 = bf16[128,896]{1,0:T(8,128)(2,1)S(1)} custom-call(bf16[256,1024]{1,0:T(8,128)(2,1)S(1)} %get-tuple-element.116.refs_0_, bf16[256,1024]{1,0:T(8,128)(2,1)S(1)} %get-tuple-element.117.refs_1_, bf16[896,1024]{1,0:T(8,128)(2,1)S(1)} %copy-done, bf16[896,1024]{1,0:T(8,128)(2,1)S(1)} %copy-done.1), custom_call_target="tpu_custom_call" | custom-call | flops 469762048 | bytes 4423680 | tf_op jit(solution)/shard_map/slot_terms/pallas_call | solution.py:472
  64.8 2.6 %collective-permute-done.13.refs_8_ = bf16[128,1024]{1,0:T(8,128)(2,1)S(1)} collective-permute-done((bf16[128,1024]{1,0:T(8,128)(2,1)S(1)}, bf16[128,1024]{1,0:T(8,128)(2,1)S(1)}, u32[]{:S(2)}, u32[]{:S(2)}) %collective-permute-start.13) | collective-permute-done | bytes 262176 | tf_op jit(solution)/shard_map/ppermute | solution.py:588
  67.4 1.3 %slot_terms.7 = bf16[128,896]{1,0:T(8,128)(2,1)S(1)} custom-call(bf16[256,1024]{1,0:T(8,128)(2,1)S(1)} %get-tuple-element.116.refs_0_, bf16[256,1024]{1,0:T(8,128)(2,1)S(1)} %get-tuple-element.117.refs_1_, bf16[896,1024]{1,0:T(8,128)(2,1)S(1)} %copy-done, bf16[896,1024]{1,0:T(8,128)(2,1)S(1)} %copy-done.1), custom_call_target="tpu_custom_call" | custom-call | flops 469762048 | bytes 4423680 | tf_op jit(solution)/shard_map/slot_terms/pallas_call | solution.py:472
  68.7 0.6 collective-permute-start.17
  69.3 4.8 %attend.3 = (bf16[128,1024]{1,0:T(8,128)(2,1)S(1)}, bf16[256,1024]{1,0:T(8,128)(2,1)S(1)}, bf16[256,1024]{1,0:T(8,128)(2,1)S(1)}, bf16[256,1024]{1,0:T(8,128)(2,1)S(1)}, bf16[256,1024]{1,0:T(8,128)(2,1)S(1)}) custom-call(bf16[256,1024]{1,0:T(8,128)(2,1)S(1)} %get-tuple-element.108.refs_0_, bf16[256,1024]{1,0:T(8,128)(2,1)S(1)} %get-tuple-element.109.refs_1_, ...), custom_call_target="tpu_custom_call" | custom-call | flops 1610612736 | bytes 6815744 | tf_op jit(solution)/shard_map/attend/pallas_call | solution.py:439
  74.1 1.3 %slot_terms.13 = bf16[128,896]{1,0:T(8,128)(2,1)S(1)} custom-call(bf16[256,1024]{1,0:T(8,128)(2,1)S(1)} %get-tuple-element.126.refs_0_, bf16[256,1024]{1,0:T(8,128)(2,1)S(1)} %get-tuple-element.127.refs_1_, bf16[896,1024]{1,0:T(8,128)(2,1)S(1)} %copy-done, bf16[896,1024]{1,0:T(8,128)(2,1)S(1)} %copy-done.1), custom_call_target="tpu_custom_call" | custom-call | flops 469762048 | bytes 4423680 | tf_op jit(solution)/shard_map/slot_terms/pallas_call | solution.py:472
  75.7 1.3 %slot_terms.10 = bf16[128,896]{1,0:T(8,128)(2,1)S(1)} custom-call(bf16[256,1024]{1,0:T(8,128)(2,1)S(1)} %get-tuple-element.107.refs_0_, bf16[256,1024]{1,0:T(8,128)(2,1)S(1)} %get-tuple-element.113.refs_2_.refs_1_, bf16[896,1024]{1,0:T(8,128)(2,1)S(1)} %copy-done, bf16[896,1024]{1,0:T(8,128)(2,1)S(1)} %copy-done.1), custom_call_target="tpu_custom_call" | custom-call | flops 469762048 | bytes 4423680 | tf_op jit(solution)/shard_map/slot_terms/pallas_call | solution.py:472
  77.3 1.3 %slot_terms.11 = bf16[128,896]{1,0:T(8,128)(2,1)S(1)} custom-call(bf16[256,1024]{1,0:T(8,128)(2,1)S(1)} %get-tuple-element.120.refs_1_.refs_0_, bf16[256,1024]{1,0:T(8,128)(2,1)S(1)} %get-tuple-element.121.refs_3_.refs_1_, bf16[896,1024]{1,0:T(8,128)(2,1)S(1)} %copy-done, bf16[896,1024]{1,0:T(8,128)(2,1)S(1)} %copy-done.1), custom_call_target="tpu_custom_call" | custom-call | flops 469762048 | bytes 4423680 | tf_op jit(solution)/shard_map/slot_terms/pallas_call | solution.py:472
  78.9 1.3 %slot_terms.12 = bf16[128,896]{1,0:T(8,128)(2,1)S(1)} custom-call(bf16[256,1024]{1,0:T(8,128)(2,1)S(1)} %get-tuple-element.126.refs_0_, bf16[256,1024]{1,0:T(8,128)(2,1)S(1)} %get-tuple-element.127.refs_1_, bf16[896,1024]{1,0:T(8,128)(2,1)S(1)} %copy-done, bf16[896,1024]{1,0:T(8,128)(2,1)S(1)} %copy-done.1), custom_call_target="tpu_custom_call" | custom-call | flops 469762048 | bytes 4423680 | tf_op jit(solution)/shard_map/slot_terms/pallas_call | solution.py:472
  80.2 1.6 %collective-permute-start.19 = (bf16[128,896]{1,0:T(8,128)(2,1)S(1)}, bf16[128,896]{1,0:T(8,128)(2,1)S(1)}, u32[]{:S(2)}, u32[]{:S(2)}) collective-permute-start(bf16[128,896]{1,0:T(8,128)(2,1)S(1)} %add_convert_fusion), channel_id=1, source_target_pairs={{0,2},{1,3},{2,0},{3,1},{4,6},{5,7},{6,4},{7,5},{8,10},{9,11},{10,... | collective-permute-start | bytes 688136 | tf_op jit(solution)/shard_map/ppermute | solution.py:592
  81.8 2.2 %collective-permute-start.20 = (bf16[64,1024]{1,0:T(8,128)(2,1)S(1)}, bf16[64,1024]{1,0:T(8,128)(2,1)S(1)}, u32[]{:S(2)}, u32[]{:S(2)}) collective-permute-start(bf16[64,1024]{1,0:T(8,128)(2,1)S(1)} %slice.9), channel_id=1, source_target_pairs={{0,4},{4,8},{8,12},{1,5},{5,9},{9,13},{2,6},{6,10},{10,14},{3,7},{... | collective-permute-start | bytes 393224 | tf_op jit(solution)/shard_map/ppermute | solution.py:588
  84.2 1.3 %slot_terms.9 = bf16[256,896]{1,0:T(8,128)(2,1)S(1)} custom-call(bf16[256,1024]{1,0:T(8,128)(2,1)S(1)} %get-tuple-element.107.refs_0_, bf16[256,1024]{1,0:T(8,128)(2,1)S(1)} %get-tuple-element.120.refs_1_.refs_0_, bf16[256,1024]{1,0:T(8,128)(2,1)S(1)} %get-tuple-element.113.refs_2_.refs_1_, bf16[256,1024]{1,0:T(8,128)(2,1)S(1)} %get-tuple-element.121.refs_3_.refs_1_, ...), custom_call_target="tpu_custom_call" | custom-call | flops 939524096 | bytes 5177344 | tf_op jit(solution)/shard_map/slot_terms/pallas_call | solution.py:472
  85.5 1.5 %collective-permute-done.20 = bf16[64,1024]{1,0:T(8,128)(2,1)S(1)} collective-permute-done((bf16[64,1024]{1,0:T(8,128)(2,1)S(1)}, bf16[64,1024]{1,0:T(8,128)(2,1)S(1)}, u32[]{:S(2)}, u32[]{:S(2)}) %collective-permute-start.20) | collective-permute-done | bytes 131104 | tf_op jit(solution)/shard_map/ppermute | solution.py:588
  87.0 1.1 collective-permute-done.19
  88.1 1.9 %return_grads.1 = (bf16[2,32,896]{2,1,0:T(8,128)(2,1)S(1)}, bf16[2,32,896]{2,1,0:T(8,128)(2,1)S(1)}, bf16[2,32,896]{2,1,0:T(8,128)(2,1)S(1)}, bf16[2,32,896]{2,1...) custom-call(s32[2,4]{1,0:T(2,128)S(1)} %bitcast.23, ...), custom_call_target="tpu_custom_call" | custom-call | tf_op jit(solution)/shard_map/return_grads/pallas_call | solution.py:318
  90.0 1.4 %collective-permute-start.21 = (bf16[2,32,896]{2,1,0:T(8,128)(2,1)S(1)}, bf16[2,32,896]{2,1,0:T(8,128)(2,1)S(1)}, u32[]{:S(2)}, u32[]{:S(2)}) collective-permute-start(bf16[2,32,896]{2,1,0:T(8,128)(2,1)S(1)} %get-tuple-element.136), channel_id=1, source_target_pairs={{0,20},{4,16},{8,28},{12,24},{16,4},{20,0},{24,12},{28,8},{1,21},{... | collective-permute-start | bytes 344072 | tf_op jit(solution)/shard_map/ppermute | solution.py:592
  91.4 1.5 %collective-permute-start.22 = (bf16[2,32,896]{2,1,0:T(8,128)(2,1)S(1)}, bf16[2,32,896]{2,1,0:T(8,128)(2,1)S(1)}, u32[]{:S(2)}, u32[]{:S(2)}) collective-permute-start(bf16[2,32,896]{2,1,0:T(8,128)(2,1)S(1)} %get-tuple-element.138), channel_id=1, source_target_pairs={{0,16},{4,20},{8,24},{12,28},{16,0},{20,4},{24,8},{28,12},{1,17},{... | collective-permute-start | bytes 344072 | tf_op jit(solution)/shard_map/ppermute | solution.py:592
  92.9 2.1 %collective-permute-start.23 = (bf16[2,32,896]{2,1,0:T(8,128)(2,1)S(1)}, bf16[2,32,896]{2,1,0:T(8,128)(2,1)S(1)}, u32[]{:S(2)}, u32[]{:S(2)}) collective-permute-start(bf16[2,32,896]{2,1,0:T(8,128)(2,1)S(1)} %get-tuple-element.149), channel_id=1, source_target_pairs={{0,28},{4,24},{8,20},{12,16},{16,12},{20,8},{24,4},{28,0},{1,29},{... | collective-permute-start | bytes 344072 | tf_op jit(solution)/shard_map/ppermute | solution.py:592
  95.0 0.9 collective-permute-start.24
  95.9 1.5 %collective-permute-start.25 = (bf16[2,32,896]{2,1,0:T(8,128)(2,1)S(1)}, bf16[2,32,896]{2,1,0:T(8,128)(2,1)S(1)}, u32[]{:S(2)}, u32[]{:S(2)}) collective-permute-start(bf16[2,32,896]{2,1,0:T(8,128)(2,1)S(1)} %get-tuple-element.151), channel_id=1, source_target_pairs={{0,12},{4,8},{8,4},{12,0},{16,28},{20,24},{24,20},{28,16},{1,13},{... | collective-permute-start | bytes 344072 | tf_op jit(solution)/shard_map/ppermute | solution.py:592
  97.4 0.9 pad_maximum_fusion
  98.3 0.9 collective-permute-done.22.refs_1_
  99.2 2.1 %collective-permute-start.27 = (bf16[2,32,896]{2,1,0:T(8,128)(2,1)S(1)}, bf16[2,32,896]{2,1,0:T(8,128)(2,1)S(1)}, u32[]{:S(2)}, u32[]{:S(2)}) collective-permute-start(bf16[2,32,896]{2,1,0:T(8,128)(2,1)S(1)} %get-tuple-element.153), channel_id=1, source_target_pairs={{0,4},{4,0},{8,12},{12,8},{16,20},{20,16},{24,28},{28,24},{1,5},{5... | collective-permute-start | bytes 344072 | tf_op jit(solution)/shard_map/ppermute | solution.py:592
  101.3 0.5 collective-permute-start.26
  101.8 3.8 %stage.1 = (f32[512,1]{1,0:T(8,128)S(1)}, f32[512,1792]{1,0:T(8,128)S(1)}, bf16[1792,896]{1,0:T(8,128)(2,1)S(1)}, bf16[896,1792]{1,0:T(8,128)(2,1)S(1)}) custom-call(f32[896]{0:T(1024)S(1)} %copy-done.6, bf16[512,896]{1,0:T(8,128)(2,1)S(1)} %bitcast.13, bf16[896,1792]{1,0:T(8,128)(2,1)S(1)} %copy-done.4, bf16[1792,896]{1,0:T(8,128)(2,1)S(1)} %copy-done.5), custom_call_target="tpu_custom_call" | custom-call | flops 1644167168 | bytes 18350080 | tf_op jit(solution)/shard_map/stage/pallas_call | solution.py:509
  105.6 6.3 %collective-permute-done.24.refs_4_ = bf16[2,32,896]{2,1,0:T(8,128)(2,1)S(1)} collective-permute-done((bf16[2,32,896]{2,1,0:T(8,128)(2,1)S(1)}, bf16[2,32,896]{2,1,0:T(8,128)(2,1)S(1)}, u32[]{:S(2)}, u32[]{:S(2)}) %collective-permute-start.24) | collective-permute-done | bytes 114720 | tf_op jit(solution)/shard_map/ppermute | solution.py:592
  111.9 2.9 %collective-permute-done.26.refs_6_ = bf16[2,32,896]{2,1,0:T(8,128)(2,1)S(1)} collective-permute-done((bf16[2,32,896]{2,1,0:T(8,128)(2,1)S(1)}, bf16[2,32,896]{2,1,0:T(8,128)(2,1)S(1)}, u32[]{:S(2)}, u32[]{:S(2)}) %collective-permute-start.26) | collective-permute-done | bytes 114720 | tf_op jit(solution)/shard_map/ppermute | solution.py:592
  114.8 7.2 %encode_back.1 = bf16[512,896]{1,0:T(8,128)(2,1)} custom-call(s32[8,2,4]{2,1,0:T(2,128)S(1)} %all-to-all-done.ids_ref, s32[1]{0:T(128)} %bitcast.1.me_ref, f32[896]{0:T(1024)S(1)} %copy-done.6, bf16[512,896]{1,0:T(8,128)(2,1)S(1)} %bitcast.14, f32[512,1]{1,0:T(8,128)S(1)} %get-tuple-element.142.inv_ref, f32[512,1792]{1,0:T(8,128)S(1)} %get-tuple-element.143.slope_ref, ...), custom_call_target="tpu_custom_call" | custom-call | flops 3288334336 | bytes 13762560 | tf_op jit(solution)/shard_map/encode_back/pallas_call | solution.py:565
  (50 shorter events, 1.6 us)
Async XLA Ops:
  1.9 14.2 %all-to-all-start = ((s32[8,2,4]{2,1,0:T(2,128)}), s32[8,2,4]{2,1,0:T(2,128)S(1)}, u32[]{:S(2)}, u32[]{:S(2)}) async-start(s32[8,2,4]{2,1,0:T(2,128)} %broadcast_in_dim.2), calls=%async_computation | async-start | bytes 16384 | tf_op jit(solution)/shard_map/all_to_all | solution.py:623
  16.1 17.4 %copy-start.2 = (bf16[256,1024]{1,0:T(8,128)(2,1)S(1)}, bf16[256,1024]{1,0:T(8,128)(2,1)}, u32[]{:S(2)}) copy-start(bf16[256,1024]{1,0:T(8,128)(2,1)} %refs_7_.1) | copy-start | bytes 1572868
  19.3 9.6 %collective-permute-start.1 = (bf16[2,32,896]{2,1,0:T(8,128)(2,1)S(1)}, bf16[2,32,896]{2,1,0:T(8,128)(2,1)S(1)}, u32[]{:S(2)}, u32[]{:S(2)}) collective-permute-start(bf16[2,32,896]{2,1,0:T(8,128)(2,1)S(1)} %get-tuple-element.81), channel_id=1, source_target_pairs={{0,16},{4,20},{8,24},{12,28},{16,0},{20,4},{24,8},{28,12},{1,17},{... | collective-permute-start | bytes 344072 | tf_op jit(solution)/shard_map/ppermute | solution.py:592
  21.2 7.7 %collective-permute-start = (bf16[2,32,896]{2,1,0:T(8,128)(2,1)S(1)}, bf16[2,32,896]{2,1,0:T(8,128)(2,1)S(1)}, u32[]{:S(2)}, u32[]{:S(2)}) collective-permute-start(bf16[2,32,896]{2,1,0:T(8,128)(2,1)S(1)} %get-tuple-element.79), channel_id=1, source_target_pairs={{0,20},{4,16},{8,28},{12,24},{16,4},{20,0},{24,12},{28,8},{1,21},{... | collective-permute-start | bytes 344072 | tf_op jit(solution)/shard_map/ppermute | solution.py:592
  22.7 19.2 %collective-permute-start.2 = (bf16[2,32,896]{2,1,0:T(8,128)(2,1)S(1)}, bf16[2,32,896]{2,1,0:T(8,128)(2,1)S(1)}, u32[]{:S(2)}, u32[]{:S(2)}) collective-permute-start(bf16[2,32,896]{2,1,0:T(8,128)(2,1)S(1)} %get-tuple-element.90), channel_id=1, source_target_pairs={{0,28},{4,24},{8,20},{12,16},{16,12},{20,8},{24,4},{28,0},{1,29},{... | collective-permute-start | bytes 344072 | tf_op jit(solution)/shard_map/ppermute | solution.py:592
  26.0 15.9 %collective-permute-start.3 = (bf16[2,32,896]{2,1,0:T(8,128)(2,1)S(1)}, bf16[2,32,896]{2,1,0:T(8,128)(2,1)S(1)}, u32[]{:S(2)}, u32[]{:S(2)}) collective-permute-start(bf16[2,32,896]{2,1,0:T(8,128)(2,1)S(1)} %get-tuple-element.91), channel_id=1, source_target_pairs={{0,24},{4,28},{8,16},{12,20},{16,8},{20,12},{24,0},{28,4},{1,25},{... | collective-permute-start | bytes 344072 | tf_op jit(solution)/shard_map/ppermute | solution.py:592
  26.0 15.9 %collective-permute-start.4 = (bf16[2,32,896]{2,1,0:T(8,128)(2,1)S(1)}, bf16[2,32,896]{2,1,0:T(8,128)(2,1)S(1)}, u32[]{:S(2)}, u32[]{:S(2)}) collective-permute-start(bf16[2,32,896]{2,1,0:T(8,128)(2,1)S(1)} %get-tuple-element.92), channel_id=1, source_target_pairs={{0,12},{4,8},{8,4},{12,0},{16,28},{20,24},{24,20},{28,16},{1,13},{... | collective-permute-start | bytes 344072 | tf_op jit(solution)/shard_map/ppermute | solution.py:592
  28.9 13.0 %collective-permute-start.6 = (bf16[2,32,896]{2,1,0:T(8,128)(2,1)S(1)}, bf16[2,32,896]{2,1,0:T(8,128)(2,1)S(1)}, u32[]{:S(2)}, u32[]{:S(2)}) collective-permute-start(bf16[2,32,896]{2,1,0:T(8,128)(2,1)S(1)} %get-tuple-element.94), channel_id=1, source_target_pairs={{0,4},{4,0},{8,12},{12,8},{16,20},{20,16},{24,28},{28,24},{1,5},{5... | collective-permute-start | bytes 344072 | tf_op jit(solution)/shard_map/ppermute | solution.py:592
  31.8 13.5 %collective-permute-start.5 = (bf16[2,32,896]{2,1,0:T(8,128)(2,1)S(1)}, bf16[2,32,896]{2,1,0:T(8,128)(2,1)S(1)}, u32[]{:S(2)}, u32[]{:S(2)}) collective-permute-start(bf16[2,32,896]{2,1,0:T(8,128)(2,1)S(1)} %get-tuple-element.93), channel_id=1, source_target_pairs={{0,8},{4,12},{8,0},{12,4},{16,24},{20,28},{24,16},{28,20},{1,9},{5... | collective-permute-start | bytes 344072 | tf_op jit(solution)/shard_map/ppermute | solution.py:592
  33.5 11.8 %copy-start.7 = (s32[4,2]{0,1:T(2,128)S(1)}, s32[4,2]{0,1:T(2,128)}, u32[]{:S(2)}) copy-start(s32[4,2]{0,1:T(2,128)} %param.18) | copy-start | bytes 100
  33.5 15.9 %copy-start = (bf16[896,1024]{1,0:T(8,128)(2,1)S(1)}, bf16[896,1024]{1,0:T(8,128)(2,1)}, u32[]{:S(2)}) copy-start(bf16[896,1024]{1,0:T(8,128)(2,1)} %refs_2_.11) | copy-start | bytes 5505028
  33.5 15.9 %copy-start.1 = (bf16[896,1024]{1,0:T(8,128)(2,1)S(1)}, bf16[896,1024]{1,0:T(8,128)(2,1)}, u32[]{:S(2)}) copy-start(bf16[896,1024]{1,0:T(8,128)(2,1)} %refs_3_.11) | copy-start | bytes 5505028
  47.4 2.1 %collective-permute-start.8 = (bf16[128,896]{1,0:T(8,128)(2,1)S(1)}, bf16[128,896]{1,0:T(8,128)(2,1)S(1)}, u32[]{:S(2)}, u32[]{:S(2)}) collective-permute-start(bf16[128,896]{1,0:T(8,128)(2,1)S(1)} %bitcast.27), channel_id=1, source_target_pairs={{0,1},{1,0},{2,3},{3,2},{4,5},{5,4},{6,7},{7,6},{8,9},{9,8},{10,11... | collective-permute-start | bytes 688136 | tf_op jit(solution)/shard_map/ppermute | solution.py:592
  47.4 2.0 %collective-permute-start.9 = (bf16[128,896]{1,0:T(8,128)(2,1)S(1)}, bf16[128,896]{1,0:T(8,128)(2,1)S(1)}, u32[]{:S(2)}, u32[]{:S(2)}) collective-permute-start(bf16[128,896]{1,0:T(8,128)(2,1)S(1)} %bitcast.24), channel_id=1, source_target_pairs={{0,1},{1,0},{2,3},{3,2},{4,5},{5,4},{6,7},{7,6},{8,9},{9,8},{10,11... | collective-permute-start | bytes 688136 | tf_op jit(solution)/shard_map/ppermute | solution.py:592
  47.9 7.6 %collective-permute-start.7 = (bf16[128,896]{1,0:T(8,128)(2,1)S(1)}, bf16[128,896]{1,0:T(8,128)(2,1)S(1)}, u32[]{:S(2)}, u32[]{:S(2)}) collective-permute-start(bf16[128,896]{1,0:T(8,128)(2,1)S(1)} %bitcast.28), channel_id=1, source_target_pairs={{0,2},{1,3},{2,0},{3,1},{4,6},{5,7},{6,4},{7,5},{8,10},{9,11},{10,... | collective-permute-start | bytes 688136 | tf_op jit(solution)/shard_map/ppermute | solution.py:592
  55.5 2.8 %collective-permute-start.10 = (bf16[128,896]{1,0:T(8,128)(2,1)S(1)}, bf16[128,896]{1,0:T(8,128)(2,1)S(1)}, u32[]{:S(2)}, u32[]{:S(2)}) collective-permute-start(bf16[128,896]{1,0:T(8,128)(2,1)S(1)} %collective-permute-done.7.refs_2_), channel_id=1, source_target_pairs={{0,1},{1,0},{2,3},{3,2},{4,5},{5,4},{6,7},{7,6},{8,9},{9,8},{10,11... | collective-permute-start | bytes 688136 | tf_op jit(solution)/shard_map/ppermute | solution.py:592
  55.5 9.2 %collective-permute-start.11 = (bf16[128,896]{1,0:T(8,128)(2,1)S(1)}, bf16[128,896]{1,0:T(8,128)(2,1)S(1)}, u32[]{:S(2)}, u32[]{:S(2)}) collective-permute-start(bf16[128,896]{1,0:T(8,128)(2,1)S(1)} %bitcast.26), channel_id=1, source_target_pairs={{0,2},{1,3},{2,0},{3,1},{4,6},{5,7},{6,4},{7,5},{8,10},{9,11},{10,... | collective-permute-start | bytes 688136 | tf_op jit(solution)/shard_map/ppermute | solution.py:592
  57.1 10.3 %collective-permute-start.13 = (bf16[128,1024]{1,0:T(8,128)(2,1)S(1)}, bf16[128,1024]{1,0:T(8,128)(2,1)S(1)}, u32[]{:S(2)}, u32[]{:S(2)}) collective-permute-start(bf16[128,1024]{1,0:T(8,128)(2,1)S(1)} %get-tuple-element.112), channel_id=1, source_target_pairs={{4,0},{8,4},{12,8},{5,1},{9,5},{13,9},{6,2},{10,6},{14,10},{7,3},{... | collective-permute-start | bytes 786440 | tf_op jit(solution)/shard_map/ppermute | solution.py:588
  64.5 4.2 %collective-permute-start.14 = (bf16[128,896]{1,0:T(8,128)(2,1)S(1)}, bf16[128,896]{1,0:T(8,128)(2,1)S(1)}, u32[]{:S(2)}, u32[]{:S(2)}) collective-permute-start(bf16[128,896]{1,0:T(8,128)(2,1)S(1)} %slot_terms.8), channel_id=1, source_target_pairs={{0,1},{1,0},{2,3},{3,2},{4,5},{5,4},{6,7},{7,6},{8,9},{9,8},{10,11... | collective-permute-start | bytes 688136 | tf_op jit(solution)/shard_map/ppermute | solution.py:592
  67.4 1.9 %collective-permute-start.12 = (bf16[128,896]{1,0:T(8,128)(2,1)S(1)}, bf16[128,896]{1,0:T(8,128)(2,1)S(1)}, u32[]{:S(2)}, u32[]{:S(2)}) collective-permute-start(bf16[128,896]{1,0:T(8,128)(2,1)S(1)} %collective-permute-done.11.refs_2_), channel_id=1, source_target_pairs={{0,1},{1,0},{2,3},{3,2},{4,5},{5,4},{6,7},{7,6},{8,9},{9,8},{10,11... | collective-permute-start | bytes 688136 | tf_op jit(solution)/shard_map/ppermute | solution.py:592
  68.7 10.2 %collective-permute-start.17 = (bf16[128,896]{1,0:T(8,128)(2,1)S(1)}, bf16[128,896]{1,0:T(8,128)(2,1)S(1)}, u32[]{:S(2)}, u32[]{:S(2)}) collective-permute-start(bf16[128,896]{1,0:T(8,128)(2,1)S(1)} %add_convert_fusion.1), channel_id=1, source_target_pairs={{0,2},{1,3},{2,0},{3,1},{4,6},{5,7},{6,4},{7,5},{8,10},{9,11},{10,... | collective-permute-start | bytes 688136 | tf_op jit(solution)/shard_map/ppermute | solution.py:592
  75.4 4.8 %collective-permute-start.18 = (bf16[128,896]{1,0:T(8,128)(2,1)S(1)}, bf16[128,896]{1,0:T(8,128)(2,1)S(1)}, u32[]{:S(2)}, u32[]{:S(2)}) collective-permute-start(bf16[128,896]{1,0:T(8,128)(2,1)S(1)} %slot_terms.13), channel_id=1, source_target_pairs={{0,1},{1,0},{2,3},{3,2},{4,5},{5,4},{6,7},{7,6},{8,9},{9,8},{10,11... | collective-permute-start | bytes 688136 | tf_op jit(solution)/shard_map/ppermute | solution.py:592
  77.0 8.4 %collective-permute-start.15 = (bf16[128,896]{1,0:T(8,128)(2,1)S(1)}, bf16[128,896]{1,0:T(8,128)(2,1)S(1)}, u32[]{:S(2)}, u32[]{:S(2)}) collective-permute-start(bf16[128,896]{1,0:T(8,128)(2,1)S(1)} %slot_terms.10), channel_id=1, source_target_pairs={{0,1},{1,0},{2,3},{3,2},{4,5},{5,4},{6,7},{7,6},{8,9},{9,8},{10,11... | collective-permute-start | bytes 688136 | tf_op jit(solution)/shard_map/ppermute | solution.py:592
  78.6 8.4 %collective-permute-start.16 = (bf16[128,896]{1,0:T(8,128)(2,1)S(1)}, bf16[128,896]{1,0:T(8,128)(2,1)S(1)}, u32[]{:S(2)}, u32[]{:S(2)}) collective-permute-start(bf16[128,896]{1,0:T(8,128)(2,1)S(1)} %slot_terms.11), channel_id=1, source_target_pairs={{0,1},{1,0},{2,3},{3,2},{4,5},{5,4},{6,7},{7,6},{8,9},{9,8},{10,11... | collective-permute-start | bytes 688136 | tf_op jit(solution)/shard_map/ppermute | solution.py:592
  80.2 7.9 %collective-permute-start.19 = (bf16[128,896]{1,0:T(8,128)(2,1)S(1)}, bf16[128,896]{1,0:T(8,128)(2,1)S(1)}, u32[]{:S(2)}, u32[]{:S(2)}) collective-permute-start(bf16[128,896]{1,0:T(8,128)(2,1)S(1)} %add_convert_fusion), channel_id=1, source_target_pairs={{0,2},{1,3},{2,0},{3,1},{4,6},{5,7},{6,4},{7,5},{8,10},{9,11},{10,... | collective-permute-start | bytes 688136 | tf_op jit(solution)/shard_map/ppermute | solution.py:592
  81.8 5.1 %collective-permute-start.20 = (bf16[64,1024]{1,0:T(8,128)(2,1)S(1)}, bf16[64,1024]{1,0:T(8,128)(2,1)S(1)}, u32[]{:S(2)}, u32[]{:S(2)}) collective-permute-start(bf16[64,1024]{1,0:T(8,128)(2,1)S(1)} %slice.9), channel_id=1, source_target_pairs={{0,4},{4,8},{8,12},{1,5},{5,9},{9,13},{2,6},{6,10},{10,14},{3,7},{... | collective-permute-start | bytes 393224 | tf_op jit(solution)/shard_map/ppermute | solution.py:588
  84.1 17.7 %copy-start.3 = (bf16[16,32,896]{2,1,0:T(8,128)(2,1)S(1)}, bf16[16,32,896]{2,1,0:T(8,128)(2,1)}, u32[]{:S(2)}) copy-start(bf16[16,32,896]{2,1,0:T(8,128)(2,1)} %param.17) | copy-start | bytes 2752516
  84.1 17.7 %copy-start.4 = (bf16[896,1792]{1,0:T(8,128)(2,1)S(1)}, bf16[896,1792]{1,0:T(8,128)(2,1)}, u32[]{:S(2)}) copy-start(bf16[896,1792]{1,0:T(8,128)(2,1)} %w_in_ref.1) | copy-start | bytes 9633796
  84.1 17.7 %copy-start.5 = (bf16[1792,896]{1,0:T(8,128)(2,1)S(1)}, bf16[1792,896]{1,0:T(8,128)(2,1)}, u32[]{:S(2)}) copy-start(bf16[1792,896]{1,0:T(8,128)(2,1)} %w_out_ref.1) | copy-start | bytes 9633796
  84.1 17.7 %copy-start.6 = (f32[896]{0:T(1024)S(1)}, f32[896]{0:T(1024)}, u32[]{:S(2)}) copy-start(f32[896]{0:T(1024)} %gain_ref.3) | copy-start | bytes 10756
  90.0 9.2 %collective-permute-start.21 = (bf16[2,32,896]{2,1,0:T(8,128)(2,1)S(1)}, bf16[2,32,896]{2,1,0:T(8,128)(2,1)S(1)}, u32[]{:S(2)}, u32[]{:S(2)}) collective-permute-start(bf16[2,32,896]{2,1,0:T(8,128)(2,1)S(1)} %get-tuple-element.136), channel_id=1, source_target_pairs={{0,20},{4,16},{8,28},{12,24},{16,4},{20,0},{24,12},{28,8},{1,21},{... | collective-permute-start | bytes 344072 | tf_op jit(solution)/shard_map/ppermute | solution.py:592
  91.4 7.8 %collective-permute-start.22 = (bf16[2,32,896]{2,1,0:T(8,128)(2,1)S(1)}, bf16[2,32,896]{2,1,0:T(8,128)(2,1)S(1)}, u32[]{:S(2)}, u32[]{:S(2)}) collective-permute-start(bf16[2,32,896]{2,1,0:T(8,128)(2,1)S(1)} %get-tuple-element.138), channel_id=1, source_target_pairs={{0,16},{4,20},{8,24},{12,28},{16,0},{20,4},{24,8},{28,12},{1,17},{... | collective-permute-start | bytes 344072 | tf_op jit(solution)/shard_map/ppermute | solution.py:592
  92.9 12.7 %collective-permute-start.23 = (bf16[2,32,896]{2,1,0:T(8,128)(2,1)S(1)}, bf16[2,32,896]{2,1,0:T(8,128)(2,1)S(1)}, u32[]{:S(2)}, u32[]{:S(2)}) collective-permute-start(bf16[2,32,896]{2,1,0:T(8,128)(2,1)S(1)} %get-tuple-element.149), channel_id=1, source_target_pairs={{0,28},{4,24},{8,20},{12,16},{16,12},{20,8},{24,4},{28,0},{1,29},{... | collective-permute-start | bytes 344072 | tf_op jit(solution)/shard_map/ppermute | solution.py:592
  95.0 16.9 %collective-permute-start.24 = (bf16[2,32,896]{2,1,0:T(8,128)(2,1)S(1)}, bf16[2,32,896]{2,1,0:T(8,128)(2,1)S(1)}, u32[]{:S(2)}, u32[]{:S(2)}) collective-permute-start(bf16[2,32,896]{2,1,0:T(8,128)(2,1)S(1)} %get-tuple-element.150), channel_id=1, source_target_pairs={{0,24},{4,28},{8,16},{12,20},{16,8},{20,12},{24,0},{28,4},{1,25},{... | collective-permute-start | bytes 344072 | tf_op jit(solution)/shard_map/ppermute | solution.py:592
  95.9 16.0 %collective-permute-start.25 = (bf16[2,32,896]{2,1,0:T(8,128)(2,1)S(1)}, bf16[2,32,896]{2,1,0:T(8,128)(2,1)S(1)}, u32[]{:S(2)}, u32[]{:S(2)}) collective-permute-start(bf16[2,32,896]{2,1,0:T(8,128)(2,1)S(1)} %get-tuple-element.151), channel_id=1, source_target_pairs={{0,12},{4,8},{8,4},{12,0},{16,28},{20,24},{24,20},{28,16},{1,13},{... | collective-permute-start | bytes 344072 | tf_op jit(solution)/shard_map/ppermute | solution.py:592
  99.2 12.7 %collective-permute-start.27 = (bf16[2,32,896]{2,1,0:T(8,128)(2,1)S(1)}, bf16[2,32,896]{2,1,0:T(8,128)(2,1)S(1)}, u32[]{:S(2)}, u32[]{:S(2)}) collective-permute-start(bf16[2,32,896]{2,1,0:T(8,128)(2,1)S(1)} %get-tuple-element.153), channel_id=1, source_target_pairs={{0,4},{4,0},{8,12},{12,8},{16,20},{20,16},{24,28},{28,24},{1,5},{5... | collective-permute-start | bytes 344072 | tf_op jit(solution)/shard_map/ppermute | solution.py:592
  101.3 13.5 %collective-permute-start.26 = (bf16[2,32,896]{2,1,0:T(8,128)(2,1)S(1)}, bf16[2,32,896]{2,1,0:T(8,128)(2,1)S(1)}, u32[]{:S(2)}, u32[]{:S(2)}) collective-permute-start(bf16[2,32,896]{2,1,0:T(8,128)(2,1)S(1)} %get-tuple-element.152), channel_id=1, source_target_pairs={{0,8},{4,12},{8,0},{12,4},{16,24},{20,28},{24,16},{28,20},{1,9},{5... | collective-permute-start | bytes 344072 | tf_op jit(solution)/shard_map/ppermute | solution.py:592

commit v2 on v1

--- a/solution.py
+++ b/solution.py
@@ -60,7 +60,7 @@
     masks = range(1, groups)
     far = sorted([m for m in masks if m & (peers // 2)], reverse=True)
     near = sorted([m for m in masks if not m & (peers // 2)], key=lambda m: (m % peers != 0, -m))
-    return [0] + near[:2] + far + near[2:]
+    return [0, near[0], far[-1]] + far[1:-1] + near[1:-1] + [far[0], near[-1]]
 
 
 def each_request(ids_ref, g, first, row_count, capacity, act):
@@ -189,32 +189,59 @@
     )(all_ids, me, encoded, *hbm(tokens))
 
 
-def query_kernel(h_ref, d_ref, w_hbm, out_ref, edge_ref, blocks, total, sems):
+def stream_product(h_ref, w_hbm, first, blocks, sems, total):
     part = blocks.shape[1]
-    count = h_ref.shape[1] // part
+    count = h_ref.shape[1] // part // 2
+    at = [first + i * part for i in range(count)]
     copies = [
-        pltpu.make_async_copy(w_hbm.at[pl.ds(i * part, part), :], blocks.at[i % 3], sems.at[i % 3])
-        for i in range(count)
+        pltpu.make_async_copy(w_hbm.at[pl.ds(row, part), :], blocks.at[i % 3], sems.at[i % 3])
+        for i, row in enumerate(at)
     ]
     for copy in copies[:3]:
         copy.start()
-    for i in range(count):
+    for i, row in enumerate(at):
         copies[i].wait()
-        value = dot(h_ref[:, pl.ds(i * part, part)], blocks[i % 3])
-        total[...] = value if i == 0 else total[...] + value
+        value = dot(h_ref[:, pl.ds(row, part)], blocks[i % 3])
+        total[...] = value if first + i == 0 else total[...] + value
         if i + 3 < count:
             copies[i + 3].start()
+
+
+def query_first_kernel(h_ref, w_hbm, total, blocks, sems):
+    stream_product(h_ref, w_hbm, 0, blocks, sems, total)
+
+
+def query_last_kernel(h_ref, partial_ref, d_ref, w_hbm, out_ref, edge_ref, blocks, sems, total):
+    total[...] = partial_ref[...]
+    stream_product(h_ref, w_hbm, h_ref.shape[1] // 2, blocks, sems, total)
     out_ref[...] = total[...].astype(BF16)
     edge_ref[:STRETCH, :] = total[:STRETCH, :].astype(BF16)
     edge_ref[STRETCH:, :] = d_ref[:STRETCH, :]
 
 
-def query(tokens, w_query, cotangent):
+def query_first(tokens, w_query):
     count, depth = tokens.shape
     feats = w_query.shape[1]
     return pl.pallas_call(
-        query_kernel,
-        in_specs=[vmem()] * 2 + [anywhere()],
+        query_first_kernel,
+        in_specs=[vmem(), anywhere()],
+        out_specs=vmem(),
+        out_shape=jax.ShapeDtypeStruct((count, feats), F32),
+        scratch_shapes=[pltpu.VMEM((3, 1024, feats), BF16), pltpu.SemaphoreType.DMA((3,))],
+        compiler_params=params(12),
+        cost_estimate=pl.CostEstimate(
+            flops=count * depth * feats, bytes_accessed=depth * feats, transcendentals=0
+        ),
+        name="query_first",
+    )(tokens, *hbm(w_query))
+
+
+def query_last(tokens, partial, w_query, cotangent):
+    count, depth = tokens.shape
+    feats = w_query.shape[1]
+    return pl.pallas_call(
+        query_last_kernel,
+        in_specs=[vmem()] * 3 + [anywhere()],
         out_specs=[vmem()] * 2,
         out_shape=[
             jax.ShapeDtypeStruct((count, feats), BF16),
@@ -222,17 +249,15 @@
         ],
         scratch_shapes=[
             pltpu.VMEM((3, 1024, feats), BF16),
+            pltpu.SemaphoreType.DMA((3,)),
             pltpu.VMEM((count, feats), F32),
-            pltpu.SemaphoreType.DMA((3,)),
         ],
         compiler_params=params(12),
         cost_estimate=pl.CostEstimate(
-            flops=2 * count * depth * feats,
-            bytes_accessed=2 * depth * feats + 4 * count * feats,
-            transcendentals=0,
+            flops=count * depth * feats, bytes_accessed=depth * feats, transcendentals=0
         ),
-        name="query",
-    )(tokens, cotangent, *hbm(w_query))
+        name="query_last",
+    )(tokens, partial, cotangent, *hbm(w_query))
 
 
 def places_of(ids_ref, me, row_count, capacity):
@@ -337,12 +362,15 @@
 
 
 def project_kernel(count, *refs):
-    piece_refs, (wk_ref, wv_ref, *out_refs) = refs[:-2 - 2 * count], refs[-2 - 2 * count :]
+    piece_refs, (wk_ref, wv_ref, *out_refs) = refs[: -4 - 2 * count], refs[-4 - 2 * count :]
     each = len(piece_refs) // count
     for i in range(count):
         x = [ref[...] for ref in piece_refs[i * each : (i + 1) * each]]
         x = jnp.concatenate(x, axis=0)
         fill_keys(x, wk_ref, wv_ref, out_refs[2 * i], out_refs[2 * i + 1])
+    for w_ref, out in ((wk_ref, out_refs[-2]), (wv_ref, out_refs[-1])):
+        for at, part in tiles(w_ref.shape[1], 256):
+            out[pl.ds(at, part), :] = w_ref[:, pl.ds(at, part)].T
 
 
 def project(halves, w_key, w_value):
@@ -354,8 +382,9 @@
     out = pl.pallas_call(
         functools.partial(project_kernel, count),
         in_specs=[vmem()] * (len(pieces) + 2),
-        out_specs=[vmem()] * (2 * count),
-        out_shape=[jax.ShapeDtypeStruct((rows, feats), BF16)] * (2 * count),
+        out_specs=[vmem()] * (2 * count + 2),
+        out_shape=[jax.ShapeDtypeStruct((rows, feats), BF16)] * (2 * count)
+        + [jax.ShapeDtypeStruct((feats, width), BF16)] * 2,
         compiler_params=params(16),
         cost_estimate=pl.CostEstimate(
             flops=4 * count * rows * width * feats,
@@ -364,7 +393,7 @@
         ),
         name="project",
     )(*pieces, w_key, w_value)
-    return [out[2 * i : 2 * i + 2] for i in range(count)]
+    return [out[2 * i : 2 * i + 2] for i in range(count)], out[2 * count :]
 
 
 def two_blocks(value):
@@ -406,28 +435,32 @@
 
     def stretch(c, carry):
         mine = pl.ds(pl.multiple_of(c * block, block), block)
-        for h in range(0, block_q.shape[1], 2 * HD):
-            cols = pl.ds(h, 2 * HD)
-            here = [bands(near_refs[0], far_k, c), bands(near_refs[1], far_v, c)]
-            k, v = (jnp.concatenate([ref[b, cols] for ref, b in pair], axis=0) for pair in here)
-            q, d = two_blocks(block_q[mine, cols]), two_blocks(block_d[mine, cols])
-            scores = dot_nt(k, q) * scale
-            weights = jnp.exp(scores - jnp.max(scores, axis=0, keepdims=True))
-            probability = weights * (1.0 / jnp.sum(weights, axis=0, keepdims=True))
-            rounded = probability.astype(BF16)
-            out = dot_tn(rounded, v)
-            att_ref[mine, cols] = jnp.concatenate(
-                [out[:block, :HD], out[block:, HD:]], axis=1
-            ).astype(BF16)
-            value_grads = dot(rounded, d).astype(BF16)
-            dprobs = dot_nt(v, d)
-            centre = jnp.sum(probability * dprobs, axis=0, keepdims=True)
-            dscores = (probability * (dprobs - centre)).astype(BF16)
-            key_grads = (dot(dscores, q) * scale).astype(BF16)
-            for i, (ref, b) in enumerate(bands(near_dk, far_dk, c)):
-                ref[b, cols] = key_grads[i * part : (i + 1) * part]
-            for i, (ref, b) in enumerate(bands(near_dv, far_dv, c)):
-                ref[b, cols] = value_grads[i * part : (i + 1) * part]
+        heads = [pl.ds(h, 2 * HD) for h in range(0, block_q.shape[1], 2 * HD)]
+        for at in range(0, len(heads), 2):
+            pairs = []
+            for cols in heads[at : at + 2]:
+                here = [bands(near_refs[0], far_k, c), bands(near_refs[1], far_v, c)]
+                k, v = (jnp.concatenate([ref[b, cols] for ref, b in pair], axis=0) for pair in here)
+                q, d = two_blocks(block_q[mine, cols]), two_blocks(block_d[mine, cols])
+                pairs.append((cols, v, q, d, dot_nt(k, q) * scale, dot_nt(v, d)))
+            sums = []
+            for cols, v, q, d, scores, dprobs in pairs:
+                weights = jnp.exp(scores - jnp.max(scores, axis=0, keepdims=True))
+                probability = weights * (1.0 / jnp.sum(weights, axis=0, keepdims=True))
+                centre = jnp.sum(probability * dprobs, axis=0, keepdims=True)
+                dscores = (probability * (dprobs - centre)).astype(BF16)
+                sums.append((cols, v, q, d, probability.astype(BF16), dscores))
+            for cols, v, q, d, rounded, dscores in sums:
+                out = dot_tn(rounded, v)
+                att_ref[mine, cols] = jnp.concatenate(
+                    [out[:block, :HD], out[block:, HD:]], axis=1
+                ).astype(BF16)
+                value_grads = dot(rounded, d).astype(BF16)
+                key_grads = (dot(dscores, q) * scale).astype(BF16)
+                for i, (ref, b) in enumerate(bands(near_dk, far_dk, c)):
+                    ref[b, cols] = key_grads[i * part : (i + 1) * part]
+                for i, (ref, b) in enumerate(bands(near_dv, far_dv, c)):
+                    ref[b, cols] = value_grads[i * part : (i + 1) * part]
         return carry
 
     lax.fori_loop(0, count, stretch, 0)
@@ -454,34 +487,38 @@
     )(*near, *far, w_key, w_value, *tokens)
 
 
-def terms_kernel(number, *refs):
-    *grad_refs, wk_ref, wv_ref, term_ref = refs
-
-    def rows_of(halves):
-        part = term_ref.shape[0] // len(halves)
-        return jnp.concatenate([ref[pl.ds(number * part, part), :] for ref in halves], axis=0)
-
-    half = len(grad_refs) // 2
-    term = dot_nt(rows_of(grad_refs[:half]), wk_ref[...])
-    term = term + dot_nt(rows_of(grad_refs[half:]), wv_ref[...])
-    term_ref[...] = term.astype(BF16)
-
-
-def slot_terms(key_grads, value_grads, w_key, w_value, number, rows):
-    width, feats = w_key.shape
-    return pl.pallas_call(
-        functools.partial(terms_kernel, number),
-        in_specs=[vmem()] * (len(key_grads) + len(value_grads) + 2),
-        out_specs=vmem(),
-        out_shape=jax.ShapeDtypeStruct((rows, width), BF16),
-        compiler_params=params(16),
+def terms_kernel(numbers, *refs):
+    count = len(numbers)
+    grad_refs, (wk_ref, wv_ref), term_refs = refs[: 2 * count], refs[2 * count : -count], refs[-count:]
+    rows = term_refs[0].shape[0]
+
+    def rows_of(refs):
+        parts = [ref[pl.ds(number * rows, rows), :] for number, ref in zip(numbers, refs)]
+        return jnp.concatenate(parts, axis=0)
+
+    term = dot(rows_of(grad_refs[:count]), wk_ref[...])
+    term = term + dot(rows_of(grad_refs[count:]), wv_ref[...])
+    term = term.astype(BF16)
+    for i, ref in enumerate(term_refs):
+        ref[...] = term[i * rows : (i + 1) * rows]
+
+
+def slot_terms(asked, turned, rows):
+    feats, width = turned[0].shape
+    count = len(asked)
+    return pl.pallas_call(
+        functools.partial(terms_kernel, [number for _, _, number in asked]),
+        in_specs=[vmem()] * (2 * count + 2),
+        out_specs=[vmem()] * count,
+        out_shape=[jax.ShapeDtypeStruct((rows, width), BF16)] * count,
+        compiler_params=params(20),
         cost_estimate=pl.CostEstimate(
-            flops=4 * rows * width * feats,
-            bytes_accessed=4 * width * feats + 2 * rows * (width + 2 * feats),
+            flops=4 * count * rows * width * feats,
+            bytes_accessed=4 * width * feats + 2 * count * rows * (width + 2 * feats),
             transcendentals=0,
         ),
         name="slot_terms",
-    )(*key_grads, *value_grads, w_key, w_value)
+    )(*[keys for keys, _, _ in asked], *[values for _, values, _ in asked], *turned)
 
 
 def stage_kernel(
@@ -592,13 +629,15 @@
     return lax.ppermute(value, axis, [(i, i ^ bit) for i in range(lax.axis_size(axis))])
 
 
-def exchange(buffers, masks, later):
+def exchange(buffers, masks, later, between=None):
     axes = ("role", "seq")
     count = len(buffers)
     arrived = [buffers[0]] + [swap(buffers[k], axes, masks[k]) for k in range(1, count - 2)]
     for early, k in ((1, count - 2), (2, count - 1)):
         arrived[early], value, later = lax.optimization_barrier((arrived[early], buffers[k], later))
         arrived.append(swap(value, axes, masks[k]))
+        if early == 1 and between is not None:
+            later = between(later)
     return arrived, later
 
 
@@ -629,8 +668,10 @@
     *outgoing, hidden = send_rows(
         all_ids, me, encoded.reshape(row_count, piece, width), hidden, capacity, masks
     )
-    arrived, (d_attended,) = exchange(outgoing, masks, (d_attended,))
-    queries, edges = query(hidden, w_query, d_attended)
+    arrived, (partial, hidden) = exchange(
+        outgoing, masks, hidden, lambda tokens: (query_first(tokens, w_query), tokens)
+    )
+    queries, edges = query_last(hidden, partial, w_query, d_attended)
     queries, neighbours = lax.optimization_barrier((queries, neighbours))
     count = stretch_count // 2
     first_own, last_own = [
@@ -651,10 +692,12 @@
     first_near = gathered({0: first_own})
     last_far = swap(last_own, "tp", half)
     last_near = gathered({0: last_own})
-    first_kv, last_kv = project([first_near, last_near], w_key, w_value)
+    (first_kv, last_kv), turned = project([first_near, last_near], w_key, w_value)
     first_far, first_kv, last_kv = lax.optimization_barrier((first_far, first_kv, last_kv))
+    first_far = gathered({half: first_far})
+    first_far[-1], edges = lax.optimization_barrier((first_far[-1], edges))
     first_o, *first_grads = attend(
-        first_kv, gathered({half: first_far}), w_key, w_value, (queries, d_attended), 0, count
+        first_kv, first_far, w_key, w_value, (queries, d_attended), 0, count
     )
     first_o, last_far = lax.optimization_barrier((first_o, last_far))
     last_far = gathered({half: last_far})
@@ -667,40 +710,38 @@
                 shares[mask ^ bit].append(swap(add_up(shares.pop(mask)), "tp", bit))
         return shares[0]
 
-    def to_send(grads, tied):
-        terms = {
-            j: [slot_terms(grads[2:3], grads[3:], w_key, w_value, j, rows)]
-            for j in reversed(range(1, half))
-        }
-        near = {0: []}
-        near.update({
-            j: [slot_terms(grads[0:1], grads[1:2], w_key, w_value, j, rows)]
-            for j in reversed(range(1, half))
-        })
+    def to_send(grads, others, tied):
+        numbers = list(reversed(range(1, half)))
+        asked = [(grads[2], grads[3], j) for j in numbers]
+        asked += [(each[0], each[1], j) for each in others for j in numbers]
+        terms = slot_terms(asked, turned, rows)
+        sums = []
+        for i in range(1 + len(others)):
+            mine = terms[i * len(numbers) : (i + 1) * len(numbers)]
+            sums.append({0: [], **{j: [term] for j, term in zip(numbers, mine)}})
         tied, grads = lax.optimization_barrier((tied, grads))
-        terms[0] = [slot_terms(grads[2:3], grads[3:], w_key, w_value, 0, rows)]
-        return add_up(fold(terms)), fold(near), tied
-
-    sent, first_core, edges = to_send(first_grads, edges)
+        sums[0][0] = list(slot_terms([(grads[2], grads[3], 0)], turned, rows))
+        far, *near = [fold(shares) for shares in sums]
+        return add_up(far), near, tied
+
+    sent, _, edges = to_send(first_grads, [], edges)
     sent, edges = lax.optimization_barrier((sent, edges))
     first_back = swap(sent, "tp", half)
     last_o, *last_grads = attend(
         last_kv, last_far, w_key, w_value, (queries, d_attended, edges), count, count
     )
     o_edge = shift(last_o[last_o.shape[0] - STRETCH :], "seq", 1)
-    sent, last_core, first_back = to_send(last_grads, first_back)
+    sent, near_back, first_back = to_send(last_grads, [first_grads, last_grads], first_back)
     last_back = swap(sent, "tp", half)
-    own_term = slot_terms(
-        (first_grads[0], last_grads[0]), (first_grads[1], last_grads[1]),
-        w_key, w_value, 0, slots * piece,
+    own_terms = slot_terms(
+        [(grads[0], grads[1], 0) for grads in (first_grads, last_grads)], turned, rows
     )
-    shares = [[own_term]] + [list(pair) for pair in zip(first_core, last_core)]
+    shares = [list(own_terms)] + [list(pair) for pair in zip(*near_back)]
     shares.append([first_back, last_back])
     shares = [[part.reshape(-1, piece, width) for part in share] for share in shares]
-    shares, o_edge = lax.optimization_barrier((shares, o_edge))
     outgoing_grads = return_grads(neighbours, me, shares, row_count, masks, capacity)
     attended = jnp.concatenate([o_edge[1:], first_o, last_o[: last_o.shape[0] - edge]], axis=0)
-    totals, (flat_rows,) = exchange(outgoing_grads, masks, (flat_rows,))
+    totals, flat_rows = exchange(outgoing_grads, masks, flat_rows)
     staged = stage(flat_rows, enc_gain, w_in, w_out)
     grads = encode_back(all_ids, me, enc_gain, flat_rows, staged, totals, masks)
     return (attended, grads.reshape(row_count, piece, width))

time: 122 us -> 110 us (0.902)
  waiting for transfers between devices: 22.6 us -> 12 us
  Pallas kernels: 54 us -> 49.7 us
  starting transfers between devices: 42 us -> 44.9 us
    ppermute x26, waiting for transfers between devices: 18.4 us -> 8.1 us  [swap(): lax.ppermute(value, axis, [(i, i ^ bit) for i in range(lax.axis_size(axis...]
    pallas_call x2, Pallas kernels: 9.67 us -> 7.43 us  [attend(): pl.pallas_call(functools.partial(attend_kernel, len(far), first, count, l...]
    ppermute x2, starting transfers between devices: 3.51 us -> 5.72 us  [shift(): return lax.ppermute(value, axis, pairs)]
    pallas_call x8 -> x7, Pallas kernels: 17.2 us -> 15.2 us  [the longest x1 5.43 us: query_last(): pl.pallas_call(query_last_kernel, in_specs=[vmem()] * 3 + [anywhere()], o...]
  transfers between devices with their start and end apart: 29 -> 29, of which waited for: 8 -> 9; matrix products, arithmetic and copies ran while one was open for 1% -> 1% of each run, Pallas kernels for 33% -> 32%
where the time goes in v2:
time: 110 us
  Pallas kernels  49.7 us (45%)
  starting transfers between devices  44.9 us (41%)
  waiting for transfers between devices  12 us (11%)
  local copies, waits for them, and re-layouts  1.38 us (1%)
    ppermute x26, starting transfers between devices, swap(): lax.ppermute(value, axis, [(i, i ^ bit) for i in range(lax.axis_size(axis...  31.9 us
    ppermute x26, waiting for transfers between devices, swap(): lax.ppermute(value, axis, [(i, i ^ bit) for i in range(lax.axis_size(axis...  8.1 us
    pallas_call x2, Pallas kernels, attend(): pl.pallas_call(functools.partial(attend_kernel, len(far), first, count, l...  7.43 us
    all_to_all x1, starting transfers between devices, body(): lax.all_to_all(jnp.broadcast_to(neighbours[None], (groups, fan_out, stret...  7.25 us
    pallas_call x1, Pallas kernels, encode_back(): pl.pallas_call(functools.partial(encode_back_kernel, masks), in_specs=[sm...  7.05 us
    pallas_call x1, Pallas kernels, encode(): pl.pallas_call(encode_kernel, in_specs=[anywhere()] * 4, out_specs=vmem()...  6.94 us
    ppermute x2, starting transfers between devices, shift(): return lax.ppermute(value, axis, pairs)  5.72 us
    pallas_call x1, Pallas kernels, query_last(): pl.pallas_call(query_last_kernel, in_specs=[vmem()] * 3 + [anywhere()], o...  5.43 us
  transfers between devices with their start and end apart: 29, of which 9 were waited for; matrix products, arithmetic and copies ran while one was open for 1% of the time, Pallas kernels for 32%

profile of v2, /device:TPU:0, one launch (start us, length us, event | category | flops | bytes accessed | tf_op | source)
XLA Modules:
  0.0 109.9 jit_solution(7789514762754927495)
XLA Ops:
  0.6 1.3 %broadcast_in_dim.2 = s32[8,2,4]{2,1,0:T(2,128)} broadcast(s32[2,4]{1,0:T(2,128)} %bitcast.23), dimensions={1,2} | broadcast | bytes 288 | tf_op jit(solution)/shard_map/broadcast_in_dim | solution.py:663
  1.9 7.3 %all-to-all-start = ((s32[8,2,4]{2,1,0:T(2,128)}), s32[8,2,4]{2,1,0:T(2,128)S(1)}, u32[]{:S(2)}, u32[]{:S(2)}) async-start(s32[8,2,4]{2,1,0:T(2,128)} %broadcast_in_dim.2), calls=%async_computation | async-start | bytes 16384 | tf_op jit(solution)/shard_map/all_to_all | solution.py:662
  9.2 6.9 %encode.1 = bf16[512,896]{1,0:T(8,128)(2,1)S(1)} custom-call(f32[896]{0:T(1024)} %gain_ref.3, bf16[512,896]{1,0:T(8,128)(2,1)} %bitcast.13, bf16[896,1792]{1,0:T(8,128)(2,1)} %w_in_ref.1, bf16[1792,896]{1,0:T(8,128)(2,1)} %w_out_ref.1), custom_call_target="tpu_custom_call" | custom-call | flops 3288334336 | bytes 8257536 | tf_op jit(solution)/shard_map/encode/pallas_call | solution.py:125
  16.1 3.0 %send_rows.1 = (bf16[2,32,896]{2,1,0:T(8,128)(2,1)S(1)}, bf16[2,32,896]{2,1,0:T(8,128)(2,1)S(1)}, bf16[2,32,896]{2,1,0:T(8,128)(2,1)S(1)}, bf16[2,32,896]{2,1,0:...) custom-call(s32[8,2,4]{2,1,0:T(2,128)S(1)} %all-to-all-done.ids_ref,, ...), custom_call_target="tpu_custom_call" | custom-call | tf_op jit(solution)/shard_map/send_rows/pallas_call | solution.py:177
  19.1 2.1 %collective-permute-start.1 = (bf16[2,32,896]{2,1,0:T(8,128)(2,1)S(1)}, bf16[2,32,896]{2,1,0:T(8,128)(2,1)S(1)}, u32[]{:S(2)}, u32[]{:S(2)}) collective-permute-start(bf16[2,32,896]{2,1,0:T(8,128)(2,1)S(1)} %get-tuple-element.84), channel_id=1, source_target_pairs={{0,16},{4,20},{8,24},{12,28},{16,0},{20,4},{24,8},{28,12},{1,17},{... | collective-permute-start | bytes 344072 | tf_op jit(solution)/shard_map/ppermute | solution.py:629
  21.2 2.4 %collective-permute-start = (bf16[2,32,896]{2,1,0:T(8,128)(2,1)S(1)}, bf16[2,32,896]{2,1,0:T(8,128)(2,1)S(1)}, u32[]{:S(2)}, u32[]{:S(2)}) collective-permute-start(bf16[2,32,896]{2,1,0:T(8,128)(2,1)S(1)} %get-tuple-element.82), channel_id=1, source_target_pairs={{0,8},{4,12},{8,0},{12,4},{16,24},{20,28},{24,16},{28,20},{1,9},{5... | collective-permute-start | bytes 344072 | tf_op jit(solution)/shard_map/ppermute | solution.py:629
  23.7 3.8 %collective-permute-start.3 = (bf16[2,32,896]{2,1,0:T(8,128)(2,1)S(1)}, bf16[2,32,896]{2,1,0:T(8,128)(2,1)S(1)}, u32[]{:S(2)}, u32[]{:S(2)}) collective-permute-start(bf16[2,32,896]{2,1,0:T(8,128)(2,1)S(1)} %get-tuple-element.96), channel_id=1, source_target_pairs={{0,12},{4,8},{8,4},{12,0},{16,28},{20,24},{24,20},{28,16},{1,13},{... | collective-permute-start | bytes 344072 | tf_op jit(solution)/shard_map/ppermute | solution.py:629
  27.4 0.6 collective-permute-start.4
  28.0 1.6 %collective-permute-start.5 = (bf16[2,32,896]{2,1,0:T(8,128)(2,1)S(1)}, bf16[2,32,896]{2,1,0:T(8,128)(2,1)S(1)}, u32[]{:S(2)}, u32[]{:S(2)}) collective-permute-start(bf16[2,32,896]{2,1,0:T(8,128)(2,1)S(1)} %get-tuple-element.98), channel_id=1, source_target_pairs={{0,28},{4,24},{8,20},{12,16},{16,12},{20,8},{24,4},{28,0},{1,29},{... | collective-permute-start | bytes 344072 | tf_op jit(solution)/shard_map/ppermute | solution.py:629
  29.5 4.6 %query_first.1.partial_ref = f32[256,1024]{1,0:T(8,128)S(1)} custom-call(bf16[256,8192]{1,0:T(8,128)(2,1)S(1)} %get-tuple-element.88.h_ref, bf16[8192,1024]{1,0:T(8,128)(2,1)} %w_hbm.3), custom_call_target="tpu_custom_call" | custom-call | flops 2147483648 | bytes 8388608 | tf_op jit(solution)/shard_map/query_first/pallas_call | solution.py:225
  34.1 1.1 collective-permute-done.refs_2_
  35.3 5.4 %query_last.1 = (bf16[256,1024]{1,0:T(8,128)(2,1)S(1)}, bf16[128,1024]{1,0:T(8,128)(2,1)S(1)}) custom-call(bf16[256,8192]{1,0:T(8,128)(2,1)S(1)} %get-tuple-element.88.h_ref, f32[256,1024]{1,0:T(8,128)S(1)} %query_first.1.partial_ref, bf16[256,1024]{1,0:T(8,128)(2,1)S(1)} %copy-done.2, bf16[8192,1024]{1,0:T(8,128)(2,1)} %w_hbm.3), custom_call_target="tpu_custom_call" | custom-call | flops 2147483648 | bytes 8388608 | tf_op jit(solution)/shard_map/query_last/pallas_call | solution.py:242
  40.8 1.4 %collective-permute-done.6.refs_7_ = bf16[2,32,896]{2,1,0:T(8,128)(2,1)S(1)} collective-permute-done((bf16[2,32,896]{2,1,0:T(8,128)(2,1)S(1)}, bf16[2,32,896]{2,1,0:T(8,128)(2,1)S(1)}, u32[]{:S(2)}, u32[]{:S(2)}) %collective-permute-start.6) | collective-permute-done | bytes 114720 | tf_op jit(solution)/shard_map/ppermute | solution.py:629
  42.2 1.8 %pick_rows.1 = (bf16[4,32,896]{2,1,0:T(8,128)(2,1)S(1)}, bf16[4,32,896]{2,1,0:T(8,128)(2,1)S(1)}) custom-call(s32[2,4]{1,0:T(2,128)S(1)} %bitcast.24, s32[1]{0:T(128)} %bitcast.1.me_ref, bf16[2,32,896]{2,1,0:T(8,128)(2,1)S(1)} %get-tuple-element.92.refs_0_, bf16[2,32,896]{2,1,0:T(8,128)(2,1)S(1)} %collective-permute-done.1.refs_1_, ...), custom_call_target="tpu_custom_call" | custom-call | tf_op jit(solution)/shard_map/pick_rows/pallas_call | solution.py:301
  44.0 0.5 collective-permute-start.9
  44.5 1.5 %collective-permute-start.7 = (bf16[128,896]{1,0:T(8,128)(2,1)S(1)}, bf16[128,896]{1,0:T(8,128)(2,1)S(1)}, u32[]{:S(2)}, u32[]{:S(2)}) collective-permute-start(bf16[128,896]{1,0:T(8,128)(2,1)S(1)} %bitcast.30), channel_id=1, source_target_pairs={{0,2},{1,3},{2,0},{3,1},{4,6},{5,7},{6,4},{7,5},{8,10},{9,11},{10,... | collective-permute-start | bytes 688136 | tf_op jit(solution)/shard_map/ppermute | solution.py:629
  46.1 1.5 %collective-permute-start.11 = (bf16[128,1024]{1,0:T(8,128)(2,1)S(1)}, bf16[128,1024]{1,0:T(8,128)(2,1)S(1)}, u32[]{:S(2)}, u32[]{:S(2)}) collective-permute-start(bf16[128,1024]{1,0:T(8,128)(2,1)S(1)} %get-tuple-element.113), channel_id=1, source_target_pairs={{4,0},{8,4},{12,8},{5,1},{9,5},{13,9},{6,2},{10,6},{14,10},{7,3},{... | collective-permute-start | bytes 786440 | tf_op jit(solution)/shard_map/ppermute | solution.py:625
  47.6 2.3 %project.1 = (bf16[256,1024]{1,0:T(8,128)(2,1)S(1)}, bf16[256,1024]{1,0:T(8,128)(2,1)S(1)}, bf16[256,1024]{1,0:T(8,128)(2,1)S(1)}, bf16[256,1024]{1,0:T(8,128)(2...) custom-call(bf16[128,896]{1,0:T(8,128)(2,1)S(1)} %bitcast.31, ...), custom_call_target="tpu_custom_call" | custom-call | flops 1879048192 | bytes 6684672 | tf_op jit(solution)/shard_map/project/pallas_call | solution.py:382
  49.9 2.2 %collective-permute-done.7.refs_2_ = bf16[128,896]{1,0:T(8,128)(2,1)S(1)} collective-permute-done((bf16[128,896]{1,0:T(8,128)(2,1)S(1)}, bf16[128,896]{1,0:T(8,128)(2,1)S(1)}, u32[]{:S(2)}, u32[]{:S(2)}) %collective-permute-start.7) | collective-permute-done | bytes 229408 | tf_op jit(solution)/shard_map/ppermute | solution.py:629
  52.1 1.5 %collective-permute-start.12 = (bf16[128,896]{1,0:T(8,128)(2,1)S(1)}, bf16[128,896]{1,0:T(8,128)(2,1)S(1)}, u32[]{:S(2)}, u32[]{:S(2)}) collective-permute-start(bf16[128,896]{1,0:T(8,128)(2,1)S(1)} %bitcast.28), channel_id=1, source_target_pairs={{0,2},{1,3},{2,0},{3,1},{4,6},{5,7},{6,4},{7,5},{8,10},{9,11},{10,... | collective-permute-start | bytes 688136 | tf_op jit(solution)/shard_map/ppermute | solution.py:629
  53.7 2.3 %collective-permute-done.11.refs_8_ = bf16[128,1024]{1,0:T(8,128)(2,1)S(1)} collective-permute-done((bf16[128,1024]{1,0:T(8,128)(2,1)S(1)}, bf16[128,1024]{1,0:T(8,128)(2,1)S(1)}, u32[]{:S(2)}, u32[]{:S(2)}) %collective-permute-start.11) | collective-permute-done | bytes 262176 | tf_op jit(solution)/shard_map/ppermute | solution.py:625
  56.0 3.7 %attend.2 = (bf16[128,1024]{1,0:T(8,128)(2,1)S(1)}, bf16[256,1024]{1,0:T(8,128)(2,1)S(1)}, bf16[256,1024]{1,0:T(8,128)(2,1)S(1)}, bf16[256,1024]{1,0:T(8,128)(2,1)S(1)}, bf16[256,1024]{1,0:T(8,128)(2,1)S(1)}) custom-call(bf16[256,1024]{1,0:T(8,128)(2,1)S(1)} %get-tuple-element.110.refs_0_, bf16[256,1024]{1,0:T(8,128)(2,1)S(1)} %get-tuple-element.111.refs_1_, ...), custom_call_target="tpu_custom_call" | custom-call | flops 1610612736 | bytes 6815744 | tf_op jit(solution)/shard_map/attend/pallas_call | solution.py:472
  59.7 0.7 slot_terms.6
  60.5 0.5 collective-permute-start.13
  61.0 0.7 slot_terms.5
  62.0 0.6 collective-permute-start.18
  62.6 3.7 %attend.3 = (bf16[128,1024]{1,0:T(8,128)(2,1)S(1)}, bf16[256,1024]{1,0:T(8,128)(2,1)S(1)}, bf16[256,1024]{1,0:T(8,128)(2,1)S(1)}, bf16[256,1024]{1,0:T(8,128)(2,1)S(1)}, bf16[256,1024]{1,0:T(8,128)(2,1)S(1)}) custom-call(bf16[256,1024]{1,0:T(8,128)(2,1)S(1)} %get-tuple-element.108.refs_0_, bf16[256,1024]{1,0:T(8,128)(2,1)S(1)} %get-tuple-element.109.refs_1_, ...), custom_call_target="tpu_custom_call" | custom-call | flops 1610612736 | bytes 6815744 | tf_op jit(solution)/shard_map/attend/pallas_call | solution.py:472
  66.3 1.8 %slot_terms.8 = (bf16[128,896]{1,0:T(8,128)(2,1)S(1)}, bf16[128,896]{1,0:T(8,128)(2,1)S(1)}, bf16[128,896]{1,0:T(8,128)(2,1)S(1)}) custom-call(bf16[256,1024]{1,0:T(8,128)(2,1)S(1)} %get-tuple-element.141.refs_0_, bf16[256,1024]{1,0:T(8,128)(2,1)S(1)} %get-tuple-element.119.refs_0_.refs_1_, bf16[256,1024]{1,0:T(8,128)(2,1)S(1)} %get-tuple-element.131.refs_1_.refs_2_, ...), custom_call_target="tpu_custom_call" | custom-call | flops 1409286144 | bytes 5931008 | tf_op jit(solution)/shard_map/slot_terms/pallas_call | solution.py:509
  68.1 0.3 collective-permute-start.19
  68.4 0.3 collective-permute-start.16
  68.9 0.8 collective-permute-done.18
  69.7 0.7 slot_terms.9
  70.5 0.9 collective-permute-start.20
  71.4 4.3 %collective-permute-start.15 = (bf16[64,1024]{1,0:T(8,128)(2,1)S(1)}, bf16[64,1024]{1,0:T(8,128)(2,1)S(1)}, u32[]{:S(2)}, u32[]{:S(2)}) collective-permute-start(bf16[64,1024]{1,0:T(8,128)(2,1)S(1)} %slice.9), channel_id=1, source_target_pairs={{0,4},{4,8},{8,12},{1,5},{5,9},{9,13},{2,6},{6,10},{10,14},{3,7},{... | collective-permute-start | bytes 393224 | tf_op jit(solution)/shard_map/ppermute | solution.py:625
  75.8 1.3 %slot_terms.7 = (bf16[128,896]{1,0:T(8,128)(2,1)S(1)}, bf16[128,896]{1,0:T(8,128)(2,1)S(1)}) custom-call(bf16[256,1024]{1,0:T(8,128)(2,1)S(1)} %get-tuple-element.119.refs_0_.refs_1_, bf16[256,1024]{1,0:T(8,128)(2,1)S(1)} %get-tuple-element.131.refs_1_.refs_2_, bf16[256,1024]{1,0:T(8,128)(2,1)S(1)} %get-tuple-element.120.refs_2_.refs_4_, ...), custom_call_target="tpu_custom_call" | custom-call | flops 939524096 | bytes 5177344 | tf_op jit(solution)/shard_map/slot_terms/pallas_call | solution.py:509
  77.0 1.6 %collective-permute-done.15 = bf16[64,1024]{1,0:T(8,128)(2,1)S(1)} collective-permute-done((bf16[64,1024]{1,0:T(8,128)(2,1)S(1)}, bf16[64,1024]{1,0:T(8,128)(2,1)S(1)}, u32[]{:S(2)}, u32[]{:S(2)}) %collective-permute-start.15) | collective-permute-done | bytes 131104 | tf_op jit(solution)/shard_map/ppermute | solution.py:625
  78.7 2.1 %return_grads.1 = (bf16[2,32,896]{2,1,0:T(8,128)(2,1)S(1)}, bf16[2,32,896]{2,1,0:T(8,128)(2,1)S(1)}, bf16[2,32,896]{2,1,0:T(8,128)(2,1)S(1)}, bf16[2,32,896]{2,1...) custom-call(s32[2,4]{1,0:T(2,128)S(1)} %bitcast.25, ...), custom_call_target="tpu_custom_call" | custom-call | tf_op jit(solution)/shard_map/return_grads/pallas_call | solution.py:343
  80.8 3.7 %collective-permute-start.21 = (bf16[2,32,896]{2,1,0:T(8,128)(2,1)S(1)}, bf16[2,32,896]{2,1,0:T(8,128)(2,1)S(1)}, u32[]{:S(2)}, u32[]{:S(2)}) collective-permute-start(bf16[2,32,896]{2,1,0:T(8,128)(2,1)S(1)} %get-tuple-element.144), channel_id=1, source_target_pairs={{0,8},{4,12},{8,0},{12,4},{16,24},{20,28},{24,16},{28,20},{1,9},{5... | collective-permute-start | bytes 344072 | tf_op jit(solution)/shard_map/ppermute | solution.py:629
  84.5 1.5 %collective-permute-start.22 = (bf16[2,32,896]{2,1,0:T(8,128)(2,1)S(1)}, bf16[2,32,896]{2,1,0:T(8,128)(2,1)S(1)}, u32[]{:S(2)}, u32[]{:S(2)}) collective-permute-start(bf16[2,32,896]{2,1,0:T(8,128)(2,1)S(1)} %get-tuple-element.146), channel_id=1, source_target_pairs={{0,16},{4,20},{8,24},{12,28},{16,0},{20,4},{24,8},{28,12},{1,17},{... | collective-permute-start | bytes 344072 | tf_op jit(solution)/shard_map/ppermute | solution.py:629
  86.0 0.9 pad_maximum_fusion
  87.0 2.6 %collective-permute-start.24 = (bf16[2,32,896]{2,1,0:T(8,128)(2,1)S(1)}, bf16[2,32,896]{2,1,0:T(8,128)(2,1)S(1)}, u32[]{:S(2)}, u32[]{:S(2)}) collective-permute-start(bf16[2,32,896]{2,1,0:T(8,128)(2,1)S(1)} %get-tuple-element.158), channel_id=1, source_target_pairs={{0,12},{4,8},{8,4},{12,0},{16,28},{20,24},{24,20},{28,16},{1,13},{... | collective-permute-start | bytes 344072 | tf_op jit(solution)/shard_map/ppermute | solution.py:629
  89.5 1.7 %collective-permute-start.25 = (bf16[2,32,896]{2,1,0:T(8,128)(2,1)S(1)}, bf16[2,32,896]{2,1,0:T(8,128)(2,1)S(1)}, u32[]{:S(2)}, u32[]{:S(2)}) collective-permute-start(bf16[2,32,896]{2,1,0:T(8,128)(2,1)S(1)} %get-tuple-element.159), channel_id=1, source_target_pairs={{0,20},{4,16},{8,28},{12,24},{16,4},{20,0},{24,12},{28,8},{1,21},{... | collective-permute-start | bytes 344072 | tf_op jit(solution)/shard_map/ppermute | solution.py:629
  91.3 1.9 %collective-permute-done.21.refs_2_ = bf16[2,32,896]{2,1,0:T(8,128)(2,1)S(1)} collective-permute-done((bf16[2,32,896]{2,1,0:T(8,128)(2,1)S(1)}, bf16[2,32,896]{2,1,0:T(8,128)(2,1)S(1)}, u32[]{:S(2)}, u32[]{:S(2)}) %collective-permute-start.21) | collective-permute-done | bytes 114720 | tf_op jit(solution)/shard_map/ppermute | solution.py:629
  93.2 1.4 %collective-permute-start.27 = (bf16[2,32,896]{2,1,0:T(8,128)(2,1)S(1)}, bf16[2,32,896]{2,1,0:T(8,128)(2,1)S(1)}, u32[]{:S(2)}, u32[]{:S(2)}) collective-permute-start(bf16[2,32,896]{2,1,0:T(8,128)(2,1)S(1)} %get-tuple-element.161), channel_id=1, source_target_pairs={{0,4},{4,0},{8,12},{12,8},{16,20},{20,16},{24,28},{28,24},{1,5},{5... | collective-permute-start | bytes 344072 | tf_op jit(solution)/shard_map/ppermute | solution.py:629
  94.6 4.0 %collective-permute-start.26 = (bf16[2,32,896]{2,1,0:T(8,128)(2,1)S(1)}, bf16[2,32,896]{2,1,0:T(8,128)(2,1)S(1)}, u32[]{:S(2)}, u32[]{:S(2)}) collective-permute-start(bf16[2,32,896]{2,1,0:T(8,128)(2,1)S(1)} %get-tuple-element.160), channel_id=1, source_target_pairs={{0,28},{4,24},{8,20},{12,16},{16,12},{20,8},{24,4},{28,0},{1,29},{... | collective-permute-start | bytes 344072 | tf_op jit(solution)/shard_map/ppermute | solution.py:629
  98.6 3.8 %stage.1 = (f32[512,1]{1,0:T(8,128)S(1)}, f32[512,1792]{1,0:T(8,128)S(1)}, bf16[1792,896]{1,0:T(8,128)(2,1)S(1)}, bf16[896,1792]{1,0:T(8,128)(2,1)S(1)}) custom-call(f32[896]{0:T(1024)S(1)} %copy-done.6, bf16[512,896]{1,0:T(8,128)(2,1)S(1)} %bitcast.14, bf16[896,1792]{1,0:T(8,128)(2,1)S(1)} %copy-done.4, bf16[1792,896]{1,0:T(8,128)(2,1)S(1)} %copy-done.5), custom_call_target="tpu_custom_call" | custom-call | flops 1644167168 | bytes 18350080 | tf_op jit(solution)/shard_map/stage/pallas_call | solution.py:546
  102.4 0.4 collective-permute-done.27.refs_7_
  102.8 7.0 %encode_back.1 = bf16[512,896]{1,0:T(8,128)(2,1)} custom-call(s32[8,2,4]{2,1,0:T(2,128)S(1)} %all-to-all-done.ids_ref, s32[1]{0:T(128)} %bitcast.1.me_ref, f32[896]{0:T(1024)S(1)} %copy-done.6, bf16[512,896]{1,0:T(8,128)(2,1)S(1)} %bitcast.15, f32[512,1]{1,0:T(8,128)S(1)} %get-tuple-element.150.inv_ref, f32[512,1792]{1,0:T(8,128)S(1)} %get-tuple-element.151.slope_ref, ...), custom_call_target="tpu_custom_call" | custom-call | flops 3288334336 | bytes 13762560 | tf_op jit(solution)/shard_map/encode_back/pallas_call | solution.py:602
  (49 shorter events, 1.1 us)
Async XLA Ops:
  1.9 14.2 %all-to-all-start = ((s32[8,2,4]{2,1,0:T(2,128)}), s32[8,2,4]{2,1,0:T(2,128)S(1)}, u32[]{:S(2)}, u32[]{:S(2)}) async-start(s32[8,2,4]{2,1,0:T(2,128)} %broadcast_in_dim.2), calls=%async_computation | async-start | bytes 16384 | tf_op jit(solution)/shard_map/all_to_all | solution.py:662
  19.1 8.8 %collective-permute-start.1 = (bf16[2,32,896]{2,1,0:T(8,128)(2,1)S(1)}, bf16[2,32,896]{2,1,0:T(8,128)(2,1)S(1)}, u32[]{:S(2)}, u32[]{:S(2)}) collective-permute-start(bf16[2,32,896]{2,1,0:T(8,128)(2,1)S(1)} %get-tuple-element.84), channel_id=1, source_target_pairs={{0,16},{4,20},{8,24},{12,28},{16,0},{20,4},{24,8},{28,12},{1,17},{... | collective-permute-start | bytes 344072 | tf_op jit(solution)/shard_map/ppermute | solution.py:629
  21.2 14.0 %collective-permute-start = (bf16[2,32,896]{2,1,0:T(8,128)(2,1)S(1)}, bf16[2,32,896]{2,1,0:T(8,128)(2,1)S(1)}, u32[]{:S(2)}, u32[]{:S(2)}) collective-permute-start(bf16[2,32,896]{2,1,0:T(8,128)(2,1)S(1)} %get-tuple-element.82), channel_id=1, source_target_pairs={{0,8},{4,12},{8,0},{12,4},{16,24},{20,28},{24,16},{28,20},{1,9},{5... | collective-permute-start | bytes 344072 | tf_op jit(solution)/shard_map/ppermute | solution.py:629
  23.6 17.2 %collective-permute-start.2 = (bf16[2,32,896]{2,1,0:T(8,128)(2,1)S(1)}, bf16[2,32,896]{2,1,0:T(8,128)(2,1)S(1)}, u32[]{:S(2)}, u32[]{:S(2)}) collective-permute-start(bf16[2,32,896]{2,1,0:T(8,128)(2,1)S(1)} %get-tuple-element.95), channel_id=1, source_target_pairs={{0,24},{4,28},{8,16},{12,20},{16,8},{20,12},{24,0},{28,4},{1,25},{... | collective-permute-start | bytes 344072 | tf_op jit(solution)/shard_map/ppermute | solution.py:629
  23.7 17.1 %collective-permute-start.3 = (bf16[2,32,896]{2,1,0:T(8,128)(2,1)S(1)}, bf16[2,32,896]{2,1,0:T(8,128)(2,1)S(1)}, u32[]{:S(2)}, u32[]{:S(2)}) collective-permute-start(bf16[2,32,896]{2,1,0:T(8,128)(2,1)S(1)} %get-tuple-element.96), channel_id=1, source_target_pairs={{0,12},{4,8},{8,4},{12,0},{16,28},{20,24},{24,20},{28,16},{1,13},{... | collective-permute-start | bytes 344072 | tf_op jit(solution)/shard_map/ppermute | solution.py:629
  27.4 13.4 %collective-permute-start.4 = (bf16[2,32,896]{2,1,0:T(8,128)(2,1)S(1)}, bf16[2,32,896]{2,1,0:T(8,128)(2,1)S(1)}, u32[]{:S(2)}, u32[]{:S(2)}) collective-permute-start(bf16[2,32,896]{2,1,0:T(8,128)(2,1)S(1)} %get-tuple-element.97), channel_id=1, source_target_pairs={{0,20},{4,16},{8,28},{12,24},{16,4},{20,0},{24,12},{28,8},{1,21},{... | collective-permute-start | bytes 344072 | tf_op jit(solution)/shard_map/ppermute | solution.py:629
  28.0 7.3 %copy-start.2 = (bf16[256,1024]{1,0:T(8,128)(2,1)S(1)}, bf16[256,1024]{1,0:T(8,128)(2,1)}, u32[]{:S(2)}) copy-start(bf16[256,1024]{1,0:T(8,128)(2,1)} %refs_7_.3) | copy-start | bytes 1572868
  28.0 12.8 %collective-permute-start.5 = (bf16[2,32,896]{2,1,0:T(8,128)(2,1)S(1)}, bf16[2,32,896]{2,1,0:T(8,128)(2,1)S(1)}, u32[]{:S(2)}, u32[]{:S(2)}) collective-permute-start(bf16[2,32,896]{2,1,0:T(8,128)(2,1)S(1)} %get-tuple-element.98), channel_id=1, source_target_pairs={{0,28},{4,24},{8,20},{12,16},{16,12},{20,8},{24,4},{28,0},{1,29},{... | collective-permute-start | bytes 344072 | tf_op jit(solution)/shard_map/ppermute | solution.py:629
  35.2 6.9 %copy-start.7 = (s32[4,2]{0,1:T(2,128)S(1)}, s32[4,2]{0,1:T(2,128)}, u32[]{:S(2)}) copy-start(s32[4,2]{0,1:T(2,128)} %param.18) | copy-start | bytes 100
  35.2 12.3 %copy-start = (bf16[896,1024]{1,0:T(8,128)(2,1)S(1)}, bf16[896,1024]{1,0:T(8,128)(2,1)}, u32[]{:S(2)}) copy-start(bf16[896,1024]{1,0:T(8,128)(2,1)} %refs_4_.5) | copy-start | bytes 5505028
  35.2 12.3 %copy-start.1 = (bf16[896,1024]{1,0:T(8,128)(2,1)S(1)}, bf16[896,1024]{1,0:T(8,128)(2,1)}, u32[]{:S(2)}) copy-start(bf16[896,1024]{1,0:T(8,128)(2,1)} %refs_5_.5) | copy-start | bytes 5505028
  35.2 6.9 %collective-permute-start.6 = (bf16[2,32,896]{2,1,0:T(8,128)(2,1)S(1)}, bf16[2,32,896]{2,1,0:T(8,128)(2,1)S(1)}, u32[]{:S(2)}, u32[]{:S(2)}) collective-permute-start(bf16[2,32,896]{2,1,0:T(8,128)(2,1)S(1)} %get-tuple-element.99), channel_id=1, source_target_pairs={{0,4},{4,0},{8,12},{12,8},{16,20},{20,16},{24,28},{28,24},{1,5},{5... | collective-permute-start | bytes 344072 | tf_op jit(solution)/shard_map/ppermute | solution.py:629
  44.0 3.6 %collective-permute-start.8 = (bf16[128,896]{1,0:T(8,128)(2,1)S(1)}, bf16[128,896]{1,0:T(8,128)(2,1)S(1)}, u32[]{:S(2)}, u32[]{:S(2)}) collective-permute-start(bf16[128,896]{1,0:T(8,128)(2,1)S(1)} %bitcast.29), channel_id=1, source_target_pairs={{0,1},{1,0},{2,3},{3,2},{4,5},{5,4},{6,7},{7,6},{8,9},{9,8},{10,11... | collective-permute-start | bytes 688136 | tf_op jit(solution)/shard_map/ppermute | solution.py:629
  44.0 3.5 %collective-permute-start.9 = (bf16[128,896]{1,0:T(8,128)(2,1)S(1)}, bf16[128,896]{1,0:T(8,128)(2,1)S(1)}, u32[]{:S(2)}, u32[]{:S(2)}) collective-permute-start(bf16[128,896]{1,0:T(8,128)(2,1)S(1)} %bitcast.26), channel_id=1, source_target_pairs={{0,1},{1,0},{2,3},{3,2},{4,5},{5,4},{6,7},{7,6},{8,9},{9,8},{10,11... | collective-permute-start | bytes 688136 | tf_op jit(solution)/shard_map/ppermute | solution.py:629
  44.5 7.6 %collective-permute-start.7 = (bf16[128,896]{1,0:T(8,128)(2,1)S(1)}, bf16[128,896]{1,0:T(8,128)(2,1)S(1)}, u32[]{:S(2)}, u32[]{:S(2)}) collective-permute-start(bf16[128,896]{1,0:T(8,128)(2,1)S(1)} %bitcast.30), channel_id=1, source_target_pairs={{0,2},{1,3},{2,0},{3,1},{4,6},{5,7},{6,4},{7,5},{8,10},{9,11},{10,... | collective-permute-start | bytes 688136 | tf_op jit(solution)/shard_map/ppermute | solution.py:629
  46.1 9.9 %collective-permute-start.11 = (bf16[128,1024]{1,0:T(8,128)(2,1)S(1)}, bf16[128,1024]{1,0:T(8,128)(2,1)S(1)}, u32[]{:S(2)}, u32[]{:S(2)}) collective-permute-start(bf16[128,1024]{1,0:T(8,128)(2,1)S(1)} %get-tuple-element.113), channel_id=1, source_target_pairs={{4,0},{8,4},{12,8},{5,1},{9,5},{13,9},{6,2},{10,6},{14,10},{7,3},{... | collective-permute-start | bytes 786440 | tf_op jit(solution)/shard_map/ppermute | solution.py:625
  52.1 3.8 %collective-permute-start.10 = (bf16[128,896]{1,0:T(8,128)(2,1)S(1)}, bf16[128,896]{1,0:T(8,128)(2,1)S(1)}, u32[]{:S(2)}, u32[]{:S(2)}) collective-permute-start(bf16[128,896]{1,0:T(8,128)(2,1)S(1)} %collective-permute-done.7.refs_2_), channel_id=1, source_target_pairs={{0,1},{1,0},{2,3},{3,2},{4,5},{5,4},{6,7},{7,6},{8,9},{9,8},{10,11... | collective-permute-start | bytes 688136 | tf_op jit(solution)/shard_map/ppermute | solution.py:629
  52.1 8.3 %collective-permute-start.12 = (bf16[128,896]{1,0:T(8,128)(2,1)S(1)}, bf16[128,896]{1,0:T(8,128)(2,1)S(1)}, u32[]{:S(2)}, u32[]{:S(2)}) collective-permute-start(bf16[128,896]{1,0:T(8,128)(2,1)S(1)} %bitcast.28), channel_id=1, source_target_pairs={{0,2},{1,3},{2,0},{3,1},{4,6},{5,7},{6,4},{7,5},{8,10},{9,11},{10,... | collective-permute-start | bytes 688136 | tf_op jit(solution)/shard_map/ppermute | solution.py:629
  60.4 1.6 %collective-permute-start.14 = (bf16[128,896]{1,0:T(8,128)(2,1)S(1)}, bf16[128,896]{1,0:T(8,128)(2,1)S(1)}, u32[]{:S(2)}, u32[]{:S(2)}) collective-permute-start(bf16[128,896]{1,0:T(8,128)(2,1)S(1)} %slot_terms.6), channel_id=1, source_target_pairs={{0,1},{1,0},{2,3},{3,2},{4,5},{5,4},{6,7},{7,6},{8,9},{9,8},{10,11... | collective-permute-start | bytes 688136 | tf_op jit(solution)/shard_map/ppermute | solution.py:629
  60.5 2.1 %collective-permute-start.13 = (bf16[128,896]{1,0:T(8,128)(2,1)S(1)}, bf16[128,896]{1,0:T(8,128)(2,1)S(1)}, u32[]{:S(2)}, u32[]{:S(2)}) collective-permute-start(bf16[128,896]{1,0:T(8,128)(2,1)S(1)} %collective-permute-done.12.refs_2_), channel_id=1, source_target_pairs={{0,1},{1,0},{2,3},{3,2},{4,5},{5,4},{6,7},{7,6},{8,9},{9,8},{10,11... | collective-permute-start | bytes 688136 | tf_op jit(solution)/shard_map/ppermute | solution.py:629
  62.0 7.7 %collective-permute-start.18 = (bf16[128,896]{1,0:T(8,128)(2,1)S(1)}, bf16[128,896]{1,0:T(8,128)(2,1)S(1)}, u32[]{:S(2)}, u32[]{:S(2)}) collective-permute-start(bf16[128,896]{1,0:T(8,128)(2,1)S(1)} %add_convert_fusion.1), channel_id=1, source_target_pairs={{0,2},{1,3},{2,0},{3,1},{4,6},{5,7},{6,4},{7,5},{8,10},{9,11},{10,... | collective-permute-start | bytes 688136 | tf_op jit(solution)/shard_map/ppermute | solution.py:629
  68.1 2.3 %collective-permute-start.19 = (bf16[128,896]{1,0:T(8,128)(2,1)S(1)}, bf16[128,896]{1,0:T(8,128)(2,1)S(1)}, u32[]{:S(2)}, u32[]{:S(2)}) collective-permute-start(bf16[128,896]{1,0:T(8,128)(2,1)S(1)} %get-tuple-element.143), channel_id=1, source_target_pairs={{0,1},{1,0},{2,3},{3,2},{4,5},{5,4},{6,7},{7,6},{8,9},{9,8},{10,11... | collective-permute-start | bytes 688136 | tf_op jit(solution)/shard_map/ppermute | solution.py:629
  68.4 10.3 %collective-permute-start.16 = (bf16[128,896]{1,0:T(8,128)(2,1)S(1)}, bf16[128,896]{1,0:T(8,128)(2,1)S(1)}, u32[]{:S(2)}, u32[]{:S(2)}) collective-permute-start(bf16[128,896]{1,0:T(8,128)(2,1)S(1)} %get-tuple-element.137), channel_id=1, source_target_pairs={{0,1},{1,0},{2,3},{3,2},{4,5},{5,4},{6,7},{7,6},{8,9},{9,8},{10,11... | collective-permute-start | bytes 688136 | tf_op jit(solution)/shard_map/ppermute | solution.py:629
  68.7 10.0 %collective-permute-start.17 = (bf16[128,896]{1,0:T(8,128)(2,1)S(1)}, bf16[128,896]{1,0:T(8,128)(2,1)S(1)}, u32[]{:S(2)}, u32[]{:S(2)}) collective-permute-start(bf16[128,896]{1,0:T(8,128)(2,1)S(1)} %get-tuple-element.138), channel_id=1, source_target_pairs={{0,1},{1,0},{2,3},{3,2},{4,5},{5,4},{6,7},{7,6},{8,9},{9,8},{10,11... | collective-permute-start | bytes 688136 | tf_op jit(solution)/shard_map/ppermute | solution.py:629
  70.5 8.1 %collective-permute-start.20 = (bf16[128,896]{1,0:T(8,128)(2,1)S(1)}, bf16[128,896]{1,0:T(8,128)(2,1)S(1)}, u32[]{:S(2)}, u32[]{:S(2)}) collective-permute-start(bf16[128,896]{1,0:T(8,128)(2,1)S(1)} %add_convert_fusion), channel_id=1, source_target_pairs={{0,2},{1,3},{2,0},{3,1},{4,6},{5,7},{6,4},{7,5},{8,10},{9,11},{10,... | collective-permute-start | bytes 688136 | tf_op jit(solution)/shard_map/ppermute | solution.py:629
  71.4 7.2 %collective-permute-start.15 = (bf16[64,1024]{1,0:T(8,128)(2,1)S(1)}, bf16[64,1024]{1,0:T(8,128)(2,1)S(1)}, u32[]{:S(2)}, u32[]{:S(2)}) collective-permute-start(bf16[64,1024]{1,0:T(8,128)(2,1)S(1)} %slice.9), channel_id=1, source_target_pairs={{0,4},{4,8},{8,12},{1,5},{5,9},{9,13},{2,6},{6,10},{10,14},{3,7},{... | collective-permute-start | bytes 393224 | tf_op jit(solution)/shard_map/ppermute | solution.py:625
  75.7 22.9 %copy-start.3 = (bf16[16,32,896]{2,1,0:T(8,128)(2,1)S(1)}, bf16[16,32,896]{2,1,0:T(8,128)(2,1)}, u32[]{:S(2)}) copy-start(bf16[16,32,896]{2,1,0:T(8,128)(2,1)} %param.17) | copy-start | bytes 2752516
  75.7 22.9 %copy-start.4 = (bf16[896,1792]{1,0:T(8,128)(2,1)S(1)}, bf16[896,1792]{1,0:T(8,128)(2,1)}, u32[]{:S(2)}) copy-start(bf16[896,1792]{1,0:T(8,128)(2,1)} %w_in_ref.1) | copy-start | bytes 9633796
  75.7 22.9 %copy-start.5 = (bf16[1792,896]{1,0:T(8,128)(2,1)S(1)}, bf16[1792,896]{1,0:T(8,128)(2,1)}, u32[]{:S(2)}) copy-start(bf16[1792,896]{1,0:T(8,128)(2,1)} %w_out_ref.1) | copy-start | bytes 9633796
  75.8 22.9 %copy-start.6 = (f32[896]{0:T(1024)S(1)}, f32[896]{0:T(1024)}, u32[]{:S(2)}) copy-start(f32[896]{0:T(1024)} %gain_ref.3) | copy-start | bytes 10756
  80.8 12.4 %collective-permute-start.21 = (bf16[2,32,896]{2,1,0:T(8,128)(2,1)S(1)}, bf16[2,32,896]{2,1,0:T(8,128)(2,1)S(1)}, u32[]{:S(2)}, u32[]{:S(2)}) collective-permute-start(bf16[2,32,896]{2,1,0:T(8,128)(2,1)S(1)} %get-tuple-element.144), channel_id=1, source_target_pairs={{0,8},{4,12},{8,0},{12,4},{16,24},{20,28},{24,16},{28,20},{1,9},{5... | collective-permute-start | bytes 344072 | tf_op jit(solution)/shard_map/ppermute | solution.py:629
  84.5 6.8 %collective-permute-start.22 = (bf16[2,32,896]{2,1,0:T(8,128)(2,1)S(1)}, bf16[2,32,896]{2,1,0:T(8,128)(2,1)S(1)}, u32[]{:S(2)}, u32[]{:S(2)}) collective-permute-start(bf16[2,32,896]{2,1,0:T(8,128)(2,1)S(1)} %get-tuple-element.146), channel_id=1, source_target_pairs={{0,16},{4,20},{8,24},{12,28},{16,0},{20,4},{24,8},{28,12},{1,17},{... | collective-permute-start | bytes 344072 | tf_op jit(solution)/shard_map/ppermute | solution.py:629
  86.9 15.5 %collective-permute-start.23 = (bf16[2,32,896]{2,1,0:T(8,128)(2,1)S(1)}, bf16[2,32,896]{2,1,0:T(8,128)(2,1)S(1)}, u32[]{:S(2)}, u32[]{:S(2)}) collective-permute-start(bf16[2,32,896]{2,1,0:T(8,128)(2,1)S(1)} %get-tuple-element.157), channel_id=1, source_target_pairs={{0,24},{4,28},{8,16},{12,20},{16,8},{20,12},{24,0},{28,4},{1,25},{... | collective-permute-start | bytes 344072 | tf_op jit(solution)/shard_map/ppermute | solution.py:629
  87.0 15.5 %collective-permute-start.24 = (bf16[2,32,896]{2,1,0:T(8,128)(2,1)S(1)}, bf16[2,32,896]{2,1,0:T(8,128)(2,1)S(1)}, u32[]{:S(2)}, u32[]{:S(2)}) collective-permute-start(bf16[2,32,896]{2,1,0:T(8,128)(2,1)S(1)} %get-tuple-element.158), channel_id=1, source_target_pairs={{0,12},{4,8},{8,4},{12,0},{16,28},{20,24},{24,20},{28,16},{1,13},{... | collective-permute-start | bytes 344072 | tf_op jit(solution)/shard_map/ppermute | solution.py:629
  89.5 12.9 %collective-permute-start.25 = (bf16[2,32,896]{2,1,0:T(8,128)(2,1)S(1)}, bf16[2,32,896]{2,1,0:T(8,128)(2,1)S(1)}, u32[]{:S(2)}, u32[]{:S(2)}) collective-permute-start(bf16[2,32,896]{2,1,0:T(8,128)(2,1)S(1)} %get-tuple-element.159), channel_id=1, source_target_pairs={{0,20},{4,16},{8,28},{12,24},{16,4},{20,0},{24,12},{28,8},{1,21},{... | collective-permute-start | bytes 344072 | tf_op jit(solution)/shard_map/ppermute | solution.py:629
  93.2 9.7 %collective-permute-start.27 = (bf16[2,32,896]{2,1,0:T(8,128)(2,1)S(1)}, bf16[2,32,896]{2,1,0:T(8,128)(2,1)S(1)}, u32[]{:S(2)}, u32[]{:S(2)}) collective-permute-start(bf16[2,32,896]{2,1,0:T(8,128)(2,1)S(1)} %get-tuple-element.161), channel_id=1, source_target_pairs={{0,4},{4,0},{8,12},{12,8},{16,20},{20,16},{24,28},{28,24},{1,5},{5... | collective-permute-start | bytes 344072 | tf_op jit(solution)/shard_map/ppermute | solution.py:629
  94.6 8.2 %collective-permute-start.26 = (bf16[2,32,896]{2,1,0:T(8,128)(2,1)S(1)}, bf16[2,32,896]{2,1,0:T(8,128)(2,1)S(1)}, u32[]{:S(2)}, u32[]{:S(2)}) collective-permute-start(bf16[2,32,896]{2,1,0:T(8,128)(2,1)S(1)} %get-tuple-element.160), channel_id=1, source_target_pairs={{0,28},{4,24},{8,20},{12,16},{16,12},{20,8},{24,4},{28,0},{1,29},{... | collective-permute-start | bytes 344072 | tf_op jit(solution)/shard_map/ppermute | solution.py:629

commit v3 on v2

--- a/solution.py
+++ b/solution.py
@@ -436,9 +436,9 @@
     def stretch(c, carry):
         mine = pl.ds(pl.multiple_of(c * block, block), block)
         heads = [pl.ds(h, 2 * HD) for h in range(0, block_q.shape[1], 2 * HD)]
-        for at in range(0, len(heads), 2):
+        for at in range(0, len(heads), 4):
             pairs = []
-            for cols in heads[at : at + 2]:
+            for cols in heads[at : at + 4]:
                 here = [bands(near_refs[0], far_k, c), bands(near_refs[1], far_v, c)]
                 k, v = (jnp.concatenate([ref[b, cols] for ref, b in pair], axis=0) for pair in here)
                 q, d = two_blocks(block_q[mine, cols]), two_blocks(block_d[mine, cols])
@@ -580,20 +580,30 @@
 
         each_request(ids_ref, me ^ mask, me * row_count, row_count, capacity, add)
     upstream[...] = row_grad[...].reshape(upstream.shape).astype(BF16)
-    for at, part in tiles(w_out_turned.shape[1], 256):
-        cols = pl.ds(at, part)
-        d_act = dot(upstream[...], w_out_turned[:, cols])
-        d_pre[:, cols] = (d_act * slope_ref[:, cols]).astype(BF16)
+    d_act = []
+    bands = [pl.ds(at, part) for at, part in tiles(w_out_turned.shape[1], 256)]
+    for i in range(len(bands) + 1):
+        if i < len(bands):
+            d_act.append(dot(upstream[...], w_out_turned[:, bands[i]]))
+        if i > 0:
+            cols = bands[i - 1]
+            d_pre[:, cols] = (d_act[i - 1] * slope_ref[:, cols]).astype(BF16)
     gain = gain_ref[...].reshape(1, width)
-    for at, part in tiles(rows, 256):
-        band = pl.ds(at, part)
-        scaled = dot(d_pre[band, :], w_in_turned[...]) * gain
-        x = x_ref[band, :].astype(F32)
-        inverse = inv_ref[band, :]
-        mean = jnp.mean(scaled * x, axis=-1, keepdims=True)
-        back = inverse * scaled - x * (inverse * inverse * inverse * mean)
-        summed = row_grad[at // piece : (at + part) // piece].reshape(part, width)
-        out_ref[band, :] = (summed + back).astype(BF16)
+    d_norm = []
+    bands = tiles(rows, 128)
+    for i in range(len(bands) + 1):
+        if i < len(bands):
+            d_norm.append(dot(d_pre[pl.ds(*bands[i]), :], w_in_turned[...]))
+        if i > 0:
+            at, part = bands[i - 1]
+            band = pl.ds(at, part)
+            scaled = d_norm[i - 1] * gain
+            x = x_ref[band, :].astype(F32)
+            inverse = inv_ref[band, :]
+            mean = jnp.mean(scaled * x, axis=-1, keepdims=True)
+            back = inverse * scaled - x * (inverse * inverse * inverse * mean)
+            summed = row_grad[at // piece : (at + part) // piece].reshape(part, width)
+            out_ref[band, :] = (summed + back).astype(BF16)
 
 
 def encode_back(all_ids, me, enc_gain, flat_rows, staged, arrived, masks):

time: 110 us -> 110 us (level)
  starting transfers between devices: 44.9 us -> 46.1 us
    ppermute x26, starting transfers between devices: 31.9 us -> 33.8 us  [swap(): lax.ppermute(value, axis, [(i, i ^ bit) for i in range(lax.axis_size(axis...]
    pallas_call x2, Pallas kernels: 7.43 us -> 6.18 us  [attend(): pl.pallas_call(functools.partial(attend_kernel, len(far), first, count, l...]
  transfers between devices with their start and end apart: 29 -> 29, of which waited for: 9 -> 10; matrix products, arithmetic and copies ran while one was open for 1% -> 1% of each run, Pallas kernels for 32% -> 31%
where the time goes in v3:
time: 110 us
  Pallas kernels  48.7 us (44%)
  starting transfers between devices  46.1 us (42%)
  waiting for transfers between devices  11.5 us (10%)
  local copies, waits for them, and re-layouts  1.38 us (1%)
    ppermute x26, starting transfers between devices, swap(): lax.ppermute(value, axis, [(i, i ^ bit) for i in range(lax.axis_size(axis...  33.8 us
    ppermute x26, waiting for transfers between devices, swap(): lax.ppermute(value, axis, [(i, i ^ bit) for i in range(lax.axis_size(axis...  8.01 us
    pallas_call x1, Pallas kernels, encode_back(): pl.pallas_call(functools.partial(encode_back_kernel, masks), in_specs=[sm...  7.33 us
    all_to_all x1, starting transfers between devices, body(): lax.all_to_all(jnp.broadcast_to(neighbours[None], (groups, fan_out, stret...  7.25 us
    pallas_call x1, Pallas kernels, encode(): pl.pallas_call(encode_kernel, in_specs=[anywhere()] * 4, out_specs=vmem()...  6.94 us
    pallas_call x2, Pallas kernels, attend(): pl.pallas_call(functools.partial(attend_kernel, len(far), first, count, l...  6.18 us
    pallas_call x1, Pallas kernels, query_last(): pl.pallas_call(query_last_kernel, in_specs=[vmem()] * 3 + [anywhere()], o...  5.43 us
    pallas_call x5, Pallas kernels, slot_terms(): pl.pallas_call(functools.partial(terms_kernel, [number for _, _, number i...  5.19 us
  transfers between devices with their start and end apart: 29, of which 10 were waited for; matrix products, arithmetic and copies ran while one was open for 1% of the time, Pallas kernels for 31%

profile of v3, /device:TPU:0, one launch (start us, length us, event | category | flops | bytes accessed | tf_op | source)
XLA Modules:
  0.0 109.7 jit_solution(2761840318734209003)
XLA Ops:
  0.6 1.3 %broadcast_in_dim.2 = s32[8,2,4]{2,1,0:T(2,128)} broadcast(s32[2,4]{1,0:T(2,128)} %bitcast.23), dimensions={1,2} | broadcast | bytes 288 | tf_op jit(solution)/shard_map/broadcast_in_dim | solution.py:673
  1.9 7.3 %all-to-all-start = ((s32[8,2,4]{2,1,0:T(2,128)}), s32[8,2,4]{2,1,0:T(2,128)S(1)}, u32[]{:S(2)}, u32[]{:S(2)}) async-start(s32[8,2,4]{2,1,0:T(2,128)} %broadcast_in_dim.2), calls=%async_computation | async-start | bytes 16384 | tf_op jit(solution)/shard_map/all_to_all | solution.py:672
  9.2 6.9 %encode.1 = bf16[512,896]{1,0:T(8,128)(2,1)S(1)} custom-call(f32[896]{0:T(1024)} %gain_ref.3, bf16[512,896]{1,0:T(8,128)(2,1)} %bitcast.13, bf16[896,1792]{1,0:T(8,128)(2,1)} %w_in_ref.1, bf16[1792,896]{1,0:T(8,128)(2,1)} %w_out_ref.1), custom_call_target="tpu_custom_call" | custom-call | flops 3288334336 | bytes 8257536 | tf_op jit(solution)/shard_map/encode/pallas_call | solution.py:125
  16.1 3.0 %send_rows.1 = (bf16[2,32,896]{2,1,0:T(8,128)(2,1)S(1)}, bf16[2,32,896]{2,1,0:T(8,128)(2,1)S(1)}, bf16[2,32,896]{2,1,0:T(8,128)(2,1)S(1)}, bf16[2,32,896]{2,1,0:...) custom-call(s32[8,2,4]{2,1,0:T(2,128)S(1)} %all-to-all-done.ids_ref,, ...), custom_call_target="tpu_custom_call" | custom-call | tf_op jit(solution)/shard_map/send_rows/pallas_call | solution.py:177
  19.1 2.1 %collective-permute-start.1 = (bf16[2,32,896]{2,1,0:T(8,128)(2,1)S(1)}, bf16[2,32,896]{2,1,0:T(8,128)(2,1)S(1)}, u32[]{:S(2)}, u32[]{:S(2)}) collective-permute-start(bf16[2,32,896]{2,1,0:T(8,128)(2,1)S(1)} %get-tuple-element.84), channel_id=1, source_target_pairs={{0,16},{4,20},{8,24},{12,28},{16,0},{20,4},{24,8},{28,12},{1,17},{... | collective-permute-start | bytes 344072 | tf_op jit(solution)/shard_map/ppermute | solution.py:639
  21.2 2.4 %collective-permute-start = (bf16[2,32,896]{2,1,0:T(8,128)(2,1)S(1)}, bf16[2,32,896]{2,1,0:T(8,128)(2,1)S(1)}, u32[]{:S(2)}, u32[]{:S(2)}) collective-permute-start(bf16[2,32,896]{2,1,0:T(8,128)(2,1)S(1)} %get-tuple-element.82), channel_id=1, source_target_pairs={{0,8},{4,12},{8,0},{12,4},{16,24},{20,28},{24,16},{28,20},{1,9},{5... | collective-permute-start | bytes 344072 | tf_op jit(solution)/shard_map/ppermute | solution.py:639
  23.7 3.8 %collective-permute-start.3 = (bf16[2,32,896]{2,1,0:T(8,128)(2,1)S(1)}, bf16[2,32,896]{2,1,0:T(8,128)(2,1)S(1)}, u32[]{:S(2)}, u32[]{:S(2)}) collective-permute-start(bf16[2,32,896]{2,1,0:T(8,128)(2,1)S(1)} %get-tuple-element.96), channel_id=1, source_target_pairs={{0,12},{4,8},{8,4},{12,0},{16,28},{20,24},{24,20},{28,16},{1,13},{... | collective-permute-start | bytes 344072 | tf_op jit(solution)/shard_map/ppermute | solution.py:639
  27.4 0.6 collective-permute-start.4
  28.0 1.5 %collective-permute-start.5 = (bf16[2,32,896]{2,1,0:T(8,128)(2,1)S(1)}, bf16[2,32,896]{2,1,0:T(8,128)(2,1)S(1)}, u32[]{:S(2)}, u32[]{:S(2)}) collective-permute-start(bf16[2,32,896]{2,1,0:T(8,128)(2,1)S(1)} %get-tuple-element.98), channel_id=1, source_target_pairs={{0,28},{4,24},{8,20},{12,16},{16,12},{20,8},{24,4},{28,0},{1,29},{... | collective-permute-start | bytes 344072 | tf_op jit(solution)/shard_map/ppermute | solution.py:639
  29.4 4.6 %query_first.1.partial_ref = f32[256,1024]{1,0:T(8,128)S(1)} custom-call(bf16[256,8192]{1,0:T(8,128)(2,1)S(1)} %get-tuple-element.88.h_ref, bf16[8192,1024]{1,0:T(8,128)(2,1)} %w_hbm.3), custom_call_target="tpu_custom_call" | custom-call | flops 2147483648 | bytes 8388608 | tf_op jit(solution)/shard_map/query_first/pallas_call | solution.py:225
  34.0 1.2 %collective-permute-done.refs_2_ = bf16[2,32,896]{2,1,0:T(8,128)(2,1)S(1)} collective-permute-done((bf16[2,32,896]{2,1,0:T(8,128)(2,1)S(1)}, bf16[2,32,896]{2,1,0:T(8,128)(2,1)S(1)}, u32[]{:S(2)}, u32[]{:S(2)}) %collective-permute-start) | collective-permute-done | bytes 114720 | tf_op jit(solution)/shard_map/ppermute | solution.py:639
  35.3 5.4 %query_last.1 = (bf16[256,1024]{1,0:T(8,128)(2,1)S(1)}, bf16[128,1024]{1,0:T(8,128)(2,1)S(1)}) custom-call(bf16[256,8192]{1,0:T(8,128)(2,1)S(1)} %get-tuple-element.88.h_ref, f32[256,1024]{1,0:T(8,128)S(1)} %query_first.1.partial_ref, bf16[256,1024]{1,0:T(8,128)(2,1)S(1)} %copy-done.2, bf16[8192,1024]{1,0:T(8,128)(2,1)} %w_hbm.3), custom_call_target="tpu_custom_call" | custom-call | flops 2147483648 | bytes 8388608 | tf_op jit(solution)/shard_map/query_last/pallas_call | solution.py:242
  40.8 1.4 %collective-permute-done.6.refs_7_ = bf16[2,32,896]{2,1,0:T(8,128)(2,1)S(1)} collective-permute-done((bf16[2,32,896]{2,1,0:T(8,128)(2,1)S(1)}, bf16[2,32,896]{2,1,0:T(8,128)(2,1)S(1)}, u32[]{:S(2)}, u32[]{:S(2)}) %collective-permute-start.6) | collective-permute-done | bytes 114720 | tf_op jit(solution)/shard_map/ppermute | solution.py:639
  42.2 1.8 %pick_rows.1 = (bf16[4,32,896]{2,1,0:T(8,128)(2,1)S(1)}, bf16[4,32,896]{2,1,0:T(8,128)(2,1)S(1)}) custom-call(s32[2,4]{1,0:T(2,128)S(1)} %bitcast.24, s32[1]{0:T(128)} %bitcast.1.me_ref, bf16[2,32,896]{2,1,0:T(8,128)(2,1)S(1)} %get-tuple-element.92.refs_0_, bf16[2,32,896]{2,1,0:T(8,128)(2,1)S(1)} %collective-permute-done.1.refs_1_, ...), custom_call_target="tpu_custom_call" | custom-call | tf_op jit(solution)/shard_map/pick_rows/pallas_call | solution.py:301
  44.1 0.5 collective-permute-start.9
  44.6 1.5 %collective-permute-start.7 = (bf16[128,896]{1,0:T(8,128)(2,1)S(1)}, bf16[128,896]{1,0:T(8,128)(2,1)S(1)}, u32[]{:S(2)}, u32[]{:S(2)}) collective-permute-start(bf16[128,896]{1,0:T(8,128)(2,1)S(1)} %bitcast.30), channel_id=1, source_target_pairs={{0,2},{1,3},{2,0},{3,1},{4,6},{5,7},{6,4},{7,5},{8,10},{9,11},{10,... | collective-permute-start | bytes 688136 | tf_op jit(solution)/shard_map/ppermute | solution.py:639
  46.1 1.5 %collective-permute-start.11 = (bf16[128,1024]{1,0:T(8,128)(2,1)S(1)}, bf16[128,1024]{1,0:T(8,128)(2,1)S(1)}, u32[]{:S(2)}, u32[]{:S(2)}) collective-permute-start(bf16[128,1024]{1,0:T(8,128)(2,1)S(1)} %get-tuple-element.113), channel_id=1, source_target_pairs={{4,0},{8,4},{12,8},{5,1},{9,5},{13,9},{6,2},{10,6},{14,10},{7,3},{... | collective-permute-start | bytes 786440 | tf_op jit(solution)/shard_map/ppermute | solution.py:635
  47.6 2.3 %project.1 = (bf16[256,1024]{1,0:T(8,128)(2,1)S(1)}, bf16[256,1024]{1,0:T(8,128)(2,1)S(1)}, bf16[256,1024]{1,0:T(8,128)(2,1)S(1)}, bf16[256,1024]{1,0:T(8,128)(2...) custom-call(bf16[128,896]{1,0:T(8,128)(2,1)S(1)} %bitcast.31, ...), custom_call_target="tpu_custom_call" | custom-call | flops 1879048192 | bytes 6684672 | tf_op jit(solution)/shard_map/project/pallas_call | solution.py:382
  49.9 2.2 %collective-permute-done.7.refs_2_ = bf16[128,896]{1,0:T(8,128)(2,1)S(1)} collective-permute-done((bf16[128,896]{1,0:T(8,128)(2,1)S(1)}, bf16[128,896]{1,0:T(8,128)(2,1)S(1)}, u32[]{:S(2)}, u32[]{:S(2)}) %collective-permute-start.7) | collective-permute-done | bytes 229408 | tf_op jit(solution)/shard_map/ppermute | solution.py:639
  52.2 1.5 %collective-permute-start.12 = (bf16[128,896]{1,0:T(8,128)(2,1)S(1)}, bf16[128,896]{1,0:T(8,128)(2,1)S(1)}, u32[]{:S(2)}, u32[]{:S(2)}) collective-permute-start(bf16[128,896]{1,0:T(8,128)(2,1)S(1)} %bitcast.28), channel_id=1, source_target_pairs={{0,2},{1,3},{2,0},{3,1},{4,6},{5,7},{6,4},{7,5},{8,10},{9,11},{10,... | collective-permute-start | bytes 688136 | tf_op jit(solution)/shard_map/ppermute | solution.py:639
  53.7 2.3 %collective-permute-done.11.refs_8_ = bf16[128,1024]{1,0:T(8,128)(2,1)S(1)} collective-permute-done((bf16[128,1024]{1,0:T(8,128)(2,1)S(1)}, bf16[128,1024]{1,0:T(8,128)(2,1)S(1)}, u32[]{:S(2)}, u32[]{:S(2)}) %collective-permute-start.11) | collective-permute-done | bytes 262176 | tf_op jit(solution)/shard_map/ppermute | solution.py:635
  56.0 3.1 %attend.2 = (bf16[128,1024]{1,0:T(8,128)(2,1)S(1)}, bf16[256,1024]{1,0:T(8,128)(2,1)S(1)}, bf16[256,1024]{1,0:T(8,128)(2,1)S(1)}, bf16[256,1024]{1,0:T(8,128)(2,1)S(1)}, bf16[256,1024]{1,0:T(8,128)(2,1)S(1)}) custom-call(bf16[256,1024]{1,0:T(8,128)(2,1)S(1)} %get-tuple-element.110.refs_0_, bf16[256,1024]{1,0:T(8,128)(2,1)S(1)} %get-tuple-element.111.refs_1_, ...), custom_call_target="tpu_custom_call" | custom-call | flops 1610612736 | bytes 6815744 | tf_op jit(solution)/shard_map/attend/pallas_call | solution.py:472
  59.1 0.7 slot_terms.6
  59.9 0.3 collective-permute-done.12.refs_2_
  60.4 0.7 slot_terms.5
  61.4 1.2 %collective-permute-start.18 = (bf16[128,896]{1,0:T(8,128)(2,1)S(1)}, bf16[128,896]{1,0:T(8,128)(2,1)S(1)}, u32[]{:S(2)}, u32[]{:S(2)}) collective-permute-start(bf16[128,896]{1,0:T(8,128)(2,1)S(1)} %add_convert_fusion.1), channel_id=1, source_target_pairs={{0,2},{1,3},{2,0},{3,1},{4,6},{5,7},{6,4},{7,5},{8,10},{9,11},{10,... | collective-permute-start | bytes 688136 | tf_op jit(solution)/shard_map/ppermute | solution.py:639
  62.6 3.1 %attend.3 = (bf16[128,1024]{1,0:T(8,128)(2,1)S(1)}, bf16[256,1024]{1,0:T(8,128)(2,1)S(1)}, bf16[256,1024]{1,0:T(8,128)(2,1)S(1)}, bf16[256,1024]{1,0:T(8,128)(2,1)S(1)}, bf16[256,1024]{1,0:T(8,128)(2,1)S(1)}) custom-call(bf16[256,1024]{1,0:T(8,128)(2,1)S(1)} %get-tuple-element.108.refs_0_, bf16[256,1024]{1,0:T(8,128)(2,1)S(1)} %get-tuple-element.109.refs_1_, ...), custom_call_target="tpu_custom_call" | custom-call | flops 1610612736 | bytes 6815744 | tf_op jit(solution)/shard_map/attend/pallas_call | solution.py:472
  65.7 1.8 %slot_terms.8 = (bf16[128,896]{1,0:T(8,128)(2,1)S(1)}, bf16[128,896]{1,0:T(8,128)(2,1)S(1)}, bf16[128,896]{1,0:T(8,128)(2,1)S(1)}) custom-call(bf16[256,1024]{1,0:T(8,128)(2,1)S(1)} %get-tuple-element.141.refs_0_, bf16[256,1024]{1,0:T(8,128)(2,1)S(1)} %get-tuple-element.119.refs_0_.refs_1_, bf16[256,1024]{1,0:T(8,128)(2,1)S(1)} %get-tuple-element.131.refs_1_.refs_2_, ...), custom_call_target="tpu_custom_call" | custom-call | flops 1409286144 | bytes 5931008 | tf_op jit(solution)/shard_map/slot_terms/pallas_call | solution.py:509
  67.5 0.3 collective-permute-start.19
  67.8 0.3 collective-permute-start.16
  68.3 0.8 collective-permute-done.18
  69.1 0.7 slot_terms.9
  69.9 1.5 %collective-permute-start.20 = (bf16[128,896]{1,0:T(8,128)(2,1)S(1)}, bf16[128,896]{1,0:T(8,128)(2,1)S(1)}, u32[]{:S(2)}, u32[]{:S(2)}) collective-permute-start(bf16[128,896]{1,0:T(8,128)(2,1)S(1)} %add_convert_fusion), channel_id=1, source_target_pairs={{0,2},{1,3},{2,0},{3,1},{4,6},{5,7},{6,4},{7,5},{8,10},{9,11},{10,... | collective-permute-start | bytes 688136 | tf_op jit(solution)/shard_map/ppermute | solution.py:639
  71.5 3.6 %collective-permute-start.15 = (bf16[64,1024]{1,0:T(8,128)(2,1)S(1)}, bf16[64,1024]{1,0:T(8,128)(2,1)S(1)}, u32[]{:S(2)}, u32[]{:S(2)}) collective-permute-start(bf16[64,1024]{1,0:T(8,128)(2,1)S(1)} %slice.9), channel_id=1, source_target_pairs={{0,4},{4,8},{8,12},{1,5},{5,9},{9,13},{2,6},{6,10},{10,14},{3,7},{... | collective-permute-start | bytes 393224 | tf_op jit(solution)/shard_map/ppermute | solution.py:635
  75.1 1.3 %slot_terms.7 = (bf16[128,896]{1,0:T(8,128)(2,1)S(1)}, bf16[128,896]{1,0:T(8,128)(2,1)S(1)}) custom-call(bf16[256,1024]{1,0:T(8,128)(2,1)S(1)} %get-tuple-element.119.refs_0_.refs_1_, bf16[256,1024]{1,0:T(8,128)(2,1)S(1)} %get-tuple-element.131.refs_1_.refs_2_, bf16[256,1024]{1,0:T(8,128)(2,1)S(1)} %get-tuple-element.120.refs_2_.refs_4_, ...), custom_call_target="tpu_custom_call" | custom-call | flops 939524096 | bytes 5177344 | tf_op jit(solution)/shard_map/slot_terms/pallas_call | solution.py:509
  76.4 1.2 %collective-permute-done.15 = bf16[64,1024]{1,0:T(8,128)(2,1)S(1)} collective-permute-done((bf16[64,1024]{1,0:T(8,128)(2,1)S(1)}, bf16[64,1024]{1,0:T(8,128)(2,1)S(1)}, u32[]{:S(2)}, u32[]{:S(2)}) %collective-permute-start.15) | collective-permute-done | bytes 131104 | tf_op jit(solution)/shard_map/ppermute | solution.py:635
  77.6 2.1 %return_grads.1 = (bf16[2,32,896]{2,1,0:T(8,128)(2,1)S(1)}, bf16[2,32,896]{2,1,0:T(8,128)(2,1)S(1)}, bf16[2,32,896]{2,1,0:T(8,128)(2,1)S(1)}, bf16[2,32,896]{2,1...) custom-call(s32[2,4]{1,0:T(2,128)S(1)} %bitcast.25, ...), custom_call_target="tpu_custom_call" | custom-call | tf_op jit(solution)/shard_map/return_grads/pallas_call | solution.py:343
  79.8 4.4 %collective-permute-start.21 = (bf16[2,32,896]{2,1,0:T(8,128)(2,1)S(1)}, bf16[2,32,896]{2,1,0:T(8,128)(2,1)S(1)}, u32[]{:S(2)}, u32[]{:S(2)}) collective-permute-start(bf16[2,32,896]{2,1,0:T(8,128)(2,1)S(1)} %get-tuple-element.144), channel_id=1, source_target_pairs={{0,8},{4,12},{8,0},{12,4},{16,24},{20,28},{24,16},{28,20},{1,9},{5... | collective-permute-start | bytes 344072 | tf_op jit(solution)/shard_map/ppermute | solution.py:639
  84.2 1.5 %collective-permute-start.22 = (bf16[2,32,896]{2,1,0:T(8,128)(2,1)S(1)}, bf16[2,32,896]{2,1,0:T(8,128)(2,1)S(1)}, u32[]{:S(2)}, u32[]{:S(2)}) collective-permute-start(bf16[2,32,896]{2,1,0:T(8,128)(2,1)S(1)} %get-tuple-element.146), channel_id=1, source_target_pairs={{0,16},{4,20},{8,24},{12,28},{16,0},{20,4},{24,8},{28,12},{1,17},{... | collective-permute-start | bytes 344072 | tf_op jit(solution)/shard_map/ppermute | solution.py:639
  85.7 0.9 pad_maximum_fusion
  86.6 2.5 %collective-permute-start.24 = (bf16[2,32,896]{2,1,0:T(8,128)(2,1)S(1)}, bf16[2,32,896]{2,1,0:T(8,128)(2,1)S(1)}, u32[]{:S(2)}, u32[]{:S(2)}) collective-permute-start(bf16[2,32,896]{2,1,0:T(8,128)(2,1)S(1)} %get-tuple-element.158), channel_id=1, source_target_pairs={{0,12},{4,8},{8,4},{12,0},{16,28},{20,24},{24,20},{28,16},{1,13},{... | collective-permute-start | bytes 344072 | tf_op jit(solution)/shard_map/ppermute | solution.py:639
  89.1 1.9 %collective-permute-start.25 = (bf16[2,32,896]{2,1,0:T(8,128)(2,1)S(1)}, bf16[2,32,896]{2,1,0:T(8,128)(2,1)S(1)}, u32[]{:S(2)}, u32[]{:S(2)}) collective-permute-start(bf16[2,32,896]{2,1,0:T(8,128)(2,1)S(1)} %get-tuple-element.159), channel_id=1, source_target_pairs={{0,20},{4,16},{8,28},{12,24},{16,4},{20,0},{24,12},{28,8},{1,21},{... | collective-permute-start | bytes 344072 | tf_op jit(solution)/shard_map/ppermute | solution.py:639
  91.0 1.4 %collective-permute-done.21.refs_2_ = bf16[2,32,896]{2,1,0:T(8,128)(2,1)S(1)} collective-permute-done((bf16[2,32,896]{2,1,0:T(8,128)(2,1)S(1)}, bf16[2,32,896]{2,1,0:T(8,128)(2,1)S(1)}, u32[]{:S(2)}, u32[]{:S(2)}) %collective-permute-start.21) | collective-permute-done | bytes 114720 | tf_op jit(solution)/shard_map/ppermute | solution.py:639
  92.4 1.7 %collective-permute-start.27 = (bf16[2,32,896]{2,1,0:T(8,128)(2,1)S(1)}, bf16[2,32,896]{2,1,0:T(8,128)(2,1)S(1)}, u32[]{:S(2)}, u32[]{:S(2)}) collective-permute-start(bf16[2,32,896]{2,1,0:T(8,128)(2,1)S(1)} %get-tuple-element.161), channel_id=1, source_target_pairs={{0,4},{4,0},{8,12},{12,8},{16,20},{20,16},{24,28},{28,24},{1,5},{5... | collective-permute-start | bytes 344072 | tf_op jit(solution)/shard_map/ppermute | solution.py:639
  94.1 4.1 %collective-permute-start.26 = (bf16[2,32,896]{2,1,0:T(8,128)(2,1)S(1)}, bf16[2,32,896]{2,1,0:T(8,128)(2,1)S(1)}, u32[]{:S(2)}, u32[]{:S(2)}) collective-permute-start(bf16[2,32,896]{2,1,0:T(8,128)(2,1)S(1)} %get-tuple-element.160), channel_id=1, source_target_pairs={{0,28},{4,24},{8,20},{12,16},{16,12},{20,8},{24,4},{28,0},{1,29},{... | collective-permute-start | bytes 344072 | tf_op jit(solution)/shard_map/ppermute | solution.py:639
  98.2 3.8 %stage.1 = (f32[512,1]{1,0:T(8,128)S(1)}, f32[512,1792]{1,0:T(8,128)S(1)}, bf16[1792,896]{1,0:T(8,128)(2,1)S(1)}, bf16[896,1792]{1,0:T(8,128)(2,1)S(1)}) custom-call(f32[896]{0:T(1024)S(1)} %copy-done.6, bf16[512,896]{1,0:T(8,128)(2,1)S(1)} %bitcast.14, bf16[896,1792]{1,0:T(8,128)(2,1)S(1)} %copy-done.4, bf16[1792,896]{1,0:T(8,128)(2,1)S(1)} %copy-done.5), custom_call_target="tpu_custom_call" | custom-call | flops 1644167168 | bytes 18350080 | tf_op jit(solution)/shard_map/stage/pallas_call | solution.py:546
  102.1 0.3 collective-permute-done.26.refs_6_
  102.4 7.3 %encode_back.1 = bf16[512,896]{1,0:T(8,128)(2,1)} custom-call(s32[8,2,4]{2,1,0:T(2,128)S(1)} %all-to-all-done.ids_ref, s32[1]{0:T(128)} %bitcast.1.me_ref, f32[896]{0:T(1024)S(1)} %copy-done.6, bf16[512,896]{1,0:T(8,128)(2,1)S(1)} %bitcast.15, f32[512,1]{1,0:T(8,128)S(1)} %get-tuple-element.150.inv_ref, f32[512,1792]{1,0:T(8,128)S(1)} %get-tuple-element.151.slope_ref, ...), custom_call_target="tpu_custom_call" | custom-call | flops 3288334336 | bytes 13762560 | tf_op jit(solution)/shard_map/encode_back/pallas_call | solution.py:612
  (49 shorter events, 1.3 us)
Async XLA Ops:
  1.9 14.2 %all-to-all-start = ((s32[8,2,4]{2,1,0:T(2,128)}), s32[8,2,4]{2,1,0:T(2,128)S(1)}, u32[]{:S(2)}, u32[]{:S(2)}) async-start(s32[8,2,4]{2,1,0:T(2,128)} %broadcast_in_dim.2), calls=%async_computation | async-start | bytes 16384 | tf_op jit(solution)/shard_map/all_to_all | solution.py:672
  19.1 8.8 %collective-permute-start.1 = (bf16[2,32,896]{2,1,0:T(8,128)(2,1)S(1)}, bf16[2,32,896]{2,1,0:T(8,128)(2,1)S(1)}, u32[]{:S(2)}, u32[]{:S(2)}) collective-permute-start(bf16[2,32,896]{2,1,0:T(8,128)(2,1)S(1)} %get-tuple-element.84), channel_id=1, source_target_pairs={{0,16},{4,20},{8,24},{12,28},{16,0},{20,4},{24,8},{28,12},{1,17},{... | collective-permute-start | bytes 344072 | tf_op jit(solution)/shard_map/ppermute | solution.py:639
  21.2 14.0 %collective-permute-start = (bf16[2,32,896]{2,1,0:T(8,128)(2,1)S(1)}, bf16[2,32,896]{2,1,0:T(8,128)(2,1)S(1)}, u32[]{:S(2)}, u32[]{:S(2)}) collective-permute-start(bf16[2,32,896]{2,1,0:T(8,128)(2,1)S(1)} %get-tuple-element.82), channel_id=1, source_target_pairs={{0,8},{4,12},{8,0},{12,4},{16,24},{20,28},{24,16},{28,20},{1,9},{5... | collective-permute-start | bytes 344072 | tf_op jit(solution)/shard_map/ppermute | solution.py:639
  23.6 17.2 %collective-permute-start.2 = (bf16[2,32,896]{2,1,0:T(8,128)(2,1)S(1)}, bf16[2,32,896]{2,1,0:T(8,128)(2,1)S(1)}, u32[]{:S(2)}, u32[]{:S(2)}) collective-permute-start(bf16[2,32,896]{2,1,0:T(8,128)(2,1)S(1)} %get-tuple-element.95), channel_id=1, source_target_pairs={{0,24},{4,28},{8,16},{12,20},{16,8},{20,12},{24,0},{28,4},{1,25},{... | collective-permute-start | bytes 344072 | tf_op jit(solution)/shard_map/ppermute | solution.py:639
  23.7 17.1 %collective-permute-start.3 = (bf16[2,32,896]{2,1,0:T(8,128)(2,1)S(1)}, bf16[2,32,896]{2,1,0:T(8,128)(2,1)S(1)}, u32[]{:S(2)}, u32[]{:S(2)}) collective-permute-start(bf16[2,32,896]{2,1,0:T(8,128)(2,1)S(1)} %get-tuple-element.96), channel_id=1, source_target_pairs={{0,12},{4,8},{8,4},{12,0},{16,28},{20,24},{24,20},{28,16},{1,13},{... | collective-permute-start | bytes 344072 | tf_op jit(solution)/shard_map/ppermute | solution.py:639
  27.4 13.4 %collective-permute-start.4 = (bf16[2,32,896]{2,1,0:T(8,128)(2,1)S(1)}, bf16[2,32,896]{2,1,0:T(8,128)(2,1)S(1)}, u32[]{:S(2)}, u32[]{:S(2)}) collective-permute-start(bf16[2,32,896]{2,1,0:T(8,128)(2,1)S(1)} %get-tuple-element.97), channel_id=1, source_target_pairs={{0,20},{4,16},{8,28},{12,24},{16,4},{20,0},{24,12},{28,8},{1,21},{... | collective-permute-start | bytes 344072 | tf_op jit(solution)/shard_map/ppermute | solution.py:639
  28.0 7.3 %copy-start.2 = (bf16[256,1024]{1,0:T(8,128)(2,1)S(1)}, bf16[256,1024]{1,0:T(8,128)(2,1)}, u32[]{:S(2)}) copy-start(bf16[256,1024]{1,0:T(8,128)(2,1)} %refs_7_.3) | copy-start | bytes 1572868
  28.0 12.8 %collective-permute-start.5 = (bf16[2,32,896]{2,1,0:T(8,128)(2,1)S(1)}, bf16[2,32,896]{2,1,0:T(8,128)(2,1)S(1)}, u32[]{:S(2)}, u32[]{:S(2)}) collective-permute-start(bf16[2,32,896]{2,1,0:T(8,128)(2,1)S(1)} %get-tuple-element.98), channel_id=1, source_target_pairs={{0,28},{4,24},{8,20},{12,16},{16,12},{20,8},{24,4},{28,0},{1,29},{... | collective-permute-start | bytes 344072 | tf_op jit(solution)/shard_map/ppermute | solution.py:639
  35.2 6.9 %copy-start.7 = (s32[4,2]{0,1:T(2,128)S(1)}, s32[4,2]{0,1:T(2,128)}, u32[]{:S(2)}) copy-start(s32[4,2]{0,1:T(2,128)} %param.18) | copy-start | bytes 100
  35.2 12.3 %copy-start = (bf16[896,1024]{1,0:T(8,128)(2,1)S(1)}, bf16[896,1024]{1,0:T(8,128)(2,1)}, u32[]{:S(2)}) copy-start(bf16[896,1024]{1,0:T(8,128)(2,1)} %refs_4_.5) | copy-start | bytes 5505028
  35.2 12.4 %copy-start.1 = (bf16[896,1024]{1,0:T(8,128)(2,1)S(1)}, bf16[896,1024]{1,0:T(8,128)(2,1)}, u32[]{:S(2)}) copy-start(bf16[896,1024]{1,0:T(8,128)(2,1)} %refs_5_.5) | copy-start | bytes 5505028
  35.2 6.9 %collective-permute-start.6 = (bf16[2,32,896]{2,1,0:T(8,128)(2,1)S(1)}, bf16[2,32,896]{2,1,0:T(8,128)(2,1)S(1)}, u32[]{:S(2)}, u32[]{:S(2)}) collective-permute-start(bf16[2,32,896]{2,1,0:T(8,128)(2,1)S(1)} %get-tuple-element.99), channel_id=1, source_target_pairs={{0,4},{4,0},{8,12},{12,8},{16,20},{20,16},{24,28},{28,24},{1,5},{5... | collective-permute-start | bytes 344072 | tf_op jit(solution)/shard_map/ppermute | solution.py:639
  44.0 3.6 %collective-permute-start.8 = (bf16[128,896]{1,0:T(8,128)(2,1)S(1)}, bf16[128,896]{1,0:T(8,128)(2,1)S(1)}, u32[]{:S(2)}, u32[]{:S(2)}) collective-permute-start(bf16[128,896]{1,0:T(8,128)(2,1)S(1)} %bitcast.29), channel_id=1, source_target_pairs={{0,1},{1,0},{2,3},{3,2},{4,5},{5,4},{6,7},{7,6},{8,9},{9,8},{10,11... | collective-permute-start | bytes 688136 | tf_op jit(solution)/shard_map/ppermute | solution.py:639
  44.1 3.5 %collective-permute-start.9 = (bf16[128,896]{1,0:T(8,128)(2,1)S(1)}, bf16[128,896]{1,0:T(8,128)(2,1)S(1)}, u32[]{:S(2)}, u32[]{:S(2)}) collective-permute-start(bf16[128,896]{1,0:T(8,128)(2,1)S(1)} %bitcast.26), channel_id=1, source_target_pairs={{0,1},{1,0},{2,3},{3,2},{4,5},{5,4},{6,7},{7,6},{8,9},{9,8},{10,11... | collective-permute-start | bytes 688136 | tf_op jit(solution)/shard_map/ppermute | solution.py:639
  44.6 7.6 %collective-permute-start.7 = (bf16[128,896]{1,0:T(8,128)(2,1)S(1)}, bf16[128,896]{1,0:T(8,128)(2,1)S(1)}, u32[]{:S(2)}, u32[]{:S(2)}) collective-permute-start(bf16[128,896]{1,0:T(8,128)(2,1)S(1)} %bitcast.30), channel_id=1, source_target_pairs={{0,2},{1,3},{2,0},{3,1},{4,6},{5,7},{6,4},{7,5},{8,10},{9,11},{10,... | collective-permute-start | bytes 688136 | tf_op jit(solution)/shard_map/ppermute | solution.py:639
  46.1 9.9 %collective-permute-start.11 = (bf16[128,1024]{1,0:T(8,128)(2,1)S(1)}, bf16[128,1024]{1,0:T(8,128)(2,1)S(1)}, u32[]{:S(2)}, u32[]{:S(2)}) collective-permute-start(bf16[128,1024]{1,0:T(8,128)(2,1)S(1)} %get-tuple-element.113), channel_id=1, source_target_pairs={{4,0},{8,4},{12,8},{5,1},{9,5},{13,9},{6,2},{10,6},{14,10},{7,3},{... | collective-permute-start | bytes 786440 | tf_op jit(solution)/shard_map/ppermute | solution.py:635
  52.2 3.8 %collective-permute-start.10 = (bf16[128,896]{1,0:T(8,128)(2,1)S(1)}, bf16[128,896]{1,0:T(8,128)(2,1)S(1)}, u32[]{:S(2)}, u32[]{:S(2)}) collective-permute-start(bf16[128,896]{1,0:T(8,128)(2,1)S(1)} %collective-permute-done.7.refs_2_), channel_id=1, source_target_pairs={{0,1},{1,0},{2,3},{3,2},{4,5},{5,4},{6,7},{7,6},{8,9},{9,8},{10,11... | collective-permute-start | bytes 688136 | tf_op jit(solution)/shard_map/ppermute | solution.py:639
  52.2 8.0 %collective-permute-start.12 = (bf16[128,896]{1,0:T(8,128)(2,1)S(1)}, bf16[128,896]{1,0:T(8,128)(2,1)S(1)}, u32[]{:S(2)}, u32[]{:S(2)}) collective-permute-start(bf16[128,896]{1,0:T(8,128)(2,1)S(1)} %bitcast.28), channel_id=1, source_target_pairs={{0,2},{1,3},{2,0},{3,1},{4,6},{5,7},{6,4},{7,5},{8,10},{9,11},{10,... | collective-permute-start | bytes 688136 | tf_op jit(solution)/shard_map/ppermute | solution.py:639
  59.8 1.6 %collective-permute-start.14 = (bf16[128,896]{1,0:T(8,128)(2,1)S(1)}, bf16[128,896]{1,0:T(8,128)(2,1)S(1)}, u32[]{:S(2)}, u32[]{:S(2)}) collective-permute-start(bf16[128,896]{1,0:T(8,128)(2,1)S(1)} %slot_terms.6), channel_id=1, source_target_pairs={{0,1},{1,0},{2,3},{3,2},{4,5},{5,4},{6,7},{7,6},{8,9},{9,8},{10,11... | collective-permute-start | bytes 688136 | tf_op jit(solution)/shard_map/ppermute | solution.py:639
  60.2 2.4 %collective-permute-start.13 = (bf16[128,896]{1,0:T(8,128)(2,1)S(1)}, bf16[128,896]{1,0:T(8,128)(2,1)S(1)}, u32[]{:S(2)}, u32[]{:S(2)}) collective-permute-start(bf16[128,896]{1,0:T(8,128)(2,1)S(1)} %collective-permute-done.12.refs_2_), channel_id=1, source_target_pairs={{0,1},{1,0},{2,3},{3,2},{4,5},{5,4},{6,7},{7,6},{8,9},{9,8},{10,11... | collective-permute-start | bytes 688136 | tf_op jit(solution)/shard_map/ppermute | solution.py:639
  61.4 7.7 %collective-permute-start.18 = (bf16[128,896]{1,0:T(8,128)(2,1)S(1)}, bf16[128,896]{1,0:T(8,128)(2,1)S(1)}, u32[]{:S(2)}, u32[]{:S(2)}) collective-permute-start(bf16[128,896]{1,0:T(8,128)(2,1)S(1)} %add_convert_fusion.1), channel_id=1, source_target_pairs={{0,2},{1,3},{2,0},{3,1},{4,6},{5,7},{6,4},{7,5},{8,10},{9,11},{10,... | collective-permute-start | bytes 688136 | tf_op jit(solution)/shard_map/ppermute | solution.py:639
  67.5 2.4 %collective-permute-start.19 = (bf16[128,896]{1,0:T(8,128)(2,1)S(1)}, bf16[128,896]{1,0:T(8,128)(2,1)S(1)}, u32[]{:S(2)}, u32[]{:S(2)}) collective-permute-start(bf16[128,896]{1,0:T(8,128)(2,1)S(1)} %get-tuple-element.143), channel_id=1, source_target_pairs={{0,1},{1,0},{2,3},{3,2},{4,5},{5,4},{6,7},{7,6},{8,9},{9,8},{10,11... | collective-permute-start | bytes 688136 | tf_op jit(solution)/shard_map/ppermute | solution.py:639
  67.8 9.9 %collective-permute-start.16 = (bf16[128,896]{1,0:T(8,128)(2,1)S(1)}, bf16[128,896]{1,0:T(8,128)(2,1)S(1)}, u32[]{:S(2)}, u32[]{:S(2)}) collective-permute-start(bf16[128,896]{1,0:T(8,128)(2,1)S(1)} %get-tuple-element.137), channel_id=1, source_target_pairs={{0,1},{1,0},{2,3},{3,2},{4,5},{5,4},{6,7},{7,6},{8,9},{9,8},{10,11... | collective-permute-start | bytes 688136 | tf_op jit(solution)/shard_map/ppermute | solution.py:639
  68.0 9.6 %collective-permute-start.17 = (bf16[128,896]{1,0:T(8,128)(2,1)S(1)}, bf16[128,896]{1,0:T(8,128)(2,1)S(1)}, u32[]{:S(2)}, u32[]{:S(2)}) collective-permute-start(bf16[128,896]{1,0:T(8,128)(2,1)S(1)} %get-tuple-element.138), channel_id=1, source_target_pairs={{0,1},{1,0},{2,3},{3,2},{4,5},{5,4},{6,7},{7,6},{8,9},{9,8},{10,11... | collective-permute-start | bytes 688136 | tf_op jit(solution)/shard_map/ppermute | solution.py:639
  69.9 7.7 %collective-permute-start.20 = (bf16[128,896]{1,0:T(8,128)(2,1)S(1)}, bf16[128,896]{1,0:T(8,128)(2,1)S(1)}, u32[]{:S(2)}, u32[]{:S(2)}) collective-permute-start(bf16[128,896]{1,0:T(8,128)(2,1)S(1)} %add_convert_fusion), channel_id=1, source_target_pairs={{0,2},{1,3},{2,0},{3,1},{4,6},{5,7},{6,4},{7,5},{8,10},{9,11},{10,... | collective-permute-start | bytes 688136 | tf_op jit(solution)/shard_map/ppermute | solution.py:639
  71.5 6.1 %collective-permute-start.15 = (bf16[64,1024]{1,0:T(8,128)(2,1)S(1)}, bf16[64,1024]{1,0:T(8,128)(2,1)S(1)}, u32[]{:S(2)}, u32[]{:S(2)}) collective-permute-start(bf16[64,1024]{1,0:T(8,128)(2,1)S(1)} %slice.9), channel_id=1, source_target_pairs={{0,4},{4,8},{8,12},{1,5},{5,9},{9,13},{2,6},{6,10},{10,14},{3,7},{... | collective-permute-start | bytes 393224 | tf_op jit(solution)/shard_map/ppermute | solution.py:635
  75.1 23.1 %copy-start.3 = (bf16[16,32,896]{2,1,0:T(8,128)(2,1)S(1)}, bf16[16,32,896]{2,1,0:T(8,128)(2,1)}, u32[]{:S(2)}) copy-start(bf16[16,32,896]{2,1,0:T(8,128)(2,1)} %param.17) | copy-start | bytes 2752516
  75.1 23.1 %copy-start.4 = (bf16[896,1792]{1,0:T(8,128)(2,1)S(1)}, bf16[896,1792]{1,0:T(8,128)(2,1)}, u32[]{:S(2)}) copy-start(bf16[896,1792]{1,0:T(8,128)(2,1)} %w_in_ref.1) | copy-start | bytes 9633796
  75.1 23.1 %copy-start.5 = (bf16[1792,896]{1,0:T(8,128)(2,1)S(1)}, bf16[1792,896]{1,0:T(8,128)(2,1)}, u32[]{:S(2)}) copy-start(bf16[1792,896]{1,0:T(8,128)(2,1)} %w_out_ref.1) | copy-start | bytes 9633796
  75.1 23.1 %copy-start.6 = (f32[896]{0:T(1024)S(1)}, f32[896]{0:T(1024)}, u32[]{:S(2)}) copy-start(f32[896]{0:T(1024)} %gain_ref.3) | copy-start | bytes 10756
  79.8 12.6 %collective-permute-start.21 = (bf16[2,32,896]{2,1,0:T(8,128)(2,1)S(1)}, bf16[2,32,896]{2,1,0:T(8,128)(2,1)S(1)}, u32[]{:S(2)}, u32[]{:S(2)}) collective-permute-start(bf16[2,32,896]{2,1,0:T(8,128)(2,1)S(1)} %get-tuple-element.144), channel_id=1, source_target_pairs={{0,8},{4,12},{8,0},{12,4},{16,24},{20,28},{24,16},{28,20},{1,9},{5... | collective-permute-start | bytes 344072 | tf_op jit(solution)/shard_map/ppermute | solution.py:639
  84.2 6.8 %collective-permute-start.22 = (bf16[2,32,896]{2,1,0:T(8,128)(2,1)S(1)}, bf16[2,32,896]{2,1,0:T(8,128)(2,1)S(1)}, u32[]{:S(2)}, u32[]{:S(2)}) collective-permute-start(bf16[2,32,896]{2,1,0:T(8,128)(2,1)S(1)} %get-tuple-element.146), channel_id=1, source_target_pairs={{0,16},{4,20},{8,24},{12,28},{16,0},{20,4},{24,8},{28,12},{1,17},{... | collective-permute-start | bytes 344072 | tf_op jit(solution)/shard_map/ppermute | solution.py:639
  86.6 15.4 %collective-permute-start.23 = (bf16[2,32,896]{2,1,0:T(8,128)(2,1)S(1)}, bf16[2,32,896]{2,1,0:T(8,128)(2,1)S(1)}, u32[]{:S(2)}, u32[]{:S(2)}) collective-permute-start(bf16[2,32,896]{2,1,0:T(8,128)(2,1)S(1)} %get-tuple-element.157), channel_id=1, source_target_pairs={{0,24},{4,28},{8,16},{12,20},{16,8},{20,12},{24,0},{28,4},{1,25},{... | collective-permute-start | bytes 344072 | tf_op jit(solution)/shard_map/ppermute | solution.py:639
  86.6 15.4 %collective-permute-start.24 = (bf16[2,32,896]{2,1,0:T(8,128)(2,1)S(1)}, bf16[2,32,896]{2,1,0:T(8,128)(2,1)S(1)}, u32[]{:S(2)}, u32[]{:S(2)}) collective-permute-start(bf16[2,32,896]{2,1,0:T(8,128)(2,1)S(1)} %get-tuple-element.158), channel_id=1, source_target_pairs={{0,12},{4,8},{8,4},{12,0},{16,28},{20,24},{24,20},{28,16},{1,13},{... | collective-permute-start | bytes 344072 | tf_op jit(solution)/shard_map/ppermute | solution.py:639
  89.1 12.9 %collective-permute-start.25 = (bf16[2,32,896]{2,1,0:T(8,128)(2,1)S(1)}, bf16[2,32,896]{2,1,0:T(8,128)(2,1)S(1)}, u32[]{:S(2)}, u32[]{:S(2)}) collective-permute-start(bf16[2,32,896]{2,1,0:T(8,128)(2,1)S(1)} %get-tuple-element.159), channel_id=1, source_target_pairs={{0,20},{4,16},{8,28},{12,24},{16,4},{20,0},{24,12},{28,8},{1,21},{... | collective-permute-start | bytes 344072 | tf_op jit(solution)/shard_map/ppermute | solution.py:639
  92.4 9.7 %collective-permute-start.27 = (bf16[2,32,896]{2,1,0:T(8,128)(2,1)S(1)}, bf16[2,32,896]{2,1,0:T(8,128)(2,1)S(1)}, u32[]{:S(2)}, u32[]{:S(2)}) collective-permute-start(bf16[2,32,896]{2,1,0:T(8,128)(2,1)S(1)} %get-tuple-element.161), channel_id=1, source_target_pairs={{0,4},{4,0},{8,12},{12,8},{16,20},{20,16},{24,28},{28,24},{1,5},{5... | collective-permute-start | bytes 344072 | tf_op jit(solution)/shard_map/ppermute | solution.py:639
  94.1 8.2 %collective-permute-start.26 = (bf16[2,32,896]{2,1,0:T(8,128)(2,1)S(1)}, bf16[2,32,896]{2,1,0:T(8,128)(2,1)S(1)}, u32[]{:S(2)}, u32[]{:S(2)}) collective-permute-start(bf16[2,32,896]{2,1,0:T(8,128)(2,1)S(1)} %get-tuple-element.160), channel_id=1, source_target_pairs={{0,28},{4,24},{8,20},{12,16},{16,12},{20,8},{24,4},{28,0},{1,29},{... | collective-permute-start | bytes 344072 | tf_op jit(solution)/shard_map/ppermute | solution.py:639
